TPU v7x, 128 devices: a whole 4x4x4 slice. The times are simulated.
128 devices in a mesh: row: 16 (over y, z), col: 8 (over x, core).
Axes of the slice: x: 4, y: 4, z: 4, core: 2. Of those that a mesh axis runs over, the one named last changes fastest.
Arguments:
- panel: float32 [196608, 1024], P('row', 'col'), may hold values from -6 to 6
- test_matrix: float32 [1024, 128], P('col'), may hold values from -0.1875 to 0.1875
- prior_sketch: float32 [196608, 128], P(('row', 'col')), may hold values from -180 to 180, as said below
Outputs:
- basis: float32 [196608, 128], P(('row', 'col'))
- projected: float32 [128, 1024], P('row', 'col')
Inputs may be any that keep to these rules, and one draw needn't show every extreme that they name: `prior_sketch`: real entries of full rank; columns differ in scale.
All inputs are finite; a program needn't handle non-finite values.
Results may differ from a plain program's by a relative error of at most 0.0003.
Values sent between devices are 32-bit elements; how exact they have to be, the bound alone decides.
No kernel may reach another device: no remote copies, remote signals or barrier semaphores. Data moves between devices by JAX's collectives and lax.ppermute only.
A program may use at most 128 MiB of HBM per device.

v0:
```python
import jax
import jax.numpy as jnp
from jax import lax
from jax.sharding import PartitionSpec as P

HIGH = lax.Precision.HIGHEST


def gram_of(block):
    return jnp.dot(block.T, block, precision=HIGH, preferred_element_type=jnp.float32)


def lower_factor(own):
    gram = gram_of(own)
    total = lax.psum(gram, ("row", "col"))
    return jnp.linalg.cholesky(total)


def solve_rows(lower, block):
    return lax.linalg.triangular_solve(lower, block.T, left_side=True, lower=True)


def shards(panel, test_matrix, prior_sketch):
    rows_dev = panel.shape[0]
    term = jnp.dot(panel, test_matrix, precision=HIGH, preferred_element_type=jnp.float32)
    own = lax.psum_scatter(term, "col", scatter_dimension=0, tiled=True) + prior_sketch
    lower = lower_factor(own)
    own_basis = solve_rows(lower, own).T
    partial_sums = jnp.dot(
        lax.all_gather(own_basis, "col", axis=0, tiled=True).T,
        panel,
        precision=HIGH,
        preferred_element_type=jnp.float32,
    )
    projected = lax.psum_scatter(partial_sums, "row", scatter_dimension=0, tiled=True)
    scale = jnp.sqrt(jnp.float32(rows_dev * lax.axis_size("row")))
    return (own_basis * scale, projected)


def solution(mesh):
    placed = (P("row", "col"), P("col", None), P(("row", "col"), None))
    return jax.shard_map(
        shards,
        mesh=mesh,
        in_specs=placed,
        out_specs=(P(("row", "col"), None), P("row", "col")),
        check_vma=False,
    )
```

profile of v0, /device:TPU:1, one launch (start us, length us, event | category | flops | bytes accessed | tf_op | source)
XLA Modules:
  0.0 371.2 jit_solution(6926164240268235535)
XLA Ops:
  7.2 0.0 reduce-scatter.2.cloned.1.call-start
  7.2 0.8 copy-done
  8.0 8.8 %fusion.4 = f32[12288,128]{1,0:T(8,128)} fusion(f32[12288,128]{1,0:T(8,128)} %param.3, f32[128,128]{1,0:T(8,128)S(1)} %copy-done), kind=kOutput, calls=%fused_computation.12 | convolution fusion | flops 2415919104 | bytes 12648448 | tf_op jit(solution)/shard_map/dot_general | solution.py:25
  16.9 0.0 all-reduce.4.cloned.1.call-start
  16.9 45.2 %reduce-scatter.2.cloned.1.call-done = f32[1536,128]{1,0:T(8,128)} async-done(((f32[12288,128]{1,0:T(8,128)}), f32[1536,128]{1,0:T(8,128)}) %reduce-scatter.2.cloned.1.call-update) | async-done | bytes 786448 | tf_op jit(solution)/shard_map/reduce_scatter | solution.py:26
  62.1 1.2 add.20
  63.4 2.0 fusion.5
  65.4 0.0 all-reduce.4.cloned.1.call-update
  65.4 0.0 all-gather.2.cloned.1.call-start
  65.5 140.1 %all-reduce.4.cloned.1.call-done = f32[128,128]{0,1:T(8,128)} async-done(((f32[128,128]{0,1:T(8,128)}), f32[128,128]{0,1:T(8,128)}) %all-reduce.4.cloned.1.call-update) | async-done | bytes 65552 | tf_op jit(solution)/shard_map/psum | solution.py:15
  205.5 0.9 copy.8
  206.5 0.9 fusion.3
  207.3 11.7 %cholesky.16 = f32[128,128]{1,0:T(8,128)S(1)} custom-call(f32[128,128]{1,0:T(8,128)S(1)} %fusion.3), custom_call_target="Cholesky" | custom-call | tf_op jit(solution)/shard_map/jit(cholesky)/cholesky | solution.py:16
  219.1 0.6 compare_reduce_fusion
  219.7 0.7 fusion
  220.4 9.8 %custom-call.6 = f32[1,128,128]{1,2,0:T(8,128)S(1)} custom-call(f32[1,128,128]{2,1,0:T(8,128)S(1)} %fusion), custom_call_target="InvertDiagBlocksLowerTriangular" | custom-call | tf_op jit(solution)/shard_map/triangular_solve | solution.py:20
  230.2 1.9 broadcast_multiply_fusion
  232.1 0.0 all-gather.2.cloned.1.call-update
  232.1 0.2 all-reduce.6.cloned.1.call-start
  232.4 38.1 %all-gather.2.cloned.1.call-done = f32[12288,128]{1,0:T(8,128)} async-done(((f32[1536,128]{1,0:T(8,128)}), f32[12288,128]{1,0:T(8,128)}) %all-gather.2.cloned.1.call-update) | async-done | bytes 6291472 | tf_op jit(solution)/shard_map/all_gather | solution.py:30
  270.4 13.7 %fusion.6 = f32[128,128]{1,0:T(8,128)} fusion(f32[12288,128]{1,0:T(8,128)} %all-gather.2.cloned.1.call-done, f32[12288,128]{1,0:T(8,128)} %param.3), kind=kOutput, calls=%fused_computation.14 | convolution fusion | flops 2415919104 | bytes 12648448 | tf_op jit(solution)/shard_map/dot_general | solution.py:29
  284.1 0.6 dynamic-slice
  285.4 78.0 %all-reduce.6.cloned.1.call-done = f32[128,128]{1,0:T(8,128)} async-done(((f32[128,128]{1,0:T(8,128)}), f32[128,128]{1,0:T(8,128)}) %all-reduce.6.cloned.1.call-update) | async-done | bytes 65552
  363.4 1.3 constant_dynamic-slice_fusion
  (8 shorter events, 0.1 us)
Async XLA Ops:
  7.2 0.8 copy-start
  7.2 55.0 %reduce-scatter.2.cloned.1.call-start = ((), (), s32[]{:S(2)}) async-start(), calls=%async_computation.1 | async-start | bytes 7077888 | tf_op jit(solution)/shard_map/reduce_scatter | solution.py:26
  16.8 45.3 %copy-start.1 = (f32[1536,128]{1,0:T(8,128)S(1)}, f32[1536,128]{1,0:T(8,128)}, u32[]{:S(2)}) copy-start(f32[1536,128]{1,0:T(8,128)} %param.5) | copy-start | bytes 2359300
  16.9 188.7 %all-reduce.4.cloned.1.call-start = ((), (), s32[]{:S(2)}) async-start(), calls=%async_computation.2 | async-start | bytes 131072 | tf_op jit(solution)/shard_map/psum | solution.py:15
  65.4 205.0 %all-gather.2.cloned.1.call-start = ((), (), s32[]{:S(2)}) async-start(), calls=%async_computation.3 | async-start | bytes 7077888 | tf_op jit(solution)/shard_map/all_gather | solution.py:30
  232.1 52.0 %copy-start.2 = (u32[128]{0:T(128)S(1)}, u32[128]{0:T(128)}, u32[]{:S(2)}) copy-start(u32[128]{0:T(128)} %constant.45) | copy-start | bytes 1540
  232.1 131.3 %all-reduce.6.cloned.1.call-start = ((), (), s32[]{:S(2)}) async-start(), calls=%async_computation.4 | async-start | bytes 131072
Sparse Core Ops, SparseCore 0:
  17.0 45.0 reduce-scatter.1
  67.5 138.0 all-reduce.3
  232.2 38.1 all-gather.1
  284.2 79.1 all-reduce.5
where the time goes:
time: 372 us; the launch traced here: 371 us
  waiting for transfers between devices  301 us (81%)
  matrix products  26.4 us (7%)
  other arithmetic  24.9 us (7%)
  between operations  14.5 us (4%)
    psum x1, waiting for transfers between devices, lower_factor(): total = lax.psum(gram, ('row', 'col'))  140 us
    unnamed x5, waiting for transfers between devices  78.1 us
    reduce_scatter x1, waiting for transfers between devices, shards(): lax.psum_scatter(term, 'col', scatter_dimension=0, tiled=True)  45.2 us
    all_gather x1, waiting for transfers between devices, shards(): lax.all_gather(own_basis, 'col', axis=0, tiled=True)  38.1 us
    dot_general x1, matrix products, shards(): jnp.dot(lax.all_gather(own_basis, 'col', axis=0, tiled=True).T, panel, pr...  13.7 us
    another operation x3, other arithmetic, lower_factor(): return jnp.linalg.cholesky(total)  12.4 us
    another operation x2, other arithmetic, solve_rows(): lax.linalg.triangular_solve(lower, block.T, left_side=True, lower=True)  10.5 us
    dot_general x1, matrix products, shards(): jnp.dot(panel, test_matrix, precision=HIGH, preferred_element_type=jnp.fl...  8.84 us
  transfers between devices with their start and end apart: 4, of which 4 were waited for; matrix products, arithmetic and copies ran while one was open for 0% of the time, Pallas kernels for 0%

commit v1 on v0

v1 whole, which is shorter than its diff:
```python
import jax
import jax.numpy as jnp
from jax import lax
from jax.sharding import Mesh, PartitionSpec as P

HIGH = lax.Precision.HIGH
HIGHEST = lax.Precision.HIGHEST
AXES = ("y", "z", "x", "core")


def shift(block, axis, by):
    n = lax.axis_size(axis)
    return lax.ppermute(block, axis, [(i, (i + by) % n) for i in range(n)])


def swap(block):
    return shift(block, "core", 1)


def axis_sum(block, axis):
    near = block + shift(block, axis, 1)
    return near + shift(near, axis, 2)


def axis_scatter(block, axis):
    me = lax.axis_index(axis)
    n = lax.axis_size(axis)
    parts = block.reshape((n, block.shape[0] // n) + block.shape[1:])
    take = lambda i: lax.dynamic_index_in_dim(parts, (me + i) % n, 0, keepdims=False)
    total = take(0)
    for by in (2, 1, 3):
        total = total + shift(take(by), axis, by)
    return total


def dot(a, b, precision=HIGH):
    return jnp.dot(a, b, precision=precision, preferred_element_type=jnp.float32)


def shards(panel, test_matrix, prior_sketch):
    x = lax.axis_index("x")
    core = lax.axis_index("core")
    rows = prior_sketch.shape[0]
    half = rows // 2
    rank = prior_sketch.shape[1]
    cols = panel.shape[1]
    total_rows = panel.shape[0] * lax.axis_size("y") * lax.axis_size("z")

    blocks = panel.reshape(4, 2, rows, cols)
    pick = lambda d, c: lax.dynamic_slice(blocks, (d, c, 0, 0), (1, 1, rows, cols))[0, 0]
    test_other = swap(test_matrix)
    mine, other, part = [], [], []
    for step in (2, 1, 3, 0):
        d = (x + step) % 4
        mine.append(pick(d, core))
        other.append(swap(pick(d, 1 - core)))
        part.append(dot(mine[-1], test_matrix) + dot(other[-1], test_other))
    far, right, left, here = part

    far_top = shift(far[:half], "x", 1)
    far_bot = shift(far[half:], "x", 3)
    near_bot = shift(right[half:], "x", 1)
    near_top = shift(left[:half], "x", 3)
    both_top = shift(right[:half] + far_top, "x", 1)
    both_bot = shift(left[half:] + far_bot, "x", 3)
    base = here + prior_sketch
    own_top = base[:half] + near_top + both_top
    own_bot = base[half:] + near_bot + both_bot

    from_left_bot = shift(own_bot, "x", 1)
    from_right_top = shift(own_top, "x", 3)
    from_left_top = shift(own_top, "x", 1)
    from_right_bot = shift(own_bot, "x", 3)
    from_far_bot = shift(from_left_bot, "x", 1)
    from_far_top = shift(from_right_top, "x", 3)

    own = jnp.concatenate([own_top, own_bot], 0)
    gram = dot(own.T, own, HIGHEST)
    for axis in ("y", "z", "x"):
        gram = axis_sum(gram, axis)
    gram = gram + swap(gram)
    lower = jnp.linalg.cholesky(gram)
    inverse = lax.linalg.triangular_solve(
        lower, jnp.eye(rank, dtype=jnp.float32), left_side=True, lower=True
    )
    scale = jnp.sqrt(jnp.float32(total_rows))
    basis = dot(own, inverse.T * scale, HIGHEST)

    tops = (from_far_top, from_right_top, from_left_top, own_top)
    bots = (from_far_bot, from_right_bot, from_left_bot, own_bot)
    keep = jnp.zeros((rank, cols), jnp.float32)
    give = jnp.zeros((rank, cols), jnp.float32)
    for order in (3, 1, 2, 0):
        for rows_in, span in ((tops, slice(0, half)), (bots, slice(half, rows))):
            keep = keep + dot(rows_in[order].T, mine[order][span])
            give = give + dot(rows_in[order].T, other[order][span])
    weights = dot(inverse, keep + swap(give), HIGHEST)
    projected = axis_scatter(axis_scatter(weights, "y"), "z")
    return basis, projected


def solution(mesh):
    fine = Mesh(mesh.devices.reshape(4, 4, 4, 2), AXES)
    return jax.shard_map(
        shards,
        mesh=fine,
        in_specs=(P(("y", "z"), ("x", "core")), P(("x", "core"), None), P(AXES, None)),
        out_specs=(P(AXES, None), P(("y", "z"), ("x", "core"))),
        check_vma=False,
    )
```

time: 372 us -> 152 us (0.41)
  waiting for transfers between devices: 301 us -> 46.9 us
  starting transfers between devices: 0.34 us -> 41.9 us
  between operations: 14.5 us -> 1.08 us
  matrix products: 26.4 us -> 30.9 us
    psum x1 -> x0, waiting for transfers between devices: 140 us -> none  [lower_factor(): total = lax.psum(gram, ('row', 'col'))]
    unnamed x5 -> x0, waiting for transfers between devices: 78.1 us -> none
    ppermute x0 -> x31, waiting for transfers between devices: none -> 46.9 us  [shift(): return lax.ppermute(block, axis, [(i, (i + by) % n) for i in range(n)])]
    reduce_scatter x1 -> x0, waiting for transfers between devices: 45.2 us -> none  [shards(): lax.psum_scatter(term, 'col', scatter_dimension=0, tiled=True)]
    ppermute x0 -> x31, starting transfers between devices: none -> 41.9 us  [shift(): return lax.ppermute(block, axis, [(i, (i + by) % n) for i in range(n)])]
    all_gather x1 -> x0, waiting for transfers between devices: 38.1 us -> none  [shards(): lax.all_gather(own_basis, 'col', axis=0, tiled=True)]
    dot_general x3 -> x27, matrix products: 24.5 us -> 30.7 us  [dot(): jnp.dot(a, b, precision=precision, preferred_element_type=jnp.float32)]
  transfers between devices with their start and end apart: 4 -> 31, of which waited for: 4 -> 10; matrix products, arithmetic and copies ran while one was open for 0% -> 34% of each run, Pallas kernels for 0% -> 0%
where the time goes in v1:
time: 152 us; the launch traced here: 150 us
  waiting for transfers between devices  46.9 us (31%)
  starting transfers between devices  41.9 us (28%)
  matrix products  30.9 us (20%)
  other arithmetic  25.3 us (17%)
  local copies, waits for them, and re-layouts  3.77 us (2%)
    ppermute x31, waiting for transfers between devices, shift(): return lax.ppermute(block, axis, [(i, (i + by) % n) for i in range(n)])  46.9 us
    ppermute x31, starting transfers between devices, shift(): return lax.ppermute(block, axis, [(i, (i + by) % n) for i in range(n)])  41.9 us
    dot_general x27, matrix products, dot(): jnp.dot(a, b, precision=precision, preferred_element_type=jnp.float32)  30.7 us
    another operation x3, other arithmetic, shards(): lower = jnp.linalg.cholesky(gram)  12.4 us
    another operation x2, other arithmetic, shards(): lax.linalg.triangular_solve(lower, jnp.eye(rank, dtype=jnp.float32), left...  10.5 us
    squeeze x1, local copies, waits for them, and re-layouts, shards(): lax.dynamic_slice(blocks, (d, c, 0, 0), (1, 1, rows, cols))[0, 0]  3.58 us
  transfers between devices with their start and end apart: 31, of which 10 were waited for; matrix products, arithmetic and copies ran while one was open for 34% of the time, Pallas kernels for 0%

profile of v1, /device:TPU:1, one launch (start us, length us, event | category | flops | bytes accessed | tf_op | source)
XLA Modules:
  0.0 149.9 jit_solution(10180333001515577986)
XLA Ops:
  0.7 3.6 %dynamic-slice_bitcast_fusion.3 = (f32[1536,128]{1,0:T(8,128)}, f32[1536,128]{1,0:T(8,128)}, f32[1536,128]{1,0:T(8,128)}, f32[1536,128]{1,0:T(8,128)}) fusion(f32[4,2,1536,128]{3,2,1,0:T(8,128)} %bitcast.115, s32[]{:T(128)S(6)} %select_n.110, s32[]{:T(128)S(6)} %select_n.112, s32[]{:T(128)S(6)} %select_n.118, s32[]{:T(128)S(6)} %select_n.116, s32[]{:T(128)S(6)} %select_n.114), kind=kLoop, calls=%fused_computation.35 | loop fusion | bytes 6291476 | tf_op jit(solution)/shard_map/squeeze | solution.py:50
  12.1 2.6 %collective-permute-start.9 = (f32[768,128]{1,0:T(8,128)S(1)}, f32[768,128]{1,0:T(8,128)S(1)}, u32[]{:S(2)}, u32[]{:S(2)}) collective-permute-start(f32[768,128]{1,0:T(8,128)S(1)} %get-tuple-element.13), channel_id=1, source_target_pairs={{0,6},{2,0},{4,2},{6,4},{1,7},{3,1},{5,3},{7,5},{8,14},{10,8},{12,... | collective-permute-start | bytes 1179656 | tf_op jit(solution)/shard_map/ppermute | solution.py:13
  15.8 7.5 %collective-permute-done.9 = f32[768,128]{1,0:T(8,128)S(1)} collective-permute-done((f32[768,128]{1,0:T(8,128)S(1)}, f32[768,128]{1,0:T(8,128)S(1)}, u32[]{:S(2)}, u32[]{:S(2)}) %collective-permute-start.9) | collective-permute-done | bytes 393248 | tf_op jit(solution)/shard_map/ppermute | solution.py:13
  23.3 3.5 %collective-permute-start.10 = (f32[768,128]{1,0:T(8,128)S(1)}, f32[768,128]{1,0:T(8,128)S(1)}, u32[]{:S(2)}, u32[]{:S(2)}) collective-permute-start(f32[768,128]{1,0:T(8,128)S(1)} %get-tuple-element.9), channel_id=1, source_target_pairs={{0,6},{2,0},{4,2},{6,4},{1,7},{3,1},{5,3},{7,5},{8,14},{10,8},{12,... | collective-permute-start | bytes 1179656 | tf_op jit(solution)/shard_map/ppermute | solution.py:13
  30.6 3.8 %collective-permute-done.10 = f32[768,128]{1,0:T(8,128)S(1)} collective-permute-done((f32[768,128]{1,0:T(8,128)S(1)}, f32[768,128]{1,0:T(8,128)S(1)}, u32[]{:S(2)}, u32[]{:S(2)}) %collective-permute-start.10) | collective-permute-done | bytes 393248 | tf_op jit(solution)/shard_map/ppermute | solution.py:13
  34.4 8.4 %collective-permute-done.3 = f32[768,128]{1,0:T(8,128)S(1)} collective-permute-done((f32[768,128]{1,0:T(8,128)S(1)}, f32[768,128]{1,0:T(8,128)S(1)}, u32[]{:S(2)}, u32[]{:S(2)}) %collective-permute-start.3) | collective-permute-done | bytes 393248 | tf_op jit(solution)/shard_map/ppermute | solution.py:13
  42.8 3.3 %collective-permute-done.8 = f32[768,128]{1,0:T(8,128)S(1)} collective-permute-done((f32[768,128]{1,0:T(8,128)S(1)}, f32[768,128]{1,0:T(8,128)S(1)}, u32[]{:S(2)}, u32[]{:S(2)}) %collective-permute-start.8) | collective-permute-done | bytes 393248 | tf_op jit(solution)/shard_map/ppermute | solution.py:13
  49.0 3.1 %collective-permute-done.11 = f32[128,128]{0,1:T(8,128)S(1)} collective-permute-done((f32[128,128]{0,1:T(8,128)S(1)}, f32[128,128]{0,1:T(8,128)S(1)}, u32[]{:S(2)}, u32[]{:S(2)}) %collective-permute-start.11) | collective-permute-done | bytes 65568 | tf_op jit(solution)/shard_map/ppermute | solution.py:13
  52.1 1.7 %collective-permute-start.12 = (f32[128,128]{0,1:T(8,128)S(1)}, f32[128,128]{0,1:T(8,128)S(1)}, u32[]{:S(2)}, u32[]{:S(2)}) collective-permute-start(f32[128,128]{0,1:T(8,128)S(1)} %add.271), channel_id=1, source_target_pairs={{0,64},{32,96},{64,0},{96,32},{1,65},{33,97},{65,1},{97,33},{2,66}... | collective-permute-start | bytes 196616 | tf_op jit(solution)/shard_map/ppermute | solution.py:13
  53.8 3.0 %collective-permute-done.12 = f32[128,128]{0,1:T(8,128)S(1)} collective-permute-done((f32[128,128]{0,1:T(8,128)S(1)}, f32[128,128]{0,1:T(8,128)S(1)}, u32[]{:S(2)}, u32[]{:S(2)}) %collective-permute-start.12) | collective-permute-done | bytes 65568 | tf_op jit(solution)/shard_map/ppermute | solution.py:13
  56.8 1.7 %collective-permute-start.13 = (f32[128,128]{0,1:T(8,128)S(1)}, f32[128,128]{0,1:T(8,128)S(1)}, u32[]{:S(2)}, u32[]{:S(2)}) collective-permute-start(f32[128,128]{0,1:T(8,128)S(1)} %add.272), channel_id=1, source_target_pairs={{0,8},{8,16},{16,24},{24,0},{1,9},{9,17},{17,25},{25,1},{2,10},{10... | collective-permute-start | bytes 196616 | tf_op jit(solution)/shard_map/ppermute | solution.py:13
  58.5 3.8 %collective-permute-done.13 = f32[128,128]{0,1:T(8,128)S(1)} collective-permute-done((f32[128,128]{0,1:T(8,128)S(1)}, f32[128,128]{0,1:T(8,128)S(1)}, u32[]{:S(2)}, u32[]{:S(2)}) %collective-permute-start.13) | collective-permute-done | bytes 65568 | tf_op jit(solution)/shard_map/ppermute | solution.py:13
  64.6 2.7 %collective-permute-start.19 = (f32[768,128]{1,0:T(8,128)S(1)}, f32[768,128]{1,0:T(8,128)S(1)}, u32[]{:S(2)}, u32[]{:S(2)}) collective-permute-start(f32[768,128]{1,0:T(8,128)S(1)} %get-tuple-element.7), channel_id=1, source_target_pairs={{0,6},{2,0},{4,2},{6,4},{1,7},{3,1},{5,3},{7,5},{8,14},{10,8},{12,... | collective-permute-start | bytes 1179656 | tf_op jit(solution)/shard_map/ppermute | solution.py:13
  67.2 2.7 %collective-permute-start.18 = (f32[768,128]{1,0:T(8,128)S(1)}, f32[768,128]{1,0:T(8,128)}, u32[]{:S(2)}, u32[]{:S(2)}) collective-permute-start(f32[768,128]{1,0:T(8,128)S(1)} %get-tuple-element.6), channel_id=1, source_target_pairs={{0,6},{2,0},{4,2},{6,4},{1,7},{3,1},{5,3},{7,5},{8,14},{10,8},{12,... | collective-permute-start | bytes 1179656 | tf_op jit(solution)/shard_map/ppermute | solution.py:13
  71.4 9.4 %collective-permute-done.15 = f32[128,128]{0,1:T(8,128)S(1)} collective-permute-done((f32[128,128]{0,1:T(8,128)S(1)}, f32[128,128]{0,1:T(8,128)S(1)}, u32[]{:S(2)}, u32[]{:S(2)}) %collective-permute-start.15) | collective-permute-done | bytes 65568 | tf_op jit(solution)/shard_map/ppermute | solution.py:13
  82.4 3.5 %collective-permute-done.16 = f32[128,128]{0,1:T(8,128)S(1)} collective-permute-done((f32[128,128]{0,1:T(8,128)S(1)}, f32[128,128]{0,1:T(8,128)S(1)}, u32[]{:S(2)}, u32[]{:S(2)}) %collective-permute-start.16) | collective-permute-done | bytes 65568 | tf_op jit(solution)/shard_map/ppermute | solution.py:13
  85.9 7.9 %collective-permute-start.17 = (f32[128,128]{0,1:T(8,128)S(1)}, f32[128,128]{0,1:T(8,128)S(1)}, u32[]{:S(2)}, u32[]{:S(2)}) collective-permute-start(f32[128,128]{0,1:T(8,128)S(1)} %add.276), channel_id=1, source_target_pairs={{0,1},{1,0},{2,3},{3,2},{4,5},{5,4},{6,7},{7,6},{8,9},{9,8},{10,11... | collective-permute-start | bytes 196616 | tf_op jit(solution)/shard_map/ppermute | solution.py:13
  99.9 2.1 %fusion.11 = f32[128,128]{1,0:T(8,128)} fusion(f32[128,128]{1,0:T(8,128)S(1)} %fusion.41, f32[128,128]{1,0:T(8,128)S(1)} %fusion.42, f32[128,128]{1,0:T(8,128)S(1)} %fusion.43, f32[128,128]{1,0:T(8,128)S(1)} %fusion.44, f32[128,128]{1,0:T(8,128)S(1)} %fusion.45, f32[768,128]{1,0:T(8,128)S(1)} %get-tuple-element.6, f32[4,2,1536,128]{3,2,1,0:T(8,128)} %bitcast.125, ...), kind=kOutput, calls=%fused_computation.19 | convolution fusion | flops 75579392 | bytes 1179656 | tf_op jit(solution)/shard_map/dot_general | solution.py:37
  105.1 2.7 %collective-permute-start.22 = (f32[768,128]{1,0:T(8,128)}, f32[768,128]{1,0:T(8,128)S(1)}, u32[]{:S(2)}, u32[]{:S(2)}) collective-permute-start(f32[768,128]{1,0:T(8,128)} %collective-permute-done.18), channel_id=1, source_target_pairs={{0,6},{2,0},{4,2},{6,4},{1,7},{3,1},{5,3},{7,5},{8,14},{10,8},{12,... | collective-permute-start | bytes 1179656 | tf_op jit(solution)/shard_map/ppermute | solution.py:13
  109.1 11.7 %cholesky.17 = f32[128,128]{1,0:T(8,128)S(1)} custom-call(f32[128,128]{1,0:T(8,128)S(1)} %fusion.51), custom_call_target="Cholesky" | custom-call | tf_op jit(solution)/shard_map/jit(cholesky)/cholesky | solution.py:82
  122.1 9.8 %custom-call.6 = f32[1,128,128]{1,2,0:T(8,128)S(1)} custom-call(f32[1,128,128]{2,1,0:T(8,128)S(1)} %fusion.48), custom_call_target="InvertDiagBlocksLowerTriangular" | custom-call | tf_op jit(solution)/shard_map/triangular_solve | solution.py:83
  137.9 1.7 %collective-permute-start.25 = (f32[32,128]{1,0:T(8,128)S(1)}, f32[32,128]{1,0:T(8,128)S(1)}, u32[]{:S(2)}, u32[]{:S(2)}) collective-permute-start(f32[32,128]{1,0:T(8,128)S(1)} %get-tuple-element.14), channel_id=1, source_target_pairs={{0,64},{32,96},{64,0},{96,32},{1,65},{33,97},{65,1},{97,33},{2,66}... | collective-permute-start | bytes 49160 | tf_op jit(solution)/shard_map/ppermute | solution.py:13
  140.0 2.3 %collective-permute-start.27 = (f32[32,128]{1,0:T(8,128)S(1)}, f32[32,128]{1,0:T(8,128)S(1)}, u32[]{:S(2)}, u32[]{:S(2)}) collective-permute-start(f32[32,128]{1,0:T(8,128)S(1)} %get-tuple-element.15), channel_id=1, source_target_pairs={{0,96},{32,0},{64,32},{96,64},{1,97},{33,1},{65,33},{97,65},{2,98}... | collective-permute-start | bytes 49160 | tf_op jit(solution)/shard_map/ppermute | solution.py:13
  144.9 2.7 %collective-permute-start.30 = (f32[8,128]{1,0:T(8,128)S(1)}, f32[8,128]{1,0:T(8,128)S(1)}, u32[]{:S(2)}, u32[]{:S(2)}) collective-permute-start(f32[8,128]{1,0:T(8,128)S(1)} %get-tuple-element.18), channel_id=1, source_target_pairs={{0,24},{8,0},{16,8},{24,16},{1,25},{9,1},{17,9},{25,17},{2,26},{10... | collective-permute-start | bytes 12296 | tf_op jit(solution)/shard_map/ppermute | solution.py:13
  (97 shorter events, 43.7 us)
Async XLA Ops:
  4.3 7.3 %collective-permute-start.5 = (f32[1536,128]{1,0:T(8,128)}, f32[1536,128]{1,0:T(8,128)S(1)}, u32[]{:S(2)}, u32[]{:S(2)}) collective-permute-start(f32[1536,128]{1,0:T(8,128)} %get-tuple-element.3), channel_id=1, source_target_pairs={{0,1},{1,0},{2,3},{3,2},{4,5},{5,4},{6,7},{7,6},{8,9},{9,8},{10,11... | collective-permute-start | bytes 2359304 | tf_op jit(solution)/shard_map/ppermute | solution.py:13
  5.7 5.9 %collective-permute-start.1 = (f32[128,128]{1,0:T(8,128)S(1)}, f32[128,128]{1,0:T(8,128)S(1)}, u32[]{:S(2)}, u32[]{:S(2)}) collective-permute-start(f32[128,128]{1,0:T(8,128)S(1)} %copy-done.2), channel_id=1, source_target_pairs={{0,1},{1,0},{2,3},{3,2},{4,5},{5,4},{6,7},{7,6},{8,9},{9,8},{10,11... | collective-permute-start | bytes 196616 | tf_op jit(solution)/shard_map/ppermute | solution.py:13
  5.8 9.0 %collective-permute-start.2 = (f32[1536,128]{1,0:T(8,128)}, f32[1536,128]{1,0:T(8,128)S(1)}, u32[]{:S(2)}, u32[]{:S(2)}) collective-permute-start(f32[1536,128]{1,0:T(8,128)} %get-tuple-element.5), channel_id=1, source_target_pairs={{0,1},{1,0},{2,3},{3,2},{4,5},{5,4},{6,7},{7,6},{8,9},{9,8},{10,11... | collective-permute-start | bytes 2359304 | tf_op jit(solution)/shard_map/ppermute | solution.py:13
  6.2 9.1 %collective-permute-start.4 = (f32[1536,128]{1,0:T(8,128)}, f32[1536,128]{1,0:T(8,128)S(1)}, u32[]{:S(2)}, u32[]{:S(2)}) collective-permute-start(f32[1536,128]{1,0:T(8,128)} %get-tuple-element.4), channel_id=1, source_target_pairs={{0,1},{1,0},{2,3},{3,2},{4,5},{5,4},{6,7},{7,6},{8,9},{9,8},{10,11... | collective-permute-start | bytes 2359304 | tf_op jit(solution)/shard_map/ppermute | solution.py:13
  6.3 23.8 %collective-permute-start = (f32[1536,128]{1,0:T(8,128)}, f32[1536,128]{1,0:T(8,128)S(1)}, u32[]{:S(2)}, u32[]{:S(2)}) collective-permute-start(f32[1536,128]{1,0:T(8,128)} %get-tuple-element.2), channel_id=1, source_target_pairs={{0,1},{1,0},{2,3},{3,2},{4,5},{5,4},{6,7},{7,6},{8,9},{9,8},{10,11... | collective-permute-start | bytes 2359304 | tf_op jit(solution)/shard_map/ppermute | solution.py:13
  12.1 11.1 %collective-permute-start.9 = (f32[768,128]{1,0:T(8,128)S(1)}, f32[768,128]{1,0:T(8,128)S(1)}, u32[]{:S(2)}, u32[]{:S(2)}) collective-permute-start(f32[768,128]{1,0:T(8,128)S(1)} %get-tuple-element.13), channel_id=1, source_target_pairs={{0,6},{2,0},{4,2},{6,4},{1,7},{3,1},{5,3},{7,5},{8,14},{10,8},{12,... | collective-permute-start | bytes 1179656 | tf_op jit(solution)/shard_map/ppermute | solution.py:13
  14.8 12.1 %collective-permute-start.6 = (f32[768,128]{1,0:T(8,128)S(1)}, f32[768,128]{1,0:T(8,128)S(1)}, u32[]{:S(2)}, u32[]{:S(2)}) collective-permute-start(f32[768,128]{1,0:T(8,128)S(1)} %get-tuple-element.12), channel_id=1, source_target_pairs={{0,2},{2,4},{4,6},{6,0},{1,3},{3,5},{5,7},{7,1},{8,10},{10,12},{12... | collective-permute-start | bytes 1179656 | tf_op jit(solution)/shard_map/ppermute | solution.py:13
  23.3 11.0 %collective-permute-start.10 = (f32[768,128]{1,0:T(8,128)S(1)}, f32[768,128]{1,0:T(8,128)S(1)}, u32[]{:S(2)}, u32[]{:S(2)}) collective-permute-start(f32[768,128]{1,0:T(8,128)S(1)} %get-tuple-element.9), channel_id=1, source_target_pairs={{0,6},{2,0},{4,2},{6,4},{1,7},{3,1},{5,3},{7,5},{8,14},{10,8},{12,... | collective-permute-start | bytes 1179656 | tf_op jit(solution)/shard_map/ppermute | solution.py:13
  26.8 16.0 %collective-permute-start.3 = (f32[768,128]{1,0:T(8,128)S(1)}, f32[768,128]{1,0:T(8,128)S(1)}, u32[]{:S(2)}, u32[]{:S(2)}) collective-permute-start(f32[768,128]{1,0:T(8,128)S(1)} %get-tuple-element.8), channel_id=1, source_target_pairs={{0,6},{2,0},{4,2},{6,4},{1,7},{3,1},{5,3},{7,5},{8,14},{10,8},{12,... | collective-permute-start | bytes 1179656 | tf_op jit(solution)/shard_map/ppermute | solution.py:13
  27.0 15.8 %collective-permute-start.7 = (f32[768,128]{1,0:T(8,128)S(1)}, f32[768,128]{1,0:T(8,128)S(1)}, u32[]{:S(2)}, u32[]{:S(2)}) collective-permute-start(f32[768,128]{1,0:T(8,128)S(1)} %get-tuple-element.10), channel_id=1, source_target_pairs={{0,2},{2,4},{4,6},{6,0},{1,3},{3,5},{5,7},{7,1},{8,10},{10,12},{12... | collective-permute-start | bytes 1179656 | tf_op jit(solution)/shard_map/ppermute | solution.py:13
  28.4 17.7 %collective-permute-start.8 = (f32[768,128]{1,0:T(8,128)S(1)}, f32[768,128]{1,0:T(8,128)S(1)}, u32[]{:S(2)}, u32[]{:S(2)}) collective-permute-start(f32[768,128]{1,0:T(8,128)S(1)} %get-tuple-element.11), channel_id=1, source_target_pairs={{0,2},{2,4},{4,6},{6,0},{1,3},{3,5},{5,7},{7,1},{8,10},{10,12},{12... | collective-permute-start | bytes 1179656 | tf_op jit(solution)/shard_map/ppermute | solution.py:13
  52.1 4.7 %collective-permute-start.12 = (f32[128,128]{0,1:T(8,128)S(1)}, f32[128,128]{0,1:T(8,128)S(1)}, u32[]{:S(2)}, u32[]{:S(2)}) collective-permute-start(f32[128,128]{0,1:T(8,128)S(1)} %add.271), channel_id=1, source_target_pairs={{0,64},{32,96},{64,0},{96,32},{1,65},{33,97},{65,1},{97,33},{2,66}... | collective-permute-start | bytes 196616 | tf_op jit(solution)/shard_map/ppermute | solution.py:13
  56.8 5.5 %collective-permute-start.13 = (f32[128,128]{0,1:T(8,128)S(1)}, f32[128,128]{0,1:T(8,128)S(1)}, u32[]{:S(2)}, u32[]{:S(2)}) collective-permute-start(f32[128,128]{0,1:T(8,128)S(1)} %add.272), channel_id=1, source_target_pairs={{0,8},{8,16},{16,24},{24,0},{1,9},{9,17},{17,25},{25,1},{2,10},{10... | collective-permute-start | bytes 196616 | tf_op jit(solution)/shard_map/ppermute | solution.py:13
  63.0 7.0 %collective-permute-start.14 = (f32[128,128]{0,1:T(8,128)}, f32[128,128]{0,1:T(8,128)}, u32[]{:S(2)}, u32[]{:S(2)}) collective-permute-start(f32[128,128]{0,1:T(8,128)} %add.273), channel_id=1, source_target_pairs={{0,16},{8,24},{16,0},{24,8},{1,17},{9,25},{17,1},{25,9},{2,18},{10... | collective-permute-start | bytes 196616 | tf_op jit(solution)/shard_map/ppermute | solution.py:13
  64.6 29.2 %collective-permute-start.21 = (f32[768,128]{1,0:T(8,128)S(1)}, f32[768,128]{1,0:T(8,128)S(1)}, u32[]{:S(2)}, u32[]{:S(2)}) collective-permute-start(f32[768,128]{1,0:T(8,128)S(1)} %get-tuple-element.7), channel_id=1, source_target_pairs={{0,2},{2,4},{4,6},{6,0},{1,3},{3,5},{5,7},{7,1},{8,10},{10,12},{12... | collective-permute-start | bytes 1179656 | tf_op jit(solution)/shard_map/ppermute | solution.py:13
  64.6 30.7 %collective-permute-start.19 = (f32[768,128]{1,0:T(8,128)S(1)}, f32[768,128]{1,0:T(8,128)S(1)}, u32[]{:S(2)}, u32[]{:S(2)}) collective-permute-start(f32[768,128]{1,0:T(8,128)S(1)} %get-tuple-element.7), channel_id=1, source_target_pairs={{0,6},{2,0},{4,2},{6,4},{1,7},{3,1},{5,3},{7,5},{8,14},{10,8},{12,... | collective-permute-start | bytes 1179656 | tf_op jit(solution)/shard_map/ppermute | solution.py:13
  67.2 29.6 %collective-permute-start.20 = (f32[768,128]{1,0:T(8,128)S(1)}, f32[768,128]{1,0:T(8,128)S(1)}, u32[]{:S(2)}, u32[]{:S(2)}) collective-permute-start(f32[768,128]{1,0:T(8,128)S(1)} %get-tuple-element.6), channel_id=1, source_target_pairs={{0,2},{2,4},{4,6},{6,0},{1,3},{3,5},{5,7},{7,1},{8,10},{10,12},{12... | collective-permute-start | bytes 1179656 | tf_op jit(solution)/shard_map/ppermute | solution.py:13
  67.2 31.1 %collective-permute-start.18 = (f32[768,128]{1,0:T(8,128)S(1)}, f32[768,128]{1,0:T(8,128)}, u32[]{:S(2)}, u32[]{:S(2)}) collective-permute-start(f32[768,128]{1,0:T(8,128)S(1)} %get-tuple-element.6), channel_id=1, source_target_pairs={{0,6},{2,0},{4,2},{6,4},{1,7},{3,1},{5,3},{7,5},{8,14},{10,8},{12,... | collective-permute-start | bytes 1179656 | tf_op jit(solution)/shard_map/ppermute | solution.py:13
  70.8 10.0 %collective-permute-start.15 = (f32[128,128]{0,1:T(8,128)S(1)}, f32[128,128]{0,1:T(8,128)S(1)}, u32[]{:S(2)}, u32[]{:S(2)}) collective-permute-start(f32[128,128]{0,1:T(8,128)S(1)} %add.274), channel_id=1, source_target_pairs={{0,2},{2,4},{4,6},{6,0},{1,3},{3,5},{5,7},{7,1},{8,10},{10,12},{12... | collective-permute-start | bytes 196616 | tf_op jit(solution)/shard_map/ppermute | solution.py:13
  80.8 5.1 %collective-permute-start.16 = (f32[128,128]{0,1:T(8,128)S(1)}, f32[128,128]{0,1:T(8,128)S(1)}, u32[]{:S(2)}, u32[]{:S(2)}) collective-permute-start(f32[128,128]{0,1:T(8,128)S(1)} %add.275), channel_id=1, source_target_pairs={{0,4},{2,6},{4,0},{6,2},{1,5},{3,7},{5,1},{7,3},{8,12},{10,14},{12... | collective-permute-start | bytes 196616 | tf_op jit(solution)/shard_map/ppermute | solution.py:13
  85.9 23.1 %collective-permute-start.17 = (f32[128,128]{0,1:T(8,128)S(1)}, f32[128,128]{0,1:T(8,128)S(1)}, u32[]{:S(2)}, u32[]{:S(2)}) collective-permute-start(f32[128,128]{0,1:T(8,128)S(1)} %add.276), channel_id=1, source_target_pairs={{0,1},{1,0},{2,3},{3,2},{4,5},{5,4},{6,7},{7,6},{8,9},{9,8},{10,11... | collective-permute-start | bytes 196616 | tf_op jit(solution)/shard_map/ppermute | solution.py:13
  105.0 27.1 %collective-permute-start.23 = (f32[768,128]{1,0:T(8,128)S(1)}, f32[768,128]{1,0:T(8,128)S(1)}, u32[]{:S(2)}, u32[]{:S(2)}) collective-permute-start(f32[768,128]{1,0:T(8,128)S(1)} %collective-permute-done.21), channel_id=1, source_target_pairs={{0,2},{2,4},{4,6},{6,0},{1,3},{3,5},{5,7},{7,1},{8,10},{10,12},{12... | collective-permute-start | bytes 1179656 | tf_op jit(solution)/shard_map/ppermute | solution.py:13
  105.1 27.5 %collective-permute-start.22 = (f32[768,128]{1,0:T(8,128)}, f32[768,128]{1,0:T(8,128)S(1)}, u32[]{:S(2)}, u32[]{:S(2)}) collective-permute-start(f32[768,128]{1,0:T(8,128)} %collective-permute-done.18), channel_id=1, source_target_pairs={{0,6},{2,0},{4,2},{6,4},{1,7},{3,1},{5,3},{7,5},{8,14},{10,8},{12,... | collective-permute-start | bytes 1179656 | tf_op jit(solution)/shard_map/ppermute | solution.py:13
  143.5 5.8 %collective-permute-start.28 = (f32[8,128]{1,0:T(8,128)S(1)}, f32[8,128]{1,0:T(8,128)S(1)}, u32[]{:S(2)}, u32[]{:S(2)}) collective-permute-start(f32[8,128]{1,0:T(8,128)S(1)} %get-tuple-element.17), channel_id=1, source_target_pairs={{0,16},{8,24},{16,0},{24,8},{1,17},{9,25},{17,1},{25,9},{2,18},{10... | collective-permute-start | bytes 12296 | tf_op jit(solution)/shard_map/ppermute | solution.py:13
  (11 other events, 115.1 us)

commit v2 on v0

v2 whole, which is shorter than its diff:
```python
import functools

import jax
import jax.numpy as jnp
from jax import lax
from jax.experimental import pallas as pl
from jax.experimental.pallas import tpu as pltpu
from jax.sharding import Mesh, PartitionSpec as P

AXES = ("y", "z", "x", "core")
F32 = jnp.float32
BF16 = jnp.bfloat16
LIMIT = 16 * 1024 * 1024
COST = pl.CostEstimate(flops=0, bytes_accessed=0, transcendentals=0)
PARAMS = pltpu.CompilerParams(vmem_limit_bytes=LIMIT)
WHOLE = pl.BlockSpec(memory_space=pltpu.VMEM)
SCALAR = pl.BlockSpec(memory_space=pltpu.SMEM)


def shift(block, axis, by):
    n = lax.axis_size(axis)
    return lax.ppermute(block, axis, [(i, (i + by) % n) for i in range(n)])


def swap(block):
    return shift(block, "core", 1)


def trade(block, axis, stage):
    partner = (3, 2, 1, 0) if stage == 0 else (1, 0, 3, 2)
    return lax.ppermute(block, axis, [(i, partner[i]) for i in range(4)])


def axis_sum(block, axis):
    for stage in (0, 1):
        block = block + trade(block, axis, stage)
    return block


def axis_scatter(block, axis):
    me = lax.axis_index(axis)
    for stage, upper in ((0, me // 2), (1, me % 2)):
        half = block.shape[0] // 2
        keep = lax.dynamic_slice_in_dim(block, upper * half, half, 0)
        give = lax.dynamic_slice_in_dim(block, (1 - upper) * half, half, 0)
        block = keep + trade(give, axis, stage)
    return block


def split(block):
    high = block.astype(BF16)
    return high, (block - high.astype(F32)).astype(BF16)


def mm(a, b):
    return jnp.dot(a, b, preferred_element_type=F32)


def fetch_body(place_ref, panel_ref, *rest, count):
    outs, sems = rest[:count], rest[count]
    rows = outs[0].shape[0]
    copies = []
    for slot, out_ref in enumerate(outs):
        start = pl.multiple_of(place_ref[slot] * rows, rows)
        copies.append(
            pltpu.make_async_copy(panel_ref.at[pl.ds(start, rows), :], out_ref, sems.at[slot])
        )
    for copy in copies:
        copy.start()
    for copy in copies:
        copy.wait()


def fetch(places, panel, rows):
    count = places.shape[0]
    cols = panel.shape[1]
    return pl.pallas_call(
        functools.partial(fetch_body, count=count),
        out_shape=[pltpu.VMEM((rows, cols), F32)] * count,
        in_specs=[SCALAR, pl.BlockSpec(memory_space=pl.ANY)],
        out_specs=[WHOLE] * count,
        scratch_shapes=[pltpu.SemaphoreType.DMA((count,))],
        compiler_params=PARAMS,
        cost_estimate=COST,
        name="fetch",
    )(places, panel)


def term_body(mine_ref, other_ref, test_ref, test_other_ref, *rest, first, spans, block):
    rank = test_ref.shape[1]
    tests = jnp.concatenate([test_ref[...], test_other_ref[...]], 0)
    tests = jnp.concatenate(split(tests), 1)
    out_ref = rest[-1]
    for at in range(0, out_ref.shape[0], block):
        here = slice(first + at, first + at + block)
        high, low = split(jnp.concatenate([mine_ref[here, :], other_ref[here, :]], 1))
        both = mm(low, tests) + mm(high, tests)
        total = both[:, rank:] + both[:, :rank]
        for addend_ref, start in zip(rest[:-1], spans):
            total = total + addend_ref[start + at : start + at + block, :]
        out_ref[at : at + block, :] = total


def term(chunk, first, count, tests, *addends, block=384):
    rank = tests[0].shape[1]
    return pl.pallas_call(
        functools.partial(
            term_body, first=first, spans=[0 for _ in addends], block=block
        ),
        out_shape=pltpu.VMEM((count, rank), F32),
        in_specs=[WHOLE] * (4 + len(addends)),
        out_specs=WHOLE,
        compiler_params=PARAMS,
        cost_estimate=COST,
        name="term",
    )(*chunk, *tests, *addends)


def finish_body(base_ref, near_top_ref, near_bot_ref, both_top_ref, both_bot_ref, own_ref, turned_ref):
    half = near_top_ref.shape[0]
    for part, near_ref, both_ref in ((0, near_top_ref, both_top_ref), (1, near_bot_ref, both_bot_ref)):
        span = slice(part * half, (part + 1) * half)
        own = base_ref[span, :] + near_ref[...] + both_ref[...]
        own_ref[span, :] = own
        turned_ref[part] = own.T


def finish(base, *others):
    rows, rank = base.shape
    return pl.pallas_call(
        finish_body,
        out_shape=(
            pltpu.VMEM((rows, rank), F32),
            pltpu.VMEM((2, rank, rows // 2), F32),
        ),
        in_specs=[WHOLE] * 5,
        out_specs=(WHOLE, WHOLE),
        compiler_params=PARAMS,
        cost_estimate=COST,
        name="finish",
    )(base, *others)


def gram_body(core_ref, own_ref, turned_ref, keep_ref, give_ref, work_ref):
    half = keep_ref.shape[0]
    rows = turned_ref.shape[2]
    dot = functools.partial(jnp.dot, precision=lax.Precision.HIGHEST, preferred_element_type=F32)
    work_ref[...] = dot(turned_ref[0], own_ref[:rows, :]) + dot(turned_ref[1], own_ref[rows:, :])
    core = core_ref[0]
    keep_ref[...] = work_ref[pl.ds(pl.multiple_of(core * half, half), half), :]
    give_ref[...] = work_ref[pl.ds(pl.multiple_of((1 - core) * half, half), half), :]


def gram_of(core, own, turned):
    rank = own.shape[1]
    out = jax.ShapeDtypeStruct((rank // 2, rank), F32)
    return pl.pallas_call(
        gram_body,
        out_shape=(out, out),
        in_specs=[SCALAR] + [WHOLE] * 2,
        out_specs=(WHOLE, WHOLE),
        scratch_shapes=[pltpu.VMEM((rank, rank), F32)],
        compiler_params=PARAMS,
        cost_estimate=COST,
        name="gram",
    )(core, own, turned)


def factor_body(core_ref, mine_ref, other_ref, inverse_ref, turned_ref, *, scale, tile=8):
    half, n = mine_ref.shape
    blocks = n // tile
    first = core_ref[0] == 0
    upper = jnp.where(first, mine_ref[...], other_ref[...])
    lower = jnp.where(first, other_ref[...], mine_ref[...])
    gram = jnp.concatenate([upper, lower], 0)
    row = lax.broadcasted_iota(jnp.int32, (tile, n), 0)
    lane = lax.broadcasted_iota(jnp.int32, (tile, n), 1)
    mat = [gram[tile * r : tile * (r + 1), :] for r in range(blocks)]
    out = [jnp.where(lane == row + tile * r, 1.0, 0.0).astype(F32) for r in range(blocks)]
    for b in range(blocks):
        live = range(b, blocks)
        col = [
            {r: jnp.broadcast_to(mat[r][:, tile * b + s : tile * b + s + 1], (tile, n)) for r in live}
            for s in range(tile)
        ]
        inv = []
        for s in range(tile):
            inv.append(lax.rsqrt(col[s][b][s : s + 1, :]))
            for r in live:
                col[s][r] = col[s][r] * inv[s]
            for t in range(s + 1, tile):
                factor = col[s][b][t : t + 1, :]
                for r in live:
                    col[t][r] = col[t][r] - col[s][r] * factor
        top, left = mat[b], out[b]
        tops, lefts = [], []
        for s in range(tile):
            tops.append(top[s : s + 1, :] * inv[s])
            lefts.append(left[s : s + 1, :] * inv[s])
            if s + 1 < tile:
                low = jnp.where(row > s, col[s][b], 0.0)
                top = top - low * tops[s]
                left = left - low * lefts[s]
        inverse_ref[tile * b : tile * (b + 1), :] = jnp.concatenate(lefts, 0)
        for r in range(b + 1, blocks):
            for s in range(tile):
                mat[r] = mat[r] - col[s][r] * tops[s]
                out[r] = out[r] - col[s][r] * lefts[s]
    turned_ref[...] = inverse_ref[...].T * scale


def factor_inverse(core, mine, other, scale):
    rank = mine.shape[1]
    out = jax.ShapeDtypeStruct((rank, rank), F32)
    return pl.pallas_call(
        functools.partial(factor_body, scale=scale),
        out_shape=(out, out),
        in_specs=[SCALAR, WHOLE, WHOLE],
        out_specs=(WHOLE, WHOLE),
        compiler_params=PARAMS,
        cost_estimate=COST,
        name="factor",
    )(core, mine, other)


def basis_body(own_ref, turned_ref, basis_ref):
    basis_ref[...] = jnp.dot(
        own_ref[...], turned_ref[...], precision=lax.Precision.HIGHEST, preferred_element_type=F32
    )


def basis_of(own, turned):
    rows, rank = own.shape
    block = rows // 4
    return pl.pallas_call(
        basis_body,
        out_shape=jax.ShapeDtypeStruct((rows, rank), F32),
        grid=(rows // block,),
        in_specs=[
            pl.BlockSpec((block, rank), lambda i: (i, 0)),
            pl.BlockSpec((rank, rank), lambda i: (0, 0)),
        ],
        out_specs=pl.BlockSpec((block, rank), lambda i: (i, 0)),
        compiler_params=PARAMS,
        cost_estimate=COST,
        name="basis",
    )(own, turned)


def weigh_body(*refs, plan, block):
    keep_ref, give_ref = refs[-2:]
    rank, cols = keep_ref.shape
    total = None
    for turned, part, chunk, chunk_part in plan:
        size = refs[turned].shape[2]
        for at in range(0, size, block):
            rows = jnp.concatenate(split(refs[turned][part, :, at : at + block]), 0)
            here = slice(chunk_part * size + at, chunk_part * size + at + block)
            high, low = split(jnp.concatenate([refs[chunk][here, :], refs[chunk + 1][here, :]], 1))
            both = mm(rows, low) + mm(rows, high)
            total = both if total is None else total + both
    total = total[rank:] + total[:rank]
    keep, give = total[:, :cols], total[:, cols:]
    if len(refs) > 2 + max(step[2] for step in plan) + 2:
        keep = refs[-4][...] + keep
        give = refs[-3][...] + give
    keep_ref[...] = keep
    give_ref[...] = give


def weigh(turned, chunks, plan, acc=(), block=384):
    rank = turned[0].shape[1]
    cols = chunks[0][0].shape[1]
    args = list(turned) + [array for chunk in chunks for array in chunk] + list(acc)
    plan = [(t, part, len(turned) + 2 * c, chunk_part) for t, part, c, chunk_part in plan]
    return pl.pallas_call(
        functools.partial(weigh_body, plan=plan, block=block),
        out_shape=(pltpu.VMEM((rank, cols), F32),) * 2,
        in_specs=[WHOLE] * len(args),
        out_specs=(WHOLE, WHOLE),
        compiler_params=PARAMS,
        cost_estimate=COST,
        name="weigh",
    )(*args)


def project_body(core_ref, inverse_ref, keep_ref, give_ref, out_ref):
    dot = functools.partial(jnp.dot, precision=lax.Precision.HIGHEST, preferred_element_type=F32)
    rank, cols = keep_ref.shape
    keep = dot(inverse_ref[...], keep_ref[...])
    give = dot(inverse_ref[...], give_ref[...])
    first = core_ref[0] == 0
    both = jnp.concatenate([jnp.where(first, keep, give), jnp.where(first, give, keep)], 1)
    for part in range(16):
        span = slice(part * (rank // 16), (part + 1) * (rank // 16))
        out_ref[part, 0] = both[span, :cols]
        out_ref[part, 1] = both[span, cols:]


def project(core, inverse, keep, give):
    rank, cols = keep.shape
    out = pl.pallas_call(
        project_body,
        out_shape=jax.ShapeDtypeStruct((16, 2, rank // 16, cols), F32),
        in_specs=[SCALAR] + [WHOLE] * 3,
        out_specs=WHOLE,
        compiler_params=PARAMS,
        cost_estimate=COST,
        name="project",
    )(core, inverse, keep, give)
    return out.reshape(2 * rank, cols)


def shards(panel, test_matrix, prior_sketch):
    x = lax.axis_index("x")
    core = lax.axis_index("core")
    core_of = core.reshape(1)
    rows, rank = prior_sketch.shape
    half = rows // 2
    total_rows = panel.shape[0] * lax.axis_size("y") * lax.axis_size("z")

    def places(*steps):
        first = [(x + step) % 4 * 2 for step in steps]
        first = jnp.stack(first)
        return first + core, first + 1 - core

    panel = pltpu.with_memory_space_constraint(panel, pltpu.HBM)
    test_other = swap(test_matrix)
    tests = (test_matrix, test_other)
    keep, give = places(2, 1, 3, 0)
    far_give, = fetch(give[:1], panel, rows)
    panel, far_give = lax.optimization_barrier((panel, far_give))
    far_other = swap(far_give)
    far_keep, *near = fetch(jnp.concatenate([keep[:3], give[1:3]]), panel, rows)
    far = (far_keep, far_other)
    right = (near[0], swap(near[2]))
    left = (near[1], swap(near[3]))

    far_top = term(far, 0, half, tests)
    far_bot = term(far, half, half, tests)
    far_top, far_bot, right, left = lax.optimization_barrier((far_top, far_bot, right, left))
    far_top = shift(far_top, "x", 1)
    far_bot = shift(far_bot, "x", 3)
    near_bot = term(right, half, half, tests)
    near_top = term(left, 0, half, tests)
    panel, near_bot, near_top = lax.optimization_barrier((panel, near_bot, near_top))
    near_bot = shift(near_bot, "x", 1)
    near_top = shift(near_top, "x", 3)
    here_keep, here_give = fetch(jnp.stack([keep[3], give[3]]), panel, rows)
    here = (here_keep, swap(here_give))
    base = term(here, 0, rows, tests, prior_sketch)
    both_top = shift(term(right, 0, half, tests, far_top), "x", 1)
    both_bot = shift(term(left, half, half, tests, far_bot), "x", 3)
    own, turned = finish(base, near_top, near_bot, both_top, both_bot)

    from_left = shift(turned, "x", 1)
    from_right = shift(turned, "x", 3)

    keep, give = gram_of(core_of, own, turned)
    gram = keep + swap(give)
    gram = axis_sum(axis_sum(gram, "y"), "z")
    gram, turned = lax.optimization_barrier((gram, turned))
    acc = weigh([turned], [here], [(0, 0, 0, 0), (0, 1, 0, 1)])
    across = [shift(gram, "x", by) for by in (2, 1, 3)]

    acc, from_left, from_right = lax.optimization_barrier((acc, from_left, from_right))
    far_bot = shift(from_left[1:], "x", 1)
    far_top = shift(from_right[:1], "x", 3)
    acc = weigh(
        [from_left, from_right],
        [left, right],
        [(0, 0, 0, 0), (0, 1, 0, 1), (1, 0, 1, 0), (1, 1, 1, 1)],
        acc,
    )
    gram = gram + across[0] + across[1] + across[2]
    gram, acc = lax.optimization_barrier((gram, acc))
    inverse, scaled = factor_inverse(core_of, gram, swap(gram), float(total_rows) ** 0.5)
    basis = basis_of(own, scaled)

    far_top, far_bot, inverse = lax.optimization_barrier((far_top, far_bot, inverse))
    weights = weigh([far_top, far_bot], [far], [(0, 0, 0, 0), (1, 0, 0, 1)], acc)
    weights = project(core_of, inverse, *weights)
    parts = lax.all_to_all(weights, ("y", "z", "core"), 0, 0, tiled=True)
    return basis, jnp.sum(parts.reshape(-1, rank // 16, rank), 0)


def solution(mesh):
    fine = Mesh(mesh.devices.reshape(4, 4, 4, 2), AXES)
    return jax.shard_map(
        shards,
        mesh=fine,
        in_specs=(P(("y", "z"), ("x", "core")), P(("x", "core"), None), P(AXES, None)),
        out_specs=(P(AXES, None), P(("y", "z"), ("x", "core"))),
        check_vma=False,
    )
```

time: 372 us -> 105 us (0.28)
  waiting for transfers between devices: 301 us -> 42.5 us
  starting transfers between devices: 0.34 us -> 37.8 us
  matrix products: 26.4 us -> 0 us
  other arithmetic: 24.9 us -> 2.1 us
  Pallas kernels: 0 us -> 20.2 us
  between operations: 14.5 us -> 0.91 us
    psum x1 -> x0, waiting for transfers between devices: 140 us -> none  [lower_factor(): total = lax.psum(gram, ('row', 'col'))]
    unnamed x5 -> x0, waiting for transfers between devices: 78.1 us -> none
    reduce_scatter x1 -> x0, waiting for transfers between devices: 45.2 us -> none  [shards(): lax.psum_scatter(term, 'col', scatter_dimension=0, tiled=True)]
    all_gather x1 -> x0, waiting for transfers between devices: 38.1 us -> none  [shards(): lax.all_gather(own_basis, 'col', axis=0, tiled=True)]
    ppermute x0 -> x24, waiting for transfers between devices: none -> 37.1 us  [the longest x20 27.9 us: shift(): return lax.ppermute(block, axis, [(i, (i + by) % n) for i in range(n)])]
    ppermute x0 -> x24, starting transfers between devices: none -> 30.7 us  [the longest x20 24.1 us: shift(): return lax.ppermute(block, axis, [(i, (i + by) % n) for i in range(n)])]
    dot_general x3 -> x0, matrix products: 24.5 us -> none  [the longest x1 13.7 us: shards(): jnp.dot(lax.all_gather(own_basis, 'col', axis=0, tiled=True).T, panel, pr...]
    another operation x5 -> x1, other arithmetic: 22.9 us -> 1.28 us  [shards(): here_keep, here_give = fetch(jnp.stack([keep[3], give[3]]), panel, rows)]
  transfers between devices with their start and end apart: 4 -> 25, of which waited for: 4 -> 15; matrix products, arithmetic and copies ran while one was open for 0% -> 2% of each run, Pallas kernels for 0% -> 13%
where the time goes in v2:
time: 105 us
  waiting for transfers between devices  42.5 us (40%)
  starting transfers between devices  37.8 us (36%)
  Pallas kernels  20.2 us (19%)
  other arithmetic  2.1 us (2%)
  local copies, waits for them, and re-layouts  1.3 us (1%)
    ppermute x20, waiting for transfers between devices, shift(): return lax.ppermute(block, axis, [(i, (i + by) % n) for i in range(n)])  27.9 us
    ppermute x20, starting transfers between devices, shift(): return lax.ppermute(block, axis, [(i, (i + by) % n) for i in range(n)])  24.1 us
    ppermute x4, waiting for transfers between devices, trade(): return lax.ppermute(block, axis, [(i, partner[i]) for i in range(4)])  9.28 us
    all_to_all x1, starting transfers between devices, shards(): parts = lax.all_to_all(weights, ('y', 'z', 'core'), 0, 0, tiled=True)  7.12 us
    ppermute x4, starting transfers between devices, trade(): return lax.ppermute(block, axis, [(i, partner[i]) for i in range(4)])  6.6 us
    pallas_call x3, Pallas kernels, fetch(): pl.pallas_call(functools.partial(fetch_body, count=count), out_shape=[plt...  6.42 us
    all_to_all x1, waiting for transfers between devices, shards(): parts = lax.all_to_all(weights, ('y', 'z', 'core'), 0, 0, tiled=True)  5.38 us
    pallas_call x1, Pallas kernels, factor_inverse(): pl.pallas_call(functools.partial(factor_body, scale=scale), out_shape=(ou...  3.87 us
  transfers between devices with their start and end apart: 25, of which 15 were waited for; matrix products, arithmetic and copies ran while one was open for 2% of the time, Pallas kernels for 13%

profile of v2, /device:TPU:1, one launch (start us, length us, event | category | flops | bytes accessed | tf_op | source)
XLA Modules:
  0.0 104.8 jit_solution(14625113753063379777)
XLA Ops:
  1.3 1.8 %fetch.3 = f32[1536,128]{1,0:T(8,128)S(1)} custom-call(s32[1]{0:T(128)} %get-tuple-element.88.place_ref, f32[12288,128]{1,0:T(8,128)} %panel_ref.3), custom_call_target="tpu_custom_call" | custom-call | tf_op jit(solution)/shard_map/fetch/pallas_call | solution.py:77
  3.2 1.5 %collective-permute-start = (f32[1536,128]{1,0:T(8,128)S(1)}, f32[1536,128]{1,0:T(8,128)S(1)}, u32[]{:S(2)}, u32[]{:S(2)}) collective-permute-start(f32[1536,128]{1,0:T(8,128)S(1)} %fetch.3), channel_id=1, source_target_pairs={{0,1},{1,0},{2,3},{3,2},{4,5},{5,4},{6,7},{7,6},{8,9},{9,8},{10,11... | collective-permute-start | bytes 2359304 | tf_op jit(solution)/shard_map/ppermute | solution.py:22
  4.8 2.7 %fetch.4 = (f32[1536,128]{1,0:T(8,128)S(1)}, f32[1536,128]{1,0:T(8,128)S(1)}, f32[1536,128]{1,0:T(8,128)S(1)}, f32[1536,128]{1,0:T(8,128)S(1)}, f32[1536,128]{1,0:T(8,128)S(1)}) custom-call(s32[5]{0:T(128)S(1)} %pad_add_fusion.2.place_ref, f32[12288,128]{1,0:T(8,128)} %panel_ref.3), custom_call_target="tpu_custom_call" | custom-call | tf_op jit(solution)/shard_map/fetch/pallas_call | solution.py:77
  12.7 1.9 %fetch.5 = (f32[1536,128]{1,0:T(8,128)S(1)}, f32[1536,128]{1,0:T(8,128)S(1)}) custom-call(s32[2]{0:T(128)S(1)} %pad_add_fusion.1.place_ref, f32[12288,128]{1,0:T(8,128)} %panel_ref.3), custom_call_target="tpu_custom_call" | custom-call | tf_op jit(solution)/shard_map/fetch/pallas_call | solution.py:77
  18.9 7.4 %collective-permute-done.7.rest_0_ = f32[768,128]{1,0:T(8,128)S(1)} collective-permute-done((f32[768,128]{1,0:T(8,128)S(1)}, f32[768,128]{1,0:T(8,128)S(1)}, u32[]{:S(2)}, u32[]{:S(2)}) %collective-permute-start.7) | collective-permute-done | bytes 393248 | tf_op jit(solution)/shard_map/ppermute | solution.py:22
  27.3 2.6 %collective-permute-start.10 = (f32[768,128]{1,0:T(8,128)S(1)}, f32[768,128]{1,0:T(8,128)S(1)}, u32[]{:S(2)}, u32[]{:S(2)}) collective-permute-start(f32[768,128]{1,0:T(8,128)S(1)} %term.13), channel_id=1, source_target_pairs={{0,6},{2,0},{4,2},{6,4},{1,7},{3,1},{5,3},{7,5},{8,14},{10,8},{12,... | collective-permute-start | bytes 1179656 | tf_op jit(solution)/shard_map/ppermute | solution.py:22
  30.5 4.0 %collective-permute-done.5.near_top_ref = f32[768,128]{1,0:T(8,128)S(1)} collective-permute-done((f32[768,128]{1,0:T(8,128)S(1)}, f32[768,128]{1,0:T(8,128)S(1)}, u32[]{:S(2)}, u32[]{:S(2)}) %collective-permute-start.5) | collective-permute-done | bytes 393248 | tf_op jit(solution)/shard_map/ppermute | solution.py:22
  34.8 8.4 %collective-permute-done.8.both_top_ref = f32[768,128]{1,0:T(8,128)S(1)} collective-permute-done((f32[768,128]{1,0:T(8,128)S(1)}, f32[768,128]{1,0:T(8,128)S(1)}, u32[]{:S(2)}, u32[]{:S(2)}) %collective-permute-start.8) | collective-permute-done | bytes 393248 | tf_op jit(solution)/shard_map/ppermute | solution.py:22
  43.5 2.4 %collective-permute-start.20 = (f32[2,128,768]{2,1,0:T(8,128)S(1)}, f32[2,128,768]{2,1,0:T(8,128)S(1)}, u32[]{:S(2)}, u32[]{:S(2)}) collective-permute-start(f32[2,128,768]{2,1,0:T(8,128)S(1)} %get-tuple-element.67.turned_ref.refs_0_), channel_id=1, source_target_pairs={{0,6},{2,0},{4,2},{6,4},{1,7},{3,1},{5,3},{7,5},{8,14},{10,8},{12,... | collective-permute-start | bytes 2359304 | tf_op jit(solution)/shard_map/ppermute | solution.py:22
  46.7 1.9 %collective-permute-start.11 = (f32[64,128]{1,0:T(8,128)S(1)}, f32[64,128]{1,0:T(8,128)S(1)}, u32[]{:S(2)}, u32[]{:S(2)}) collective-permute-start(f32[64,128]{1,0:T(8,128)S(1)} %get-tuple-element.65), channel_id=1, source_target_pairs={{0,1},{1,0},{2,3},{3,2},{4,5},{5,4},{6,7},{7,6},{8,9},{9,8},{10,11... | collective-permute-start | bytes 98312 | tf_op jit(solution)/shard_map/ppermute | solution.py:22
  49.5 2.8 %collective-permute-start.12 = (f32[64,128]{1,0:T(8,128)S(1)}, f32[64,128]{1,0:T(8,128)S(1)}, u32[]{:S(2)}, u32[]{:S(2)}) collective-permute-start(f32[64,128]{1,0:T(8,128)S(1)} %add.65), channel_id=1, source_target_pairs={{0,96},{32,64},{64,32},{96,0},{1,97},{33,65},{65,33},{97,1},{2,98}... | collective-permute-start | bytes 98312 | tf_op jit(solution)/shard_map/ppermute | solution.py:31
  52.3 1.6 %collective-permute-done.12 = f32[64,128]{1,0:T(8,128)S(1)} collective-permute-done((f32[64,128]{1,0:T(8,128)S(1)}, f32[64,128]{1,0:T(8,128)S(1)}, u32[]{:S(2)}, u32[]{:S(2)}) %collective-permute-start.12) | collective-permute-done | bytes 32800 | tf_op jit(solution)/shard_map/ppermute | solution.py:31
  53.9 3.0 %collective-permute-done.13 = f32[64,128]{1,0:T(8,128)S(1)} collective-permute-done((f32[64,128]{1,0:T(8,128)S(1)}, f32[64,128]{1,0:T(8,128)S(1)}, u32[]{:S(2)}, u32[]{:S(2)}) %collective-permute-start.13) | collective-permute-done | bytes 32800 | tf_op jit(solution)/shard_map/ppermute | solution.py:31
  57.0 3.8 %collective-permute-start.14 = (f32[64,128]{1,0:T(8,128)S(1)}, f32[64,128]{1,0:T(8,128)S(1)}, u32[]{:S(2)}, u32[]{:S(2)}) collective-permute-start(f32[64,128]{1,0:T(8,128)S(1)} %add.67), channel_id=1, source_target_pairs={{0,24},{8,16},{16,8},{24,0},{1,25},{9,17},{17,9},{25,1},{2,26},{10... | collective-permute-start | bytes 98312 | tf_op jit(solution)/shard_map/ppermute | solution.py:31
  60.7 1.6 %collective-permute-done.14 = f32[64,128]{1,0:T(8,128)S(1)} collective-permute-done((f32[64,128]{1,0:T(8,128)S(1)}, f32[64,128]{1,0:T(8,128)S(1)}, u32[]{:S(2)}, u32[]{:S(2)}) %collective-permute-start.14) | collective-permute-done | bytes 32800 | tf_op jit(solution)/shard_map/ppermute | solution.py:31
  62.3 3.1 %collective-permute-done.15 = f32[64,128]{1,0:T(8,128)S(1)} collective-permute-done((f32[64,128]{1,0:T(8,128)S(1)}, f32[64,128]{1,0:T(8,128)S(1)}, u32[]{:S(2)}, u32[]{:S(2)}) %collective-permute-start.15) | collective-permute-done | bytes 32800 | tf_op jit(solution)/shard_map/ppermute | solution.py:31
  66.3 2.7 %collective-permute-start.22 = (f32[1,128,768]{2,1,0:T(8,128)S(1)}, f32[1,128,768]{2,1,0:T(8,128)S(1)}, u32[]{:S(2)}, u32[]{:S(2)}) collective-permute-start(f32[1,128,768]{2,1,0:T(8,128)S(1)} %slice.26), channel_id=1, source_target_pairs={{0,6},{2,0},{4,2},{6,4},{1,7},{3,1},{5,3},{7,5},{8,14},{10,8},{12,... | collective-permute-start | bytes 1179656 | tf_op jit(solution)/shard_map/ppermute | solution.py:22
  69.0 1.4 %collective-permute-start.18 = (f32[64,128]{1,0:T(8,128)S(1)}, f32[64,128]{1,0:T(8,128)S(1)}, u32[]{:S(2)}, u32[]{:S(2)}) collective-permute-start(f32[64,128]{1,0:T(8,128)S(1)} %add.69), channel_id=1, source_target_pairs={{0,6},{2,0},{4,2},{6,4},{1,7},{3,1},{5,3},{7,5},{8,14},{10,8},{12,... | collective-permute-start | bytes 98312 | tf_op jit(solution)/shard_map/ppermute | solution.py:22
  71.6 2.8 %collective-permute-done.18 = f32[64,128]{1,0:T(8,128)S(1)} collective-permute-done((f32[64,128]{1,0:T(8,128)S(1)}, f32[64,128]{1,0:T(8,128)S(1)}, u32[]{:S(2)}, u32[]{:S(2)}) %collective-permute-start.18) | collective-permute-done | bytes 32800 | tf_op jit(solution)/shard_map/ppermute | solution.py:22
  77.9 5.0 %collective-permute-start.21 = (f32[64,128]{1,0:T(8,128)S(1)}, f32[64,128]{1,0:T(8,128)S(1)}, u32[]{:S(2)}, u32[]{:S(2)}) collective-permute-start(f32[64,128]{1,0:T(8,128)S(1)} %add_add_fusion.mine_ref), channel_id=1, source_target_pairs={{0,1},{1,0},{2,3},{3,2},{4,5},{5,4},{6,7},{7,6},{8,9},{9,8},{10,11... | collective-permute-start | bytes 98312 | tf_op jit(solution)/shard_map/ppermute | solution.py:22
  83.8 3.9 %factor.1 = (f32[128,128]{1,0:T(8,128)S(1)}, f32[128,128]{1,0:T(8,128)S(1)}) custom-call(s32[1]{0:T(128)} %bitcast.4.core_ref, f32[64,128]{1,0:T(8,128)S(1)} %add_add_fusion.mine_ref, f32[64,128]{1,0:T(8,128)S(1)} %collective-permute-done.21.other_ref), custom_call_target="tpu_custom_call" | custom-call | tf_op jit(solution)/shard_map/factor/pallas_call | solution.py:215
  89.3 7.1 %all-to-all-start = ((f32[32,8,128]{2,1,0:T(8,128)}), f32[32,8,128]{2,1,0:T(8,128)S(1)}, u32[]{:S(2)}, u32[]{:S(2)}) async-start(f32[32,8,128]{2,1,0:T(8,128)} %bitcast.5), calls=%async_computation | async-start | bytes 262144 | tf_op jit(solution)/shard_map/all_to_all | solution.py:383
  96.5 2.3 %basis.1 = f32[1536,128]{1,0:T(8,128)} custom-call(f32[1536,128]{1,0:T(8,128)S(1)} %get-tuple-element.62.own_ref, f32[128,128]{1,0:T(8,128)S(1)} %get-tuple-element.77.turned_ref), custom_call_target="tpu_custom_call" | custom-call | tf_op jit(solution)/shard_map/basis/pallas_call | solution.py:235
  98.8 5.4 %all-to-all-done = f32[32,8,128]{2,1,0:T(8,128)S(1)} async-done(((f32[32,8,128]{2,1,0:T(8,128)}), f32[32,8,128]{2,1,0:T(8,128)S(1)}, u32[]{:S(2)}, u32[]{:S(2)}) %all-to-all-start) | async-done | bytes 131104 | tf_op jit(solution)/shard_map/all_to_all | solution.py:383
  (64 shorter events, 22.8 us)
Async XLA Ops:
  3.2 7.9 %collective-permute-start = (f32[1536,128]{1,0:T(8,128)S(1)}, f32[1536,128]{1,0:T(8,128)S(1)}, u32[]{:S(2)}, u32[]{:S(2)}) collective-permute-start(f32[1536,128]{1,0:T(8,128)S(1)} %fetch.3), channel_id=1, source_target_pairs={{0,1},{1,0},{2,3},{3,2},{4,5},{5,4},{6,7},{7,6},{8,9},{9,8},{10,11... | collective-permute-start | bytes 2359304 | tf_op jit(solution)/shard_map/ppermute | solution.py:22
  7.5 4.4 %collective-permute-start.2 = (f32[1536,128]{1,0:T(8,128)S(1)}, f32[1536,128]{1,0:T(8,128)S(1)}, u32[]{:S(2)}, u32[]{:S(2)}) collective-permute-start(f32[1536,128]{1,0:T(8,128)S(1)} %get-tuple-element.48), channel_id=1, source_target_pairs={{0,1},{1,0},{2,3},{3,2},{4,5},{5,4},{6,7},{7,6},{8,9},{9,8},{10,11... | collective-permute-start | bytes 2359304 | tf_op jit(solution)/shard_map/ppermute | solution.py:22
  7.6 4.3 %collective-permute-start.3 = (f32[1536,128]{1,0:T(8,128)S(1)}, f32[1536,128]{1,0:T(8,128)S(1)}, u32[]{:S(2)}, u32[]{:S(2)}) collective-permute-start(f32[1536,128]{1,0:T(8,128)S(1)} %get-tuple-element.50), channel_id=1, source_target_pairs={{0,1},{1,0},{2,3},{3,2},{4,5},{5,4},{6,7},{7,6},{8,9},{9,8},{10,11... | collective-permute-start | bytes 2359304 | tf_op jit(solution)/shard_map/ppermute | solution.py:22
  8.1 3.0 %collective-permute-start.1 = (f32[128,128]{1,0:T(8,128)S(1)}, f32[128,128]{1,0:T(8,128)S(1)}, u32[]{:S(2)}, u32[]{:S(2)}) collective-permute-start(f32[128,128]{1,0:T(8,128)S(1)} %copy-done), channel_id=1, source_target_pairs={{0,1},{1,0},{2,3},{3,2},{4,5},{5,4},{6,7},{7,6},{8,9},{9,8},{10,11... | collective-permute-start | bytes 196616 | tf_op jit(solution)/shard_map/ppermute | solution.py:22
  14.6 15.3 %collective-permute-start.4 = (f32[1536,128]{1,0:T(8,128)S(1)}, f32[1536,128]{1,0:T(8,128)S(1)}, u32[]{:S(2)}, u32[]{:S(2)}) collective-permute-start(f32[1536,128]{1,0:T(8,128)S(1)} %get-tuple-element.57), channel_id=1, source_target_pairs={{0,1},{1,0},{2,3},{3,2},{4,5},{5,4},{6,7},{7,6},{8,9},{9,8},{10,11... | collective-permute-start | bytes 2359304 | tf_op jit(solution)/shard_map/ppermute | solution.py:22
  14.8 11.5 %collective-permute-start.7 = (f32[768,128]{1,0:T(8,128)S(1)}, f32[768,128]{1,0:T(8,128)S(1)}, u32[]{:S(2)}, u32[]{:S(2)}) collective-permute-start(f32[768,128]{1,0:T(8,128)S(1)} %term.7), channel_id=1, source_target_pairs={{0,2},{2,4},{4,6},{6,0},{1,3},{3,5},{5,7},{7,1},{8,10},{10,12},{12... | collective-permute-start | bytes 1179656 | tf_op jit(solution)/shard_map/ppermute | solution.py:22
  16.1 10.8 %collective-permute-start.9 = (f32[768,128]{1,0:T(8,128)S(1)}, f32[768,128]{1,0:T(8,128)S(1)}, u32[]{:S(2)}, u32[]{:S(2)}) collective-permute-start(f32[768,128]{1,0:T(8,128)S(1)} %term.8), channel_id=1, source_target_pairs={{0,6},{2,0},{4,2},{6,4},{1,7},{3,1},{5,3},{7,5},{8,14},{10,8},{12,... | collective-permute-start | bytes 1179656 | tf_op jit(solution)/shard_map/ppermute | solution.py:22
  17.5 17.1 %collective-permute-start.5 = (f32[768,128]{1,0:T(8,128)S(1)}, f32[768,128]{1,0:T(8,128)S(1)}, u32[]{:S(2)}, u32[]{:S(2)}) collective-permute-start(f32[768,128]{1,0:T(8,128)S(1)} %term.10), channel_id=1, source_target_pairs={{0,6},{2,0},{4,2},{6,4},{1,7},{3,1},{5,3},{7,5},{8,14},{10,8},{12,... | collective-permute-start | bytes 1179656 | tf_op jit(solution)/shard_map/ppermute | solution.py:22
  18.8 15.9 %collective-permute-start.6 = (f32[768,128]{1,0:T(8,128)S(1)}, f32[768,128]{1,0:T(8,128)S(1)}, u32[]{:S(2)}, u32[]{:S(2)}) collective-permute-start(f32[768,128]{1,0:T(8,128)S(1)} %term.9), channel_id=1, source_target_pairs={{0,2},{2,4},{4,6},{6,0},{1,3},{3,5},{5,7},{7,1},{8,10},{10,12},{12... | collective-permute-start | bytes 1179656 | tf_op jit(solution)/shard_map/ppermute | solution.py:22
  26.7 16.5 %collective-permute-start.8 = (f32[768,128]{1,0:T(8,128)S(1)}, f32[768,128]{1,0:T(8,128)S(1)}, u32[]{:S(2)}, u32[]{:S(2)}) collective-permute-start(f32[768,128]{1,0:T(8,128)S(1)} %term.12), channel_id=1, source_target_pairs={{0,2},{2,4},{4,6},{6,0},{1,3},{3,5},{5,7},{7,1},{8,10},{10,12},{12... | collective-permute-start | bytes 1179656 | tf_op jit(solution)/shard_map/ppermute | solution.py:22
  27.3 15.9 %collective-permute-start.10 = (f32[768,128]{1,0:T(8,128)S(1)}, f32[768,128]{1,0:T(8,128)S(1)}, u32[]{:S(2)}, u32[]{:S(2)}) collective-permute-start(f32[768,128]{1,0:T(8,128)S(1)} %term.13), channel_id=1, source_target_pairs={{0,6},{2,0},{4,2},{6,4},{1,7},{3,1},{5,3},{7,5},{8,14},{10,8},{12,... | collective-permute-start | bytes 1179656 | tf_op jit(solution)/shard_map/ppermute | solution.py:22
  43.5 22.7 %collective-permute-start.20 = (f32[2,128,768]{2,1,0:T(8,128)S(1)}, f32[2,128,768]{2,1,0:T(8,128)S(1)}, u32[]{:S(2)}, u32[]{:S(2)}) collective-permute-start(f32[2,128,768]{2,1,0:T(8,128)S(1)} %get-tuple-element.67.turned_ref.refs_0_), channel_id=1, source_target_pairs={{0,6},{2,0},{4,2},{6,4},{1,7},{3,1},{5,3},{7,5},{8,14},{10,8},{12,... | collective-permute-start | bytes 2359304 | tf_op jit(solution)/shard_map/ppermute | solution.py:22
  45.9 20.3 %collective-permute-start.19 = (f32[2,128,768]{2,1,0:T(8,128)S(1)}, f32[2,128,768]{2,1,0:T(8,128)S(1)}, u32[]{:S(2)}, u32[]{:S(2)}) collective-permute-start(f32[2,128,768]{2,1,0:T(8,128)S(1)} %get-tuple-element.67.turned_ref.refs_0_), channel_id=1, source_target_pairs={{0,2},{2,4},{4,6},{6,0},{1,3},{3,5},{5,7},{7,1},{8,10},{10,12},{12... | collective-permute-start | bytes 2359304 | tf_op jit(solution)/shard_map/ppermute | solution.py:22
  49.5 4.4 %collective-permute-start.12 = (f32[64,128]{1,0:T(8,128)S(1)}, f32[64,128]{1,0:T(8,128)S(1)}, u32[]{:S(2)}, u32[]{:S(2)}) collective-permute-start(f32[64,128]{1,0:T(8,128)S(1)} %add.65), channel_id=1, source_target_pairs={{0,96},{32,64},{64,32},{96,0},{1,97},{33,65},{65,33},{97,1},{2,98}... | collective-permute-start | bytes 98312 | tf_op jit(solution)/shard_map/ppermute | solution.py:31
  53.9 3.1 %collective-permute-start.13 = (f32[64,128]{1,0:T(8,128)S(1)}, f32[64,128]{1,0:T(8,128)S(1)}, u32[]{:S(2)}, u32[]{:S(2)}) collective-permute-start(f32[64,128]{1,0:T(8,128)S(1)} %add.66), channel_id=1, source_target_pairs={{0,32},{32,0},{64,96},{96,64},{1,33},{33,1},{65,97},{97,65},{2,34}... | collective-permute-start | bytes 98312 | tf_op jit(solution)/shard_map/ppermute | solution.py:31
  57.0 5.4 %collective-permute-start.14 = (f32[64,128]{1,0:T(8,128)S(1)}, f32[64,128]{1,0:T(8,128)S(1)}, u32[]{:S(2)}, u32[]{:S(2)}) collective-permute-start(f32[64,128]{1,0:T(8,128)S(1)} %add.67), channel_id=1, source_target_pairs={{0,24},{8,16},{16,8},{24,0},{1,25},{9,17},{17,9},{25,1},{2,26},{10... | collective-permute-start | bytes 98312 | tf_op jit(solution)/shard_map/ppermute | solution.py:31
  62.3 3.1 %collective-permute-start.15 = (f32[64,128]{1,0:T(8,128)S(1)}, f32[64,128]{1,0:T(8,128)S(1)}, u32[]{:S(2)}, u32[]{:S(2)}) collective-permute-start(f32[64,128]{1,0:T(8,128)S(1)} %add.68), channel_id=1, source_target_pairs={{0,8},{8,0},{16,24},{24,16},{1,9},{9,1},{17,25},{25,17},{2,10},{10... | collective-permute-start | bytes 98312 | tf_op jit(solution)/shard_map/ppermute | solution.py:31
  66.2 21.5 %collective-permute-start.23 = (f32[1,128,768]{2,1,0:T(8,128)S(1)}, f32[1,128,768]{2,1,0:T(8,128)S(1)}, u32[]{:S(2)}, u32[]{:S(2)}) collective-permute-start(f32[1,128,768]{2,1,0:T(8,128)S(1)} %slice.27), channel_id=1, source_target_pairs={{0,2},{2,4},{4,6},{6,0},{1,3},{3,5},{5,7},{7,1},{8,10},{10,12},{12... | collective-permute-start | bytes 1179656 | tf_op jit(solution)/shard_map/ppermute | solution.py:22
  66.3 21.4 %collective-permute-start.22 = (f32[1,128,768]{2,1,0:T(8,128)S(1)}, f32[1,128,768]{2,1,0:T(8,128)S(1)}, u32[]{:S(2)}, u32[]{:S(2)}) collective-permute-start(f32[1,128,768]{2,1,0:T(8,128)S(1)} %slice.26), channel_id=1, source_target_pairs={{0,6},{2,0},{4,2},{6,4},{1,7},{3,1},{5,3},{7,5},{8,14},{10,8},{12,... | collective-permute-start | bytes 1179656 | tf_op jit(solution)/shard_map/ppermute | solution.py:22
  69.0 5.4 %collective-permute-start.18 = (f32[64,128]{1,0:T(8,128)S(1)}, f32[64,128]{1,0:T(8,128)S(1)}, u32[]{:S(2)}, u32[]{:S(2)}) collective-permute-start(f32[64,128]{1,0:T(8,128)S(1)} %add.69), channel_id=1, source_target_pairs={{0,6},{2,0},{4,2},{6,4},{1,7},{3,1},{5,3},{7,5},{8,14},{10,8},{12,... | collective-permute-start | bytes 98312 | tf_op jit(solution)/shard_map/ppermute | solution.py:22
  70.4 5.0 %collective-permute-start.17 = (f32[64,128]{1,0:T(8,128)S(1)}, f32[64,128]{1,0:T(8,128)S(1)}, u32[]{:S(2)}, u32[]{:S(2)}) collective-permute-start(f32[64,128]{1,0:T(8,128)S(1)} %add.69), channel_id=1, source_target_pairs={{0,2},{2,4},{4,6},{6,0},{1,3},{3,5},{5,7},{7,1},{8,10},{10,12},{12... | collective-permute-start | bytes 98312 | tf_op jit(solution)/shard_map/ppermute | solution.py:22
  70.5 6.2 %collective-permute-start.16 = (f32[64,128]{1,0:T(8,128)S(1)}, f32[64,128]{1,0:T(8,128)S(1)}, u32[]{:S(2)}, u32[]{:S(2)}) collective-permute-start(f32[64,128]{1,0:T(8,128)S(1)} %add.69), channel_id=1, source_target_pairs={{0,4},{2,6},{4,0},{6,2},{1,5},{3,7},{5,1},{7,3},{8,12},{10,14},{12... | collective-permute-start | bytes 98312 | tf_op jit(solution)/shard_map/ppermute | solution.py:22
  77.9 5.9 %collective-permute-start.21 = (f32[64,128]{1,0:T(8,128)S(1)}, f32[64,128]{1,0:T(8,128)S(1)}, u32[]{:S(2)}, u32[]{:S(2)}) collective-permute-start(f32[64,128]{1,0:T(8,128)S(1)} %add_add_fusion.mine_ref), channel_id=1, source_target_pairs={{0,1},{1,0},{2,3},{3,2},{4,5},{5,4},{6,7},{7,6},{8,9},{9,8},{10,11... | collective-permute-start | bytes 98312 | tf_op jit(solution)/shard_map/ppermute | solution.py:22
  89.3 14.8 %all-to-all-start = ((f32[32,8,128]{2,1,0:T(8,128)}), f32[32,8,128]{2,1,0:T(8,128)S(1)}, u32[]{:S(2)}, u32[]{:S(2)}) async-start(f32[32,8,128]{2,1,0:T(8,128)} %bitcast.5), calls=%async_computation | async-start | bytes 262144 | tf_op jit(solution)/shard_map/all_to_all | solution.py:383
  (3 other events, 27.2 us)

commit v3 on v2

v3 whole, which is shorter than its diff:
```python
import functools

import jax
import jax.numpy as jnp
from jax import lax
from jax.experimental import pallas as pl
from jax.experimental.pallas import tpu as pltpu
from jax.sharding import Mesh, PartitionSpec as P

AXES = ("y", "z", "x", "core")
F32 = jnp.float32
BF16 = jnp.bfloat16
LIMIT = 16 * 1024 * 1024
COST = pl.CostEstimate(flops=0, bytes_accessed=0, transcendentals=0)
FIRST = pl.CostEstimate(flops=0, bytes_accessed=0, transcendentals=0)
SLOW = pl.CostEstimate(flops=2 * 10**9, bytes_accessed=0, transcendentals=0)
PARAMS = pltpu.CompilerParams(vmem_limit_bytes=LIMIT)
WHOLE = pl.BlockSpec(memory_space=pltpu.VMEM)


def shift(block, axis, by):
    n = lax.axis_size(axis)
    return lax.ppermute(block, axis, [(i, (i + by) % n) for i in range(n)])


def swap(block):
    return shift(block, "core", 1)


def axis_sum(block, axis):
    far, right, left = (shift(block, axis, by) for by in (2, 1, 3))
    return block + right + left + far


def split(block):
    high = block.astype(BF16)
    return high, (block - high.astype(F32)).astype(BF16)


def mm(a, b):
    return jnp.dot(a, b, preferred_element_type=F32)


def fetch_body(panel_ref, *rest, plan):
    outs, sems = rest[: len(plan)], rest[len(plan)]
    rows = outs[0].shape[0]
    x = lax.axis_index("x")
    core = lax.axis_index("core")
    copies = []
    for slot, (step, other) in enumerate(plan):
        chunk = lax.rem(x + step, 4) * 2 + (1 - core if other else core)
        start = pl.multiple_of(chunk * rows, rows)
        copies.append(
            pltpu.make_async_copy(panel_ref.at[pl.ds(start, rows), :], outs[slot], sems.at[slot])
        )
    for copy in copies:
        copy.start()
    for copy in copies:
        copy.wait()


def fetch(panel, rows, *plan):
    count = len(plan)
    cols = panel.shape[1]
    return pl.pallas_call(
        functools.partial(fetch_body, plan=plan),
        out_shape=[pltpu.VMEM((rows, cols), F32)] * count,
        in_specs=[pl.BlockSpec(memory_space=pl.ANY)],
        out_specs=[WHOLE] * count,
        scratch_shapes=[pltpu.SemaphoreType.DMA((count,))],
        compiler_params=PARAMS,
        cost_estimate=COST,
        name="fetch",
    )(panel)


def term_body(mine_ref, other_ref, test_ref, test_other_ref, *rest, first, sizes, block):
    rank = test_ref.shape[1]
    tests = jnp.concatenate([test_ref[...], test_other_ref[...]], 0)
    tests = jnp.concatenate(split(tests), 1)
    out_ref = rest[-1]
    for at in range(0, out_ref.shape[0], block):
        here = slice(first + at, first + at + block)
        high, low = split(jnp.concatenate([mine_ref[here, :], other_ref[here, :]], 1))
        both = mm(low, tests) + mm(high, tests)
        total = both[:, rank:] + both[:, :rank]
        slot = 0
        for size in sizes:
            addend_ref = rest[slot + at // (out_ref.shape[0] // size)]
            begin = at % (out_ref.shape[0] // size)
            total = total + addend_ref[begin : begin + block, :]
            slot += size
        out_ref[at : at + block, :] = total


def term(chunk, first, count, tests, *addends, block=384, cost=COST):
    rank = tests[0].shape[1]
    sizes = tuple(len(parts) for parts in addends)
    return pl.pallas_call(
        functools.partial(term_body, first=first, sizes=sizes, block=block),
        out_shape=pltpu.VMEM((count, rank), F32),
        in_specs=[WHOLE] * (4 + sum(sizes)),
        out_specs=WHOLE,
        compiler_params=PARAMS,
        cost_estimate=cost,
        name="term",
    )(*chunk, *tests, *(array for parts in addends for array in parts))


def finish_body(base_ref, top_ref, bot_ref, own_ref, turned_ref):
    parts, _, size = turned_ref.shape
    for part in range(parts):
        span = slice(part * size, (part + 1) * size)
        both_ref = top_ref if part < parts // 2 else bot_ref
        begin = part % (parts // 2) * size
        own = base_ref[span, :] + both_ref[begin : begin + size, :]
        own_ref[span, :] = own
        turned_ref[part] = own.T


def finish(base, top, bot, parts=2):
    rows, rank = base.shape
    return pl.pallas_call(
        finish_body,
        out_shape=(
            pltpu.VMEM((rows, rank), F32),
            pltpu.VMEM((parts, rank, rows // parts), F32),
        ),
        in_specs=[WHOLE] * 3,
        out_specs=(WHOLE, WHOLE),
        compiler_params=PARAMS,
        cost_estimate=COST,
        name="finish",
    )(base, top, bot)


def gram_body(own_ref, turned_ref, gram_ref):
    parts, _, size = turned_ref.shape
    dot = functools.partial(jnp.dot, precision=lax.Precision.HIGHEST, preferred_element_type=F32)
    total = None
    for part in range(parts):
        piece = dot(turned_ref[part], own_ref[part * size : (part + 1) * size, :])
        total = piece if total is None else total + piece
    gram_ref[...] = total


def gram_of(own, turned):
    rank = own.shape[1]
    return pl.pallas_call(
        gram_body,
        out_shape=pltpu.VMEM((rank, rank), F32),
        in_specs=[WHOLE] * 2,
        out_specs=WHOLE,
        compiler_params=PARAMS,
        cost_estimate=COST,
        name="gram",
    )(own, turned)


def gather_body(*refs):
    keep_ref, give_ref = refs[-2:]
    half = keep_ref.shape[0]
    core = lax.axis_index("core")
    for out_ref, part in ((keep_ref, core), (give_ref, 1 - core)):
        here = pl.ds(pl.multiple_of(part * half, half), half)
        total = refs[0][here, :]
        for ref in refs[1:-2]:
            total = total + ref[here, :]
        out_ref[...] = total


def gather(*parts):
    rank = parts[0].shape[1]
    return pl.pallas_call(
        gather_body,
        out_shape=(pltpu.VMEM((rank // 2, rank), F32),) * 2,
        in_specs=[WHOLE] * len(parts),
        out_specs=(WHOLE, WHOLE),
        compiler_params=PARAMS,
        cost_estimate=COST,
        name="gather",
    )(*parts)


def factor_body(mine_ref, other_ref, inverse_ref, turned_ref, *, scale, tile=8):
    half, n = mine_ref.shape
    blocks = n // tile
    first = lax.axis_index("core") == 0
    upper = jnp.where(first, mine_ref[...], other_ref[...])
    lower = jnp.where(first, other_ref[...], mine_ref[...])
    gram = jnp.concatenate([upper, lower], 0)
    row = lax.broadcasted_iota(jnp.int32, (tile, n), 0)
    lane = lax.broadcasted_iota(jnp.int32, (tile, n), 1)
    mat = [gram[tile * r : tile * (r + 1), :] for r in range(blocks)]
    out = [jnp.where(lane == row + tile * r, 1.0, 0.0).astype(F32) for r in range(blocks)]
    for b in range(blocks):
        live = range(b, blocks)
        col = [
            {r: jnp.broadcast_to(mat[r][:, tile * b + s : tile * b + s + 1], (tile, n)) for r in live}
            for s in range(tile)
        ]
        inv = []
        for s in range(tile):
            inv.append(lax.rsqrt(col[s][b][s : s + 1, :]))
            for r in live:
                col[s][r] = col[s][r] * inv[s]
            for t in range(s + 1, tile):
                factor = col[s][b][t : t + 1, :]
                for r in live:
                    col[t][r] = col[t][r] - col[s][r] * factor
        top, left = mat[b], out[b]
        tops, lefts = [], []
        for s in range(tile):
            tops.append(top[s : s + 1, :] * inv[s])
            lefts.append(left[s : s + 1, :] * inv[s])
            if s + 1 < tile:
                low = jnp.where(row > s, col[s][b], 0.0)
                top = top - low * tops[s]
                left = left - low * lefts[s]
        inverse_ref[tile * b : tile * (b + 1), :] = jnp.concatenate(lefts, 0)
        for r in range(b + 1, blocks):
            for s in range(tile):
                mat[r] = mat[r] - col[s][r] * tops[s]
                out[r] = out[r] - col[s][r] * lefts[s]
    turned_ref[...] = inverse_ref[...].T * scale


def factor_inverse(mine, other, scale):
    rank = mine.shape[1]
    out = jax.ShapeDtypeStruct((rank, rank), F32)
    return pl.pallas_call(
        functools.partial(factor_body, scale=scale),
        out_shape=(out, out),
        in_specs=[WHOLE, WHOLE],
        out_specs=(WHOLE, WHOLE),
        compiler_params=PARAMS,
        cost_estimate=SLOW,
        name="factor",
    )(mine, other)


def basis_body(own_ref, turned_ref, basis_ref):
    basis_ref[...] = jnp.dot(
        own_ref[...], turned_ref[...], precision=lax.Precision.HIGHEST, preferred_element_type=F32
    )


def basis_of(own, turned):
    rows, rank = own.shape
    block = rows // 4
    return pl.pallas_call(
        basis_body,
        out_shape=jax.ShapeDtypeStruct((rows, rank), F32),
        grid=(rows // block,),
        in_specs=[
            pl.BlockSpec((block, rank), lambda i: (i, 0)),
            pl.BlockSpec((rank, rank), lambda i: (0, 0)),
        ],
        out_specs=pl.BlockSpec((block, rank), lambda i: (i, 0)),
        compiler_params=PARAMS,
        cost_estimate=COST,
        name="basis",
    )(own, turned)


def weigh_body(*refs, plan, block):
    keep_ref, give_ref = refs[-2:]
    rank, cols = keep_ref.shape
    total = None
    for turned, part, chunk, chunk_part in plan:
        size = refs[turned].shape[2]
        for at in range(0, size, block):
            rows = jnp.concatenate(split(refs[turned][part, :, at : at + block]), 0)
            here = slice(chunk_part * size + at, chunk_part * size + at + block)
            high, low = split(jnp.concatenate([refs[chunk][here, :], refs[chunk + 1][here, :]], 1))
            both = mm(rows, low) + mm(rows, high)
            total = both if total is None else total + both
    total = total[rank:] + total[:rank]
    keep, give = total[:, :cols], total[:, cols:]
    if len(refs) > 2 + max(step[2] for step in plan) + 2:
        keep = refs[-4][...] + keep
        give = refs[-3][...] + give
    keep_ref[...] = keep
    give_ref[...] = give


def weigh(turned, chunks, plan, acc=(), cost=COST, block=384):
    rank = turned[0].shape[1]
    cols = chunks[0][0].shape[1]
    args = list(turned) + [array for chunk in chunks for array in chunk] + list(acc)
    plan = [(t, part, len(turned) + 2 * c, chunk_part) for t, part, c, chunk_part in plan]
    return pl.pallas_call(
        functools.partial(weigh_body, plan=plan, block=block),
        out_shape=(pltpu.VMEM((rank, cols), F32),) * 2,
        in_specs=[WHOLE] * len(args),
        out_specs=(WHOLE, WHOLE),
        compiler_params=PARAMS,
        cost_estimate=cost,
        name="weigh",
    )(*args)


def project_body(inverse_ref, keep_ref, give_ref, out_ref):
    dot = functools.partial(jnp.dot, precision=lax.Precision.HIGHEST, preferred_element_type=F32)
    rank, cols = keep_ref.shape
    keep = dot(inverse_ref[...], keep_ref[...])
    give = dot(inverse_ref[...], give_ref[...])
    first = lax.axis_index("core") == 0
    both = jnp.concatenate([jnp.where(first, keep, give), jnp.where(first, give, keep)], 1)
    for part in range(16):
        span = slice(part * (rank // 16), (part + 1) * (rank // 16))
        out_ref[part, 0] = both[span, :cols]
        out_ref[part, 1] = both[span, cols:]


def project(inverse, keep, give):
    rank, cols = keep.shape
    out = pl.pallas_call(
        project_body,
        out_shape=jax.ShapeDtypeStruct((16, 2, rank // 16, cols), F32),
        in_specs=[WHOLE] * 3,
        out_specs=WHOLE,
        compiler_params=PARAMS,
        cost_estimate=COST,
        name="project",
    )(inverse, keep, give)
    return out.reshape(2 * rank, cols)


def shards(panel, test_matrix, prior_sketch):
    rows, rank = prior_sketch.shape
    half = rows // 2
    total_rows = panel.shape[0] * lax.axis_size("y") * lax.axis_size("z")

    panel = pltpu.with_memory_space_constraint(panel, pltpu.HBM)
    test_other = swap(test_matrix)
    (far_give,) = fetch(panel, rows, (2, 1))
    panel, far_give, test_other = lax.optimization_barrier((panel, far_give, test_other))
    tests = (test_matrix, test_other)
    far_other = swap(far_give)
    far_keep, right_keep, left_keep, here_keep, *give = fetch(
        panel, rows, (2, 0), (1, 0), (3, 0), (0, 0), (1, 1), (3, 1), (0, 1)
    )
    far = (far_keep, far_other)
    far_top = term(far, 0, half, tests)
    far_bot = term(far, half, half, tests)
    far_top, far_bot, *give = lax.optimization_barrier((far_top, far_bot, *give))
    far_top = shift(far_top, "x", 1)
    far_bot = shift(far_bot, "x", 3)
    right = (right_keep, swap(give[0]))
    left = (left_keep, swap(give[1]))
    near_bot = term(right, half, half, tests)
    near_top = term(left, 0, half, tests)
    near_bot, near_top, here_give = lax.optimization_barrier((near_bot, near_top, give[2]))
    near_bot = shift(near_bot, "x", 1)
    near_top = shift(near_top, "x", 3)
    here = (here_keep, swap(here_give))
    base = term(here, 0, rows, tests, (prior_sketch,), (near_top, near_bot), cost=FIRST)
    far_top, far_bot = lax.optimization_barrier((far_top, far_bot))
    both_top = shift(term(right, 0, half, tests, (far_top,)), "x", 1)
    both_bot = shift(term(left, half, half, tests, (far_bot,)), "x", 3)
    own, turned = finish(base, both_top, both_bot)

    from_left = shift(turned, "x", 1)
    from_right = shift(turned, "x", 3)
    keep, give = gather(gram_of(own, turned))
    gram = keep + swap(give)
    gram = axis_sum(axis_sum(gram, "y"), "z")
    gram, turned = lax.optimization_barrier((gram, turned))
    acc = weigh([turned], [here], [(0, 0, 0, 0), (0, 1, 0, 1)])
    across = [shift(gram, "x", by) for by in (2, 1, 3)]

    acc, from_left, from_right = lax.optimization_barrier((acc, from_left, from_right))
    far_bot = shift(from_left[1:], "x", 1)
    far_top = shift(from_right[:1], "x", 3)
    acc = weigh(
        [from_left, from_right],
        [left, right],
        [(0, 0, 0, 0), (0, 1, 0, 1), (1, 0, 1, 0), (1, 1, 1, 1)],
        acc,
    )
    gram = gram + across[0] + across[1] + across[2]
    gram, acc = lax.optimization_barrier((gram, acc))
    inverse, scaled = factor_inverse(gram, swap(gram), float(total_rows) ** 0.5)
    basis = basis_of(own, scaled)

    far_top, far_bot, inverse = lax.optimization_barrier((far_top, far_bot, inverse))
    weights = weigh([far_top, far_bot], [far], [(0, 0, 0, 0), (1, 0, 0, 1)], acc)
    weights = project(inverse, *weights)
    parts = lax.all_to_all(weights, ("y", "z", "core"), 0, 0, tiled=True)
    return basis, jnp.sum(parts.reshape(-1, rank // 16, rank), 0)


def solution(mesh):
    fine = Mesh(mesh.devices.reshape(4, 4, 4, 2), AXES)
    return jax.shard_map(
        shards,
        mesh=fine,
        in_specs=(P(("y", "z"), ("x", "core")), P(("x", "core"), None), P(AXES, None)),
        out_specs=(P(AXES, None), P(("y", "z"), ("x", "core"))),
        check_vma=False,
    )
```

time: 105 us -> 94.8 us (0.903)
  waiting for transfers between devices: 42.5 us -> 35.4 us
  Pallas kernels: 20.2 us -> 17.5 us
  starting transfers between devices: 37.8 us -> 40.1 us
  other arithmetic: 2.1 us -> 0.66 us
  local copies, waits for them, and re-layouts: 1.3 us -> 0.07 us
    ppermute x20 -> x26, starting transfers between devices: 24.1 us -> 36.2 us  [shift(): return lax.ppermute(block, axis, [(i, (i + by) % n) for i in range(n)])]
    ppermute x4 -> x0, waiting for transfers between devices: 9.28 us -> none  [trade(): return lax.ppermute(block, axis, [(i, partner[i]) for i in range(4)])]
    ppermute x4 -> x0, starting transfers between devices: 6.6 us -> none  [trade(): return lax.ppermute(block, axis, [(i, partner[i]) for i in range(4)])]
    all_to_all x1, starting transfers between devices: 7.12 us -> 3.85 us  [shards(): parts = lax.all_to_all(weights, ('y', 'z', 'core'), 0, 0, tiled=True)]
    pallas_call x11, Pallas kernels: 10.1 us -> 7.43 us  [the longest x2 3.76 us: fetch(): pl.pallas_call(functools.partial(fetch_body, plan=plan), out_shape=[pltpu...]
    ppermute x20 -> x26, waiting for transfers between devices: 27.9 us -> 29.9 us  [shift(): return lax.ppermute(block, axis, [(i, (i + by) % n) for i in range(n)])]
    another operation x1 -> x0, other arithmetic: 1.28 us -> none  [shards(): here_keep, here_give = fetch(jnp.stack([keep[3], give[3]]), panel, rows)]
    slice x3 -> x0, local copies, waits for them, and re-layouts: 1.23 us -> none  [the longest x1 0.58 us: shards(): here_keep, here_give = fetch(jnp.stack([keep[3], give[3]]), panel, rows)]
  transfers between devices with their start and end apart: 25 -> 27, of which waited for: 15 -> 11; matrix products, arithmetic and copies ran while one was open for 2% -> 0% of each run, Pallas kernels for 13% -> 16%
where the time goes in v3:
time: 94.8 us; the launch traced here: 94.6 us
  starting transfers between devices  40.1 us (42%)
  waiting for transfers between devices  35.4 us (37%)
  Pallas kernels  17.5 us (18%)
    ppermute x26, starting transfers between devices, shift(): return lax.ppermute(block, axis, [(i, (i + by) % n) for i in range(n)])  36.2 us
    ppermute x26, waiting for transfers between devices, shift(): return lax.ppermute(block, axis, [(i, (i + by) % n) for i in range(n)])  29.9 us
    all_to_all x1, waiting for transfers between devices, shards(): parts = lax.all_to_all(weights, ('y', 'z', 'core'), 0, 0, tiled=True)  5.5 us
    pallas_call x1, Pallas kernels, factor_inverse(): pl.pallas_call(functools.partial(factor_body, scale=scale), out_shape=(ou...  3.87 us
    all_to_all x1, starting transfers between devices, shards(): parts = lax.all_to_all(weights, ('y', 'z', 'core'), 0, 0, tiled=True)  3.85 us
    pallas_call x2, Pallas kernels, fetch(): pl.pallas_call(functools.partial(fetch_body, plan=plan), out_shape=[pltpu...  3.76 us
    pallas_call x7, Pallas kernels, term(): pl.pallas_call(functools.partial(term_body, first=first, sizes=sizes, blo...  2.85 us
    pallas_call x3, Pallas kernels, weigh(): pl.pallas_call(functools.partial(weigh_body, plan=plan, block=block), out...  2.66 us
  transfers between devices with their start and end apart: 27, of which 11 were waited for; matrix products, arithmetic and copies ran while one was open for 0% of the time, Pallas kernels for 16%

profile of v3, /device:TPU:1, one launch (start us, length us, event | category | flops | bytes accessed | tf_op | source)
XLA Modules:
  0.0 94.6 jit_solution(9678366816562656911)
XLA Ops:
  0.6 1.5 %collective-permute-start = (f32[128,128]{1,0:T(8,128)}, f32[128,128]{1,0:T(8,128)S(1)}, u32[]{:S(2)}, u32[]{:S(2)}) collective-permute-start(f32[128,128]{1,0:T(8,128)} %test_ref.13), channel_id=1, source_target_pairs={{0,1},{1,0},{2,3},{3,2},{4,5},{5,4},{6,7},{7,6},{8,9},{9,8},{10,11... | collective-permute-start | bytes 196616 | tf_op jit(solution)/shard_map/ppermute | solution.py:23
  3.6 2.6 %fetch.3 = (f32[1536,128]{1,0:T(8,128)S(1)}, f32[1536,128]{1,0:T(8,128)S(1)}, f32[1536,128]{1,0:T(8,128)S(1)}, f32[1536,128]{1,0:T(8,128)S(1)}, f32[1536,128]{1,...) custom-call(f32[12288,128]{1,0:T(8,128)} %panel_ref.2), custom_call_target="tpu_custom_call" | custom-call | tf_op jit(solution)/shard_map/fetch/pallas_call | solution.py:65
  7.6 1.3 %collective-permute-start.7 = (f32[768,128]{1,0:T(8,128)S(1)}, f32[768,128]{1,0:T(8,128)S(1)}, u32[]{:S(2)}, u32[]{:S(2)}) collective-permute-start(f32[768,128]{1,0:T(8,128)S(1)} %term.7), channel_id=1, source_target_pairs={{0,2},{2,4},{4,6},{6,0},{1,3},{3,5},{5,7},{7,1},{8,10},{10,12},{12... | collective-permute-start | bytes 1179656 | tf_op jit(solution)/shard_map/ppermute | solution.py:23
  8.9 1.4 %collective-permute-start.8 = (f32[768,128]{1,0:T(8,128)S(1)}, f32[768,128]{1,0:T(8,128)S(1)}, u32[]{:S(2)}, u32[]{:S(2)}) collective-permute-start(f32[768,128]{1,0:T(8,128)S(1)} %term.8), channel_id=1, source_target_pairs={{0,6},{2,0},{4,2},{6,4},{1,7},{3,1},{5,3},{7,5},{8,14},{10,8},{12,... | collective-permute-start | bytes 1179656 | tf_op jit(solution)/shard_map/ppermute | solution.py:23
  12.0 7.3 %collective-permute-done.7.rest_0_ = f32[768,128]{1,0:T(8,128)S(1)} collective-permute-done((f32[768,128]{1,0:T(8,128)S(1)}, f32[768,128]{1,0:T(8,128)S(1)}, u32[]{:S(2)}, u32[]{:S(2)}) %collective-permute-start.7) | collective-permute-done | bytes 393248 | tf_op jit(solution)/shard_map/ppermute | solution.py:23
  19.3 2.4 %collective-permute-start.5 = (f32[768,128]{1,0:T(8,128)S(1)}, f32[768,128]{1,0:T(8,128)S(1)}, u32[]{:S(2)}, u32[]{:S(2)}) collective-permute-start(f32[768,128]{1,0:T(8,128)S(1)} %term.10), channel_id=1, source_target_pairs={{0,6},{2,0},{4,2},{6,4},{1,7},{3,1},{5,3},{7,5},{8,14},{10,8},{12,... | collective-permute-start | bytes 1179656 | tf_op jit(solution)/shard_map/ppermute | solution.py:23
  22.5 2.7 %collective-permute-start.10 = (f32[768,128]{1,0:T(8,128)S(1)}, f32[768,128]{1,0:T(8,128)S(1)}, u32[]{:S(2)}, u32[]{:S(2)}) collective-permute-start(f32[768,128]{1,0:T(8,128)S(1)} %term.13), channel_id=1, source_target_pairs={{0,6},{2,0},{4,2},{6,4},{1,7},{3,1},{5,3},{7,5},{8,14},{10,8},{12,... | collective-permute-start | bytes 1179656 | tf_op jit(solution)/shard_map/ppermute | solution.py:23
  25.2 3.5 %collective-permute-done.5.rest_1_ = f32[768,128]{1,0:T(8,128)S(1)} collective-permute-done((f32[768,128]{1,0:T(8,128)S(1)}, f32[768,128]{1,0:T(8,128)S(1)}, u32[]{:S(2)}, u32[]{:S(2)}) %collective-permute-start.5) | collective-permute-done | bytes 393248 | tf_op jit(solution)/shard_map/ppermute | solution.py:23
  28.7 3.0 %collective-permute-done.6.rest_2_ = f32[768,128]{1,0:T(8,128)S(1)} collective-permute-done((f32[768,128]{1,0:T(8,128)S(1)}, f32[768,128]{1,0:T(8,128)S(1)}, u32[]{:S(2)}, u32[]{:S(2)}) %collective-permute-start.6) | collective-permute-done | bytes 393248 | tf_op jit(solution)/shard_map/ppermute | solution.py:23
  32.4 7.8 %collective-permute-done.9.top_ref = f32[768,128]{1,0:T(8,128)S(1)} collective-permute-done((f32[768,128]{1,0:T(8,128)S(1)}, f32[768,128]{1,0:T(8,128)S(1)}, u32[]{:S(2)}, u32[]{:S(2)}) %collective-permute-start.9) | collective-permute-done | bytes 393248 | tf_op jit(solution)/shard_map/ppermute | solution.py:23
  42.8 3.2 %collective-permute-start.11 = (f32[64,128]{1,0:T(8,128)S(1)}, f32[64,128]{1,0:T(8,128)S(1)}, u32[]{:S(2)}, u32[]{:S(2)}) collective-permute-start(f32[64,128]{1,0:T(8,128)S(1)} %get-tuple-element.69), channel_id=1, source_target_pairs={{0,1},{1,0},{2,3},{3,2},{4,5},{5,4},{6,7},{7,6},{8,9},{9,8},{10,11... | collective-permute-start | bytes 98312 | tf_op jit(solution)/shard_map/ppermute | solution.py:23
  47.0 3.0 %collective-permute-start.14 = (f32[64,128]{1,0:T(8,128)S(1)}, f32[64,128]{1,0:T(8,128)S(1)}, u32[]{:S(2)}, u32[]{:S(2)}) collective-permute-start(f32[64,128]{1,0:T(8,128)S(1)} %add.30), channel_id=1, source_target_pairs={{0,64},{32,96},{64,0},{96,32},{1,65},{33,97},{65,1},{97,33},{2,66}... | collective-permute-start | bytes 98312 | tf_op jit(solution)/shard_map/ppermute | solution.py:23
  51.4 1.7 %collective-permute-done.13 = f32[64,128]{1,0:T(8,128)S(1)} collective-permute-done((f32[64,128]{1,0:T(8,128)S(1)}, f32[64,128]{1,0:T(8,128)S(1)}, u32[]{:S(2)}, u32[]{:S(2)}) %collective-permute-start.13) | collective-permute-done | bytes 32800 | tf_op jit(solution)/shard_map/ppermute | solution.py:23
  53.1 1.9 %collective-permute-done.12 = f32[64,128]{1,0:T(8,128)S(1)} collective-permute-done((f32[64,128]{1,0:T(8,128)S(1)}, f32[64,128]{1,0:T(8,128)S(1)}, u32[]{:S(2)}, u32[]{:S(2)}) %collective-permute-start.12) | collective-permute-done | bytes 32800 | tf_op jit(solution)/shard_map/ppermute | solution.py:23
  55.0 3.7 %collective-permute-start.17 = (f32[64,128]{1,0:T(8,128)S(1)}, f32[64,128]{1,0:T(8,128)S(1)}, u32[]{:S(2)}, u32[]{:S(2)}) collective-permute-start(f32[64,128]{1,0:T(8,128)S(1)} %add_add_fusion.2), channel_id=1, source_target_pairs={{0,16},{8,24},{16,0},{24,8},{1,17},{9,25},{17,1},{25,9},{2,18},{10... | collective-permute-start | bytes 98312 | tf_op jit(solution)/shard_map/ppermute | solution.py:23
  60.2 1.6 %collective-permute-done.16 = f32[64,128]{1,0:T(8,128)S(1)} collective-permute-done((f32[64,128]{1,0:T(8,128)S(1)}, f32[64,128]{1,0:T(8,128)S(1)}, u32[]{:S(2)}, u32[]{:S(2)}) %collective-permute-start.16) | collective-permute-done | bytes 32800 | tf_op jit(solution)/shard_map/ppermute | solution.py:23
  61.7 1.4 %collective-permute-done.15 = f32[64,128]{1,0:T(8,128)S(1)} collective-permute-done((f32[64,128]{1,0:T(8,128)S(1)}, f32[64,128]{1,0:T(8,128)S(1)}, u32[]{:S(2)}, u32[]{:S(2)}) %collective-permute-start.15) | collective-permute-done | bytes 32800 | tf_op jit(solution)/shard_map/ppermute | solution.py:23
  63.1 1.3 %collective-permute-start.20 = (f32[64,128]{1,0:T(8,128)S(1)}, f32[64,128]{1,0:T(8,128)S(1)}, u32[]{:S(2)}, u32[]{:S(2)}) collective-permute-start(f32[64,128]{1,0:T(8,128)S(1)} %add_add_fusion.1), channel_id=1, source_target_pairs={{0,6},{2,0},{4,2},{6,4},{1,7},{3,1},{5,3},{7,5},{8,14},{10,8},{12,... | collective-permute-start | bytes 98312 | tf_op jit(solution)/shard_map/ppermute | solution.py:23
  66.5 2.1 %collective-permute-start.25 = (f32[1,128,768]{2,1,0:T(8,128)S(1)}, f32[1,128,768]{2,1,0:T(8,128)S(1)}, u32[]{:S(2)}, u32[]{:S(2)}) collective-permute-start(f32[1,128,768]{2,1,0:T(8,128)S(1)} %slice.7), channel_id=1, source_target_pairs={{0,2},{2,4},{4,6},{6,0},{1,3},{3,5},{5,7},{7,1},{8,10},{10,12},{12... | collective-permute-start | bytes 1179656 | tf_op jit(solution)/shard_map/ppermute | solution.py:23
  70.5 5.4 %collective-permute-start.23 = (f32[64,128]{1,0:T(8,128)S(1)}, f32[64,128]{1,0:T(8,128)S(1)}, u32[]{:S(2)}, u32[]{:S(2)}) collective-permute-start(f32[64,128]{1,0:T(8,128)S(1)} %add_add_fusion.mine_ref), channel_id=1, source_target_pairs={{0,1},{1,0},{2,3},{3,2},{4,5},{5,4},{6,7},{7,6},{8,9},{9,8},{10,11... | collective-permute-start | bytes 98312 | tf_op jit(solution)/shard_map/ppermute | solution.py:23
  76.7 3.9 %factor.1 = (f32[128,128]{1,0:T(8,128)S(1)}, f32[128,128]{1,0:T(8,128)S(1)}) custom-call(f32[64,128]{1,0:T(8,128)S(1)} %add_add_fusion.mine_ref, f32[64,128]{1,0:T(8,128)S(1)} %collective-permute-done.23.other_ref), custom_call_target="tpu_custom_call" | custom-call | flops 2000000000 | tf_op jit(solution)/shard_map/factor/pallas_call | solution.py:231
  82.3 3.9 %all-to-all-start = ((f32[32,8,128]{2,1,0:T(8,128)}), f32[32,8,128]{2,1,0:T(8,128)S(1)}, u32[]{:S(2)}, u32[]{:S(2)}) async-start(f32[32,8,128]{2,1,0:T(8,128)} %bitcast), calls=%async_computation | async-start | bytes 262144 | tf_op jit(solution)/shard_map/all_to_all | solution.py:390
  86.1 2.3 %basis.1 = f32[1536,128]{1,0:T(8,128)} custom-call(f32[1536,128]{1,0:T(8,128)S(1)} %get-tuple-element.66.own_ref, f32[128,128]{1,0:T(8,128)S(1)} %get-tuple-element.81.turned_ref), custom_call_target="tpu_custom_call" | custom-call | tf_op jit(solution)/shard_map/basis/pallas_call | solution.py:251
  88.4 5.5 %all-to-all-done = f32[32,8,128]{2,1,0:T(8,128)S(1)} async-done(((f32[32,8,128]{2,1,0:T(8,128)}), f32[32,8,128]{2,1,0:T(8,128)S(1)}, u32[]{:S(2)}, u32[]{:S(2)}) %all-to-all-start) | async-done | bytes 131104 | tf_op jit(solution)/shard_map/all_to_all | solution.py:390
  (59 shorter events, 19.5 us)
Async XLA Ops:
  7.0 3.3 %collective-permute-start.2 = (f32[1536,128]{1,0:T(8,128)S(1)}, f32[1536,128]{1,0:T(8,128)S(1)}, u32[]{:S(2)}, u32[]{:S(2)}) collective-permute-start(f32[1536,128]{1,0:T(8,128)S(1)} %get-tuple-element.55), channel_id=1, source_target_pairs={{0,1},{1,0},{2,3},{3,2},{4,5},{5,4},{6,7},{7,6},{8,9},{9,8},{10,11... | collective-permute-start | bytes 2359304 | tf_op jit(solution)/shard_map/ppermute | solution.py:23
  7.4 3.3 %collective-permute-start.3 = (f32[1536,128]{1,0:T(8,128)S(1)}, f32[1536,128]{1,0:T(8,128)S(1)}, u32[]{:S(2)}, u32[]{:S(2)}) collective-permute-start(f32[1536,128]{1,0:T(8,128)S(1)} %get-tuple-element.57), channel_id=1, source_target_pairs={{0,1},{1,0},{2,3},{3,2},{4,5},{5,4},{6,7},{7,6},{8,9},{9,8},{10,11... | collective-permute-start | bytes 2359304 | tf_op jit(solution)/shard_map/ppermute | solution.py:23
  7.6 11.6 %collective-permute-start.7 = (f32[768,128]{1,0:T(8,128)S(1)}, f32[768,128]{1,0:T(8,128)S(1)}, u32[]{:S(2)}, u32[]{:S(2)}) collective-permute-start(f32[768,128]{1,0:T(8,128)S(1)} %term.7), channel_id=1, source_target_pairs={{0,2},{2,4},{4,6},{6,0},{1,3},{3,5},{5,7},{7,1},{8,10},{10,12},{12... | collective-permute-start | bytes 1179656 | tf_op jit(solution)/shard_map/ppermute | solution.py:23
  8.9 10.4 %collective-permute-start.8 = (f32[768,128]{1,0:T(8,128)S(1)}, f32[768,128]{1,0:T(8,128)S(1)}, u32[]{:S(2)}, u32[]{:S(2)}) collective-permute-start(f32[768,128]{1,0:T(8,128)S(1)} %term.8), channel_id=1, source_target_pairs={{0,6},{2,0},{4,2},{6,4},{1,7},{3,1},{5,3},{7,5},{8,14},{10,8},{12,... | collective-permute-start | bytes 1179656 | tf_op jit(solution)/shard_map/ppermute | solution.py:23
  11.1 20.7 %collective-permute-start.4 = (f32[1536,128]{1,0:T(8,128)S(1)}, f32[1536,128]{1,0:T(8,128)S(1)}, u32[]{:S(2)}, u32[]{:S(2)}) collective-permute-start(f32[1536,128]{1,0:T(8,128)S(1)} %get-tuple-element.59), channel_id=1, source_target_pairs={{0,1},{1,0},{2,3},{3,2},{4,5},{5,4},{6,7},{7,6},{8,9},{9,8},{10,11... | collective-permute-start | bytes 2359304 | tf_op jit(solution)/shard_map/ppermute | solution.py:23
  19.3 9.4 %collective-permute-start.5 = (f32[768,128]{1,0:T(8,128)S(1)}, f32[768,128]{1,0:T(8,128)S(1)}, u32[]{:S(2)}, u32[]{:S(2)}) collective-permute-start(f32[768,128]{1,0:T(8,128)S(1)} %term.10), channel_id=1, source_target_pairs={{0,6},{2,0},{4,2},{6,4},{1,7},{3,1},{5,3},{7,5},{8,14},{10,8},{12,... | collective-permute-start | bytes 1179656 | tf_op jit(solution)/shard_map/ppermute | solution.py:23
  21.6 10.1 %collective-permute-start.6 = (f32[768,128]{1,0:T(8,128)S(1)}, f32[768,128]{1,0:T(8,128)S(1)}, u32[]{:S(2)}, u32[]{:S(2)}) collective-permute-start(f32[768,128]{1,0:T(8,128)S(1)} %term.9), channel_id=1, source_target_pairs={{0,2},{2,4},{4,6},{6,0},{1,3},{3,5},{5,7},{7,1},{8,10},{10,12},{12... | collective-permute-start | bytes 1179656 | tf_op jit(solution)/shard_map/ppermute | solution.py:23
  22.0 18.2 %collective-permute-start.9 = (f32[768,128]{1,0:T(8,128)S(1)}, f32[768,128]{1,0:T(8,128)S(1)}, u32[]{:S(2)}, u32[]{:S(2)}) collective-permute-start(f32[768,128]{1,0:T(8,128)S(1)} %term.12), channel_id=1, source_target_pairs={{0,2},{2,4},{4,6},{6,0},{1,3},{3,5},{5,7},{7,1},{8,10},{10,12},{12... | collective-permute-start | bytes 1179656 | tf_op jit(solution)/shard_map/ppermute | solution.py:23
  22.5 17.7 %collective-permute-start.10 = (f32[768,128]{1,0:T(8,128)S(1)}, f32[768,128]{1,0:T(8,128)S(1)}, u32[]{:S(2)}, u32[]{:S(2)}) collective-permute-start(f32[768,128]{1,0:T(8,128)S(1)} %term.13), channel_id=1, source_target_pairs={{0,6},{2,0},{4,2},{6,4},{1,7},{3,1},{5,3},{7,5},{8,14},{10,8},{12,... | collective-permute-start | bytes 1179656 | tf_op jit(solution)/shard_map/ppermute | solution.py:23
  40.5 25.9 %collective-permute-start.22 = (f32[2,128,768]{2,1,0:T(8,128)S(1)}, f32[2,128,768]{2,1,0:T(8,128)S(1)}, u32[]{:S(2)}, u32[]{:S(2)}) collective-permute-start(f32[2,128,768]{2,1,0:T(8,128)S(1)} %get-tuple-element.71.turned_ref.refs_0_), channel_id=1, source_target_pairs={{0,6},{2,0},{4,2},{6,4},{1,7},{3,1},{5,3},{7,5},{8,14},{10,8},{12,... | collective-permute-start | bytes 2359304 | tf_op jit(solution)/shard_map/ppermute | solution.py:23
  40.8 25.6 %collective-permute-start.21 = (f32[2,128,768]{2,1,0:T(8,128)S(1)}, f32[2,128,768]{2,1,0:T(8,128)S(1)}, u32[]{:S(2)}, u32[]{:S(2)}) collective-permute-start(f32[2,128,768]{2,1,0:T(8,128)S(1)} %get-tuple-element.71.turned_ref.refs_0_), channel_id=1, source_target_pairs={{0,2},{2,4},{4,6},{6,0},{1,3},{3,5},{5,7},{7,1},{8,10},{10,12},{12... | collective-permute-start | bytes 2359304 | tf_op jit(solution)/shard_map/ppermute | solution.py:23
  42.8 4.1 %collective-permute-start.11 = (f32[64,128]{1,0:T(8,128)S(1)}, f32[64,128]{1,0:T(8,128)S(1)}, u32[]{:S(2)}, u32[]{:S(2)}) collective-permute-start(f32[64,128]{1,0:T(8,128)S(1)} %get-tuple-element.69), channel_id=1, source_target_pairs={{0,1},{1,0},{2,3},{3,2},{4,5},{5,4},{6,7},{7,6},{8,9},{9,8},{10,11... | collective-permute-start | bytes 98312 | tf_op jit(solution)/shard_map/ppermute | solution.py:23
  47.0 4.5 %collective-permute-start.14 = (f32[64,128]{1,0:T(8,128)S(1)}, f32[64,128]{1,0:T(8,128)S(1)}, u32[]{:S(2)}, u32[]{:S(2)}) collective-permute-start(f32[64,128]{1,0:T(8,128)S(1)} %add.30), channel_id=1, source_target_pairs={{0,64},{32,96},{64,0},{96,32},{1,65},{33,97},{65,1},{97,33},{2,66}... | collective-permute-start | bytes 98312 | tf_op jit(solution)/shard_map/ppermute | solution.py:23
  50.0 3.1 %collective-permute-start.13 = (f32[64,128]{1,0:T(8,128)S(1)}, f32[64,128]{1,0:T(8,128)S(1)}, u32[]{:S(2)}, u32[]{:S(2)}) collective-permute-start(f32[64,128]{1,0:T(8,128)S(1)} %add.30), channel_id=1, source_target_pairs={{0,96},{32,0},{64,32},{96,64},{1,97},{33,1},{65,33},{97,65},{2,98}... | collective-permute-start | bytes 98312 | tf_op jit(solution)/shard_map/ppermute | solution.py:23
  50.7 4.3 %collective-permute-start.12 = (f32[64,128]{1,0:T(8,128)S(1)}, f32[64,128]{1,0:T(8,128)S(1)}, u32[]{:S(2)}, u32[]{:S(2)}) collective-permute-start(f32[64,128]{1,0:T(8,128)S(1)} %add.30), channel_id=1, source_target_pairs={{0,32},{32,64},{64,96},{96,0},{1,33},{33,65},{65,97},{97,1},{2,34}... | collective-permute-start | bytes 98312 | tf_op jit(solution)/shard_map/ppermute | solution.py:23
  55.0 5.1 %collective-permute-start.17 = (f32[64,128]{1,0:T(8,128)S(1)}, f32[64,128]{1,0:T(8,128)S(1)}, u32[]{:S(2)}, u32[]{:S(2)}) collective-permute-start(f32[64,128]{1,0:T(8,128)S(1)} %add_add_fusion.2), channel_id=1, source_target_pairs={{0,16},{8,24},{16,0},{24,8},{1,17},{9,25},{17,1},{25,9},{2,18},{10... | collective-permute-start | bytes 98312 | tf_op jit(solution)/shard_map/ppermute | solution.py:23
  59.1 4.0 %collective-permute-start.15 = (f32[64,128]{1,0:T(8,128)S(1)}, f32[64,128]{1,0:T(8,128)S(1)}, u32[]{:S(2)}, u32[]{:S(2)}) collective-permute-start(f32[64,128]{1,0:T(8,128)S(1)} %add_add_fusion.2), channel_id=1, source_target_pairs={{0,8},{8,16},{16,24},{24,0},{1,9},{9,17},{17,25},{25,1},{2,10},{10... | collective-permute-start | bytes 98312 | tf_op jit(solution)/shard_map/ppermute | solution.py:23
  63.1 6.1 %collective-permute-start.20 = (f32[64,128]{1,0:T(8,128)S(1)}, f32[64,128]{1,0:T(8,128)S(1)}, u32[]{:S(2)}, u32[]{:S(2)}) collective-permute-start(f32[64,128]{1,0:T(8,128)S(1)} %add_add_fusion.1), channel_id=1, source_target_pairs={{0,6},{2,0},{4,2},{6,4},{1,7},{3,1},{5,3},{7,5},{8,14},{10,8},{12,... | collective-permute-start | bytes 98312 | tf_op jit(solution)/shard_map/ppermute | solution.py:23
  64.4 4.8 %collective-permute-start.19 = (f32[64,128]{1,0:T(8,128)S(1)}, f32[64,128]{1,0:T(8,128)S(1)}, u32[]{:S(2)}, u32[]{:S(2)}) collective-permute-start(f32[64,128]{1,0:T(8,128)S(1)} %add_add_fusion.1), channel_id=1, source_target_pairs={{0,2},{2,4},{4,6},{6,0},{1,3},{3,5},{5,7},{7,1},{8,10},{10,12},{12... | collective-permute-start | bytes 98312 | tf_op jit(solution)/shard_map/ppermute | solution.py:23
  64.6 4.6 %collective-permute-start.18 = (f32[64,128]{1,0:T(8,128)S(1)}, f32[64,128]{1,0:T(8,128)S(1)}, u32[]{:S(2)}, u32[]{:S(2)}) collective-permute-start(f32[64,128]{1,0:T(8,128)S(1)} %add_add_fusion.1), channel_id=1, source_target_pairs={{0,4},{2,6},{4,0},{6,2},{1,5},{3,7},{5,1},{7,3},{8,12},{10,14},{12... | collective-permute-start | bytes 98312 | tf_op jit(solution)/shard_map/ppermute | solution.py:23
  66.5 14.2 %collective-permute-start.25 = (f32[1,128,768]{2,1,0:T(8,128)S(1)}, f32[1,128,768]{2,1,0:T(8,128)S(1)}, u32[]{:S(2)}, u32[]{:S(2)}) collective-permute-start(f32[1,128,768]{2,1,0:T(8,128)S(1)} %slice.7), channel_id=1, source_target_pairs={{0,2},{2,4},{4,6},{6,0},{1,3},{3,5},{5,7},{7,1},{8,10},{10,12},{12... | collective-permute-start | bytes 1179656 | tf_op jit(solution)/shard_map/ppermute | solution.py:23
  68.5 12.1 %collective-permute-start.24 = (f32[1,128,768]{2,1,0:T(8,128)S(1)}, f32[1,128,768]{2,1,0:T(8,128)S(1)}, u32[]{:S(2)}, u32[]{:S(2)}) collective-permute-start(f32[1,128,768]{2,1,0:T(8,128)S(1)} %slice.6), channel_id=1, source_target_pairs={{0,6},{2,0},{4,2},{6,4},{1,7},{3,1},{5,3},{7,5},{8,14},{10,8},{12,... | collective-permute-start | bytes 1179656 | tf_op jit(solution)/shard_map/ppermute | solution.py:23
  70.5 6.2 %collective-permute-start.23 = (f32[64,128]{1,0:T(8,128)S(1)}, f32[64,128]{1,0:T(8,128)S(1)}, u32[]{:S(2)}, u32[]{:S(2)}) collective-permute-start(f32[64,128]{1,0:T(8,128)S(1)} %add_add_fusion.mine_ref), channel_id=1, source_target_pairs={{0,1},{1,0},{2,3},{3,2},{4,5},{5,4},{6,7},{7,6},{8,9},{9,8},{10,11... | collective-permute-start | bytes 98312 | tf_op jit(solution)/shard_map/ppermute | solution.py:23
  82.3 11.7 %all-to-all-start = ((f32[32,8,128]{2,1,0:T(8,128)}), f32[32,8,128]{2,1,0:T(8,128)S(1)}, u32[]{:S(2)}, u32[]{:S(2)}) async-start(f32[32,8,128]{2,1,0:T(8,128)} %bitcast), calls=%async_computation | async-start | bytes 262144 | tf_op jit(solution)/shard_map/all_to_all | solution.py:390
  (5 other events, 39.8 us)

commit v4 on v3

--- a/solution.py
+++ b/solution.py
@@ -12,8 +12,8 @@
 BF16 = jnp.bfloat16
 LIMIT = 16 * 1024 * 1024
 COST = pl.CostEstimate(flops=0, bytes_accessed=0, transcendentals=0)
-FIRST = pl.CostEstimate(flops=0, bytes_accessed=0, transcendentals=0)
-SLOW = pl.CostEstimate(flops=2 * 10**9, bytes_accessed=0, transcendentals=0)
+FIRST = pl.CostEstimate(flops=3 * 10**8, bytes_accessed=0, transcendentals=0)
+SLOW = pl.CostEstimate(flops=13 * 10**8, bytes_accessed=0, transcendentals=0)
 PARAMS = pltpu.CompilerParams(vmem_limit_bytes=LIMIT)
 WHOLE = pl.BlockSpec(memory_space=pltpu.VMEM)
 
@@ -263,9 +263,7 @@
     )(own, turned)
 
 
-def weigh_body(*refs, plan, block):
-    keep_ref, give_ref = refs[-2:]
-    rank, cols = keep_ref.shape
+def weigh_body(*refs, plan, block, width):
     total = None
     for turned, part, chunk, chunk_part in plan:
         size = refs[turned].shape[2]
@@ -275,56 +273,49 @@
             high, low = split(jnp.concatenate([refs[chunk][here, :], refs[chunk + 1][here, :]], 1))
             both = mm(rows, low) + mm(rows, high)
             total = both if total is None else total + both
+    rank = total.shape[0] // 2
     total = total[rank:] + total[:rank]
+    extra = refs[width:]
+    if len(extra) > 1:
+        total = extra[0][...] + total
+    if len(extra) < 3:
+        extra[-1][...] = total
+        return
+    total = jnp.dot(
+        extra[1][...], total, precision=lax.Precision.HIGHEST, preferred_element_type=F32
+    )
+    first = lax.axis_index("core") == 0
+    cols = rank
     keep, give = total[:, :cols], total[:, cols:]
-    if len(refs) > 2 + max(step[2] for step in plan) + 2:
-        keep = refs[-4][...] + keep
-        give = refs[-3][...] + give
-    keep_ref[...] = keep
-    give_ref[...] = give
-
-
-def weigh(turned, chunks, plan, acc=(), cost=COST, block=384):
+    low_core = jnp.where(first, keep, give)
+    high_core = jnp.where(first, give, keep)
+    out_ref = extra[2]
+    for part in range(out_ref.shape[0]):
+        span = slice(part * (rank // 16), (part + 1) * (rank // 16))
+        out_ref[part, 0] = low_core[span]
+        out_ref[part, 1] = high_core[span]
+
+
+def weigh(turned, chunks, plan, acc=None, inverse=None, block=384):
     rank = turned[0].shape[1]
     cols = chunks[0][0].shape[1]
-    args = list(turned) + [array for chunk in chunks for array in chunk] + list(acc)
+    args = list(turned) + [array for chunk in chunks for array in chunk]
+    width = len(args)
+    args += [array for array in (acc, inverse) if array is not None]
     plan = [(t, part, len(turned) + 2 * c, chunk_part) for t, part, c, chunk_part in plan]
-    return pl.pallas_call(
-        functools.partial(weigh_body, plan=plan, block=block),
-        out_shape=(pltpu.VMEM((rank, cols), F32),) * 2,
+    if inverse is None:
+        out = pltpu.VMEM((rank, 2 * cols), F32)
+    else:
+        out = jax.ShapeDtypeStruct((16, 2, rank // 16, cols), F32)
+    return pl.pallas_call(
+        functools.partial(weigh_body, plan=plan, block=block, width=width),
+        out_shape=out,
         in_specs=[WHOLE] * len(args),
-        out_specs=(WHOLE, WHOLE),
-        compiler_params=PARAMS,
-        cost_estimate=cost,
+        out_specs=WHOLE,
+        compiler_params=PARAMS,
+        cost_estimate=COST,
         name="weigh",
     )(*args)
-
-
-def project_body(inverse_ref, keep_ref, give_ref, out_ref):
-    dot = functools.partial(jnp.dot, precision=lax.Precision.HIGHEST, preferred_element_type=F32)
-    rank, cols = keep_ref.shape
-    keep = dot(inverse_ref[...], keep_ref[...])
-    give = dot(inverse_ref[...], give_ref[...])
-    first = lax.axis_index("core") == 0
-    both = jnp.concatenate([jnp.where(first, keep, give), jnp.where(first, give, keep)], 1)
-    for part in range(16):
-        span = slice(part * (rank // 16), (part + 1) * (rank // 16))
-        out_ref[part, 0] = both[span, :cols]
-        out_ref[part, 1] = both[span, cols:]
-
-
-def project(inverse, keep, give):
-    rank, cols = keep.shape
-    out = pl.pallas_call(
-        project_body,
-        out_shape=jax.ShapeDtypeStruct((16, 2, rank // 16, cols), F32),
-        in_specs=[WHOLE] * 3,
-        out_specs=WHOLE,
-        compiler_params=PARAMS,
-        cost_estimate=COST,
-        name="project",
-    )(inverse, keep, give)
-    return out.reshape(2 * rank, cols)
 
 
 def shards(panel, test_matrix, prior_sketch):
@@ -351,10 +342,10 @@
     left = (left_keep, swap(give[1]))
     near_bot = term(right, half, half, tests)
     near_top = term(left, 0, half, tests)
-    near_bot, near_top, here_give = lax.optimization_barrier((near_bot, near_top, give[2]))
+    near_bot, near_top = lax.optimization_barrier((near_bot, near_top))
     near_bot = shift(near_bot, "x", 1)
     near_top = shift(near_top, "x", 3)
-    here = (here_keep, swap(here_give))
+    here = (here_keep, swap(give[2]))
     base = term(here, 0, rows, tests, (prior_sketch,), (near_top, near_bot), cost=FIRST)
     far_top, far_bot = lax.optimization_barrier((far_top, far_bot))
     both_top = shift(term(right, 0, half, tests, (far_top,)), "x", 1)
@@ -379,15 +370,14 @@
         [(0, 0, 0, 0), (0, 1, 0, 1), (1, 0, 1, 0), (1, 1, 1, 1)],
         acc,
     )
+    acc, across = lax.optimization_barrier((acc, across))
     gram = gram + across[0] + across[1] + across[2]
-    gram, acc = lax.optimization_barrier((gram, acc))
     inverse, scaled = factor_inverse(gram, swap(gram), float(total_rows) ** 0.5)
     basis = basis_of(own, scaled)
 
     far_top, far_bot, inverse = lax.optimization_barrier((far_top, far_bot, inverse))
-    weights = weigh([far_top, far_bot], [far], [(0, 0, 0, 0), (1, 0, 0, 1)], acc)
-    weights = project(inverse, *weights)
-    parts = lax.all_to_all(weights, ("y", "z", "core"), 0, 0, tiled=True)
+    weights = weigh([far_top, far_bot], [far], [(0, 0, 0, 0), (1, 0, 0, 1)], acc, inverse)
+    parts = lax.all_to_all(weights.reshape(2 * rank, -1), ("y", "z", "core"), 0, 0, tiled=True)
     return basis, jnp.sum(parts.reshape(-1, rank // 16, rank), 0)
 
 

time: 94.8 us -> 92.2 us (0.973)
  waiting for transfers between devices: 35.4 us -> 32.8 us
    ppermute x26, waiting for transfers between devices: 29.9 us -> 27.3 us  [shift(): return lax.ppermute(block, axis, [(i, (i + by) % n) for i in range(n)])]
    pallas_call x4 -> x3, Pallas kernels: 3.57 us -> 3.73 us  [weigh(): pl.pallas_call(functools.partial(weigh_body, plan=plan, block=block, widt...]
where the time goes in v4:
time: 92.2 us; the launch traced here: 92 us
  starting transfers between devices  40 us (43%)
  waiting for transfers between devices  32.8 us (36%)
  Pallas kernels  17.6 us (19%)
    ppermute x26, starting transfers between devices, shift(): return lax.ppermute(block, axis, [(i, (i + by) % n) for i in range(n)])  35.5 us
    ppermute x26, waiting for transfers between devices, shift(): return lax.ppermute(block, axis, [(i, (i + by) % n) for i in range(n)])  27.3 us
    all_to_all x1, waiting for transfers between devices, shards(): lax.all_to_all(weights.reshape(2 * rank, -1), ('y', 'z', 'core'), 0, 0, t...  5.49 us
    all_to_all x1, starting transfers between devices, shards(): lax.all_to_all(weights.reshape(2 * rank, -1), ('y', 'z', 'core'), 0, 0, t...  4.45 us
    pallas_call x1, Pallas kernels, factor_inverse(): pl.pallas_call(functools.partial(factor_body, scale=scale), out_shape=(ou...  3.87 us
    pallas_call x2, Pallas kernels, fetch(): pl.pallas_call(functools.partial(fetch_body, plan=plan), out_shape=[pltpu...  3.76 us
    pallas_call x3, Pallas kernels, weigh(): pl.pallas_call(functools.partial(weigh_body, plan=plan, block=block, widt...  3.73 us
    pallas_call x7, Pallas kernels, term(): pl.pallas_call(functools.partial(term_body, first=first, sizes=sizes, blo...  2.85 us
  transfers between devices with their start and end apart: 27, of which 11 were waited for; matrix products, arithmetic and copies ran while one was open for 0% of the time, Pallas kernels for 16%

profile of v4, /device:TPU:1, one launch (start us, length us, event | category | flops | bytes accessed | tf_op | source)
XLA Modules:
  0.0 92.0 jit_solution(14464748400535614924)
XLA Ops:
  0.6 1.5 %collective-permute-start = (f32[128,128]{1,0:T(8,128)}, f32[128,128]{1,0:T(8,128)S(1)}, u32[]{:S(2)}, u32[]{:S(2)}) collective-permute-start(f32[128,128]{1,0:T(8,128)} %test_ref.13), channel_id=1, source_target_pairs={{0,1},{1,0},{2,3},{3,2},{4,5},{5,4},{6,7},{7,6},{8,9},{9,8},{10,11... | collective-permute-start | bytes 196616 | tf_op jit(solution)/shard_map/ppermute | solution.py:23
  3.6 2.6 %fetch.3 = (f32[1536,128]{1,0:T(8,128)S(1)}, f32[1536,128]{1,0:T(8,128)S(1)}, f32[1536,128]{1,0:T(8,128)S(1)}, f32[1536,128]{1,0:T(8,128)S(1)}, f32[1536,128]{1,...) custom-call(f32[12288,128]{1,0:T(8,128)} %panel_ref.2), custom_call_target="tpu_custom_call" | custom-call | tf_op jit(solution)/shard_map/fetch/pallas_call | solution.py:65
  9.2 1.4 %collective-permute-start.8 = (f32[768,128]{1,0:T(8,128)S(1)}, f32[768,128]{1,0:T(8,128)S(1)}, u32[]{:S(2)}, u32[]{:S(2)}) collective-permute-start(f32[768,128]{1,0:T(8,128)S(1)} %term.8), channel_id=1, source_target_pairs={{0,6},{2,0},{4,2},{6,4},{1,7},{3,1},{5,3},{7,5},{8,14},{10,8},{12,... | collective-permute-start | bytes 1179656 | tf_op jit(solution)/shard_map/ppermute | solution.py:23
  11.4 2.2 %collective-permute-start.5 = (f32[768,128]{1,0:T(8,128)S(1)}, f32[768,128]{1,0:T(8,128)S(1)}, u32[]{:S(2)}, u32[]{:S(2)}) collective-permute-start(f32[768,128]{1,0:T(8,128)S(1)} %term.10), channel_id=1, source_target_pairs={{0,6},{2,0},{4,2},{6,4},{1,7},{3,1},{5,3},{7,5},{8,14},{10,8},{12,... | collective-permute-start | bytes 1179656 | tf_op jit(solution)/shard_map/ppermute | solution.py:23
  13.5 6.1 %collective-permute-done.7.rest_0_ = f32[768,128]{1,0:T(8,128)S(1)} collective-permute-done((f32[768,128]{1,0:T(8,128)S(1)}, f32[768,128]{1,0:T(8,128)S(1)}, u32[]{:S(2)}, u32[]{:S(2)}) %collective-permute-start.7) | collective-permute-done | bytes 393248 | tf_op jit(solution)/shard_map/ppermute | solution.py:23
  21.4 1.8 %collective-permute-start.10 = (f32[768,128]{1,0:T(8,128)S(1)}, f32[768,128]{1,0:T(8,128)S(1)}, u32[]{:S(2)}, u32[]{:S(2)}) collective-permute-start(f32[768,128]{1,0:T(8,128)S(1)} %term.13), channel_id=1, source_target_pairs={{0,6},{2,0},{4,2},{6,4},{1,7},{3,1},{5,3},{7,5},{8,14},{10,8},{12,... | collective-permute-start | bytes 1179656 | tf_op jit(solution)/shard_map/ppermute | solution.py:23
  23.2 4.6 %collective-permute-done.5.rest_1_ = f32[768,128]{1,0:T(8,128)S(1)} collective-permute-done((f32[768,128]{1,0:T(8,128)S(1)}, f32[768,128]{1,0:T(8,128)S(1)}, u32[]{:S(2)}, u32[]{:S(2)}) %collective-permute-start.5) | collective-permute-done | bytes 393248 | tf_op jit(solution)/shard_map/ppermute | solution.py:23
  28.6 7.8 %collective-permute-done.9.top_ref = f32[768,128]{1,0:T(8,128)S(1)} collective-permute-done((f32[768,128]{1,0:T(8,128)S(1)}, f32[768,128]{1,0:T(8,128)S(1)}, u32[]{:S(2)}, u32[]{:S(2)}) %collective-permute-start.9) | collective-permute-done | bytes 393248 | tf_op jit(solution)/shard_map/ppermute | solution.py:23
  36.7 2.4 %collective-permute-start.19 = (f32[2,128,768]{2,1,0:T(8,128)S(1)}, f32[2,128,768]{2,1,0:T(8,128)S(1)}, u32[]{:S(2)}, u32[]{:S(2)}) collective-permute-start(f32[2,128,768]{2,1,0:T(8,128)S(1)} %get-tuple-element.63.turned_ref.refs_0_), channel_id=1, source_target_pairs={{0,6},{2,0},{4,2},{6,4},{1,7},{3,1},{5,3},{7,5},{8,14},{10,8},{12,... | collective-permute-start | bytes 2359304 | tf_op jit(solution)/shard_map/ppermute | solution.py:23
  40.0 1.7 %collective-permute-start.11 = (f32[64,128]{1,0:T(8,128)S(1)}, f32[64,128]{1,0:T(8,128)S(1)}, u32[]{:S(2)}, u32[]{:S(2)}) collective-permute-start(f32[64,128]{1,0:T(8,128)S(1)} %get-tuple-element.61), channel_id=1, source_target_pairs={{0,1},{1,0},{2,3},{3,2},{4,5},{5,4},{6,7},{7,6},{8,9},{9,8},{10,11... | collective-permute-start | bytes 98312 | tf_op jit(solution)/shard_map/ppermute | solution.py:23
  42.6 3.0 %collective-permute-start.14 = (f32[64,128]{1,0:T(8,128)S(1)}, f32[64,128]{1,0:T(8,128)S(1)}, u32[]{:S(2)}, u32[]{:S(2)}) collective-permute-start(f32[64,128]{1,0:T(8,128)S(1)} %add.30), channel_id=1, source_target_pairs={{0,64},{32,96},{64,0},{96,32},{1,65},{33,97},{65,1},{97,33},{2,66}... | collective-permute-start | bytes 98312 | tf_op jit(solution)/shard_map/ppermute | solution.py:23
  47.0 1.7 %collective-permute-done.13 = f32[64,128]{1,0:T(8,128)S(1)} collective-permute-done((f32[64,128]{1,0:T(8,128)S(1)}, f32[64,128]{1,0:T(8,128)S(1)}, u32[]{:S(2)}, u32[]{:S(2)}) %collective-permute-start.13) | collective-permute-done | bytes 32800 | tf_op jit(solution)/shard_map/ppermute | solution.py:23
  48.7 1.9 %collective-permute-done.12 = f32[64,128]{1,0:T(8,128)S(1)} collective-permute-done((f32[64,128]{1,0:T(8,128)S(1)}, f32[64,128]{1,0:T(8,128)S(1)}, u32[]{:S(2)}, u32[]{:S(2)}) %collective-permute-start.12) | collective-permute-done | bytes 32800 | tf_op jit(solution)/shard_map/ppermute | solution.py:23
  50.6 3.7 %collective-permute-start.17 = (f32[64,128]{1,0:T(8,128)S(1)}, f32[64,128]{1,0:T(8,128)S(1)}, u32[]{:S(2)}, u32[]{:S(2)}) collective-permute-start(f32[64,128]{1,0:T(8,128)S(1)} %add_add_fusion.2), channel_id=1, source_target_pairs={{0,16},{8,24},{16,0},{24,8},{1,17},{9,25},{17,1},{25,9},{2,18},{10... | collective-permute-start | bytes 98312 | tf_op jit(solution)/shard_map/ppermute | solution.py:23
  55.8 1.6 %collective-permute-done.16 = f32[64,128]{1,0:T(8,128)S(1)} collective-permute-done((f32[64,128]{1,0:T(8,128)S(1)}, f32[64,128]{1,0:T(8,128)S(1)}, u32[]{:S(2)}, u32[]{:S(2)}) %collective-permute-start.16) | collective-permute-done | bytes 32800 | tf_op jit(solution)/shard_map/ppermute | solution.py:23
  57.4 1.6 %collective-permute-done.15 = f32[64,128]{1,0:T(8,128)S(1)} collective-permute-done((f32[64,128]{1,0:T(8,128)S(1)}, f32[64,128]{1,0:T(8,128)S(1)}, u32[]{:S(2)}, u32[]{:S(2)}) %collective-permute-start.15) | collective-permute-done | bytes 32800 | tf_op jit(solution)/shard_map/ppermute | solution.py:23
  59.0 2.7 %collective-permute-start.22 = (f32[64,128]{1,0:T(8,128)S(1)}, f32[64,128]{1,0:T(8,128)S(1)}, u32[]{:S(2)}, u32[]{:S(2)}) collective-permute-start(f32[64,128]{1,0:T(8,128)S(1)} %add_add_fusion.1), channel_id=1, source_target_pairs={{0,6},{2,0},{4,2},{6,4},{1,7},{3,1},{5,3},{7,5},{8,14},{10,8},{12,... | collective-permute-start | bytes 98312 | tf_op jit(solution)/shard_map/ppermute | solution.py:23
  63.8 2.1 %collective-permute-start.25 = (f32[1,128,768]{2,1,0:T(8,128)S(1)}, f32[1,128,768]{2,1,0:T(8,128)S(1)}, u32[]{:S(2)}, u32[]{:S(2)}) collective-permute-start(f32[1,128,768]{2,1,0:T(8,128)S(1)} %slice.7), channel_id=1, source_target_pairs={{0,2},{2,4},{4,6},{6,0},{1,3},{3,5},{5,7},{7,1},{8,10},{10,12},{12... | collective-permute-start | bytes 1179656 | tf_op jit(solution)/shard_map/ppermute | solution.py:23
  67.9 4.7 %collective-permute-start.23 = (f32[64,128]{1,0:T(8,128)S(1)}, f32[64,128]{1,0:T(8,128)S(1)}, u32[]{:S(2)}, u32[]{:S(2)}) collective-permute-start(f32[64,128]{1,0:T(8,128)S(1)} %add_add_fusion.mine_ref), channel_id=1, source_target_pairs={{0,1},{1,0},{2,3},{3,2},{4,5},{5,4},{6,7},{7,6},{8,9},{9,8},{10,11... | collective-permute-start | bytes 98312 | tf_op jit(solution)/shard_map/ppermute | solution.py:23
  73.4 3.9 %factor.1 = (f32[128,128]{1,0:T(8,128)S(1)}, f32[128,128]{1,0:T(8,128)S(1)}) custom-call(f32[64,128]{1,0:T(8,128)S(1)} %add_add_fusion.mine_ref, f32[64,128]{1,0:T(8,128)S(1)} %collective-permute-done.23.other_ref), custom_call_target="tpu_custom_call" | custom-call | flops 1300000000 | tf_op jit(solution)/shard_map/factor/pallas_call | solution.py:231
  77.3 1.8 %weigh.5 = f32[16,2,8,128]{3,2,1,0:T(8,128)} custom-call(f32[1,128,768]{2,1,0:T(8,128)S(1)} %collective-permute-done.24.refs_0_, f32[1,128,768]{2,1,0:T(8,128)S(1)} %collective-permute-done.25.refs_1_, f32[1536,128]{1,0:T(8,128)S(1)} %get-tuple-element.41.mine_ref.refs_2_, f32[1536,128]{1,0:T(8,128)S(1)} %collective-permute-done.1.other_ref.refs_3_, ...), custom_call_target="tpu_custom_call" | custom-call | tf_op jit(solution)/shard_map/weigh/pallas_call | solution.py:310
  79.1 4.5 %all-to-all-start = ((f32[32,8,128]{2,1,0:T(8,128)}), f32[32,8,128]{2,1,0:T(8,128)S(1)}, u32[]{:S(2)}, u32[]{:S(2)}) async-start(f32[32,8,128]{2,1,0:T(8,128)} %bitcast), calls=%async_computation | async-start | bytes 262144 | tf_op jit(solution)/shard_map/all_to_all | solution.py:380
  83.5 2.3 %basis.1 = f32[1536,128]{1,0:T(8,128)} custom-call(f32[1536,128]{1,0:T(8,128)S(1)} %get-tuple-element.58.own_ref, f32[128,128]{1,0:T(8,128)S(1)} %get-tuple-element.70.turned_ref), custom_call_target="tpu_custom_call" | custom-call | tf_op jit(solution)/shard_map/basis/pallas_call | solution.py:251
  85.9 5.5 %all-to-all-done = f32[32,8,128]{2,1,0:T(8,128)S(1)} async-done(((f32[32,8,128]{2,1,0:T(8,128)}), f32[32,8,128]{2,1,0:T(8,128)S(1)}, u32[]{:S(2)}, u32[]{:S(2)}) %all-to-all-start) | async-done | bytes 131104 | tf_op jit(solution)/shard_map/all_to_all | solution.py:380
  (58 shorter events, 18.1 us)
Async XLA Ops:
  7.0 3.5 %collective-permute-start.3 = (f32[1536,128]{1,0:T(8,128)S(1)}, f32[1536,128]{1,0:T(8,128)S(1)}, u32[]{:S(2)}, u32[]{:S(2)}) collective-permute-start(f32[1536,128]{1,0:T(8,128)S(1)} %get-tuple-element.49), channel_id=1, source_target_pairs={{0,1},{1,0},{2,3},{3,2},{4,5},{5,4},{6,7},{7,6},{8,9},{9,8},{10,11... | collective-permute-start | bytes 2359304 | tf_op jit(solution)/shard_map/ppermute | solution.py:23
  7.4 3.6 %collective-permute-start.4 = (f32[1536,128]{1,0:T(8,128)S(1)}, f32[1536,128]{1,0:T(8,128)S(1)}, u32[]{:S(2)}, u32[]{:S(2)}) collective-permute-start(f32[1536,128]{1,0:T(8,128)S(1)} %get-tuple-element.51), channel_id=1, source_target_pairs={{0,1},{1,0},{2,3},{3,2},{4,5},{5,4},{6,7},{7,6},{8,9},{9,8},{10,11... | collective-permute-start | bytes 2359304 | tf_op jit(solution)/shard_map/ppermute | solution.py:23
  7.6 15.6 %collective-permute-start.2 = (f32[1536,128]{1,0:T(8,128)S(1)}, f32[1536,128]{1,0:T(8,128)S(1)}, u32[]{:S(2)}, u32[]{:S(2)}) collective-permute-start(f32[1536,128]{1,0:T(8,128)S(1)} %get-tuple-element.47), channel_id=1, source_target_pairs={{0,1},{1,0},{2,3},{3,2},{4,5},{5,4},{6,7},{7,6},{8,9},{9,8},{10,11... | collective-permute-start | bytes 2359304 | tf_op jit(solution)/shard_map/ppermute | solution.py:23
  7.9 11.7 %collective-permute-start.7 = (f32[768,128]{1,0:T(8,128)S(1)}, f32[768,128]{1,0:T(8,128)S(1)}, u32[]{:S(2)}, u32[]{:S(2)}) collective-permute-start(f32[768,128]{1,0:T(8,128)S(1)} %term.7), channel_id=1, source_target_pairs={{0,2},{2,4},{4,6},{6,0},{1,3},{3,5},{5,7},{7,1},{8,10},{10,12},{12... | collective-permute-start | bytes 1179656 | tf_op jit(solution)/shard_map/ppermute | solution.py:23
  9.2 10.4 %collective-permute-start.8 = (f32[768,128]{1,0:T(8,128)S(1)}, f32[768,128]{1,0:T(8,128)S(1)}, u32[]{:S(2)}, u32[]{:S(2)}) collective-permute-start(f32[768,128]{1,0:T(8,128)S(1)} %term.8), channel_id=1, source_target_pairs={{0,6},{2,0},{4,2},{6,4},{1,7},{3,1},{5,3},{7,5},{8,14},{10,8},{12,... | collective-permute-start | bytes 1179656 | tf_op jit(solution)/shard_map/ppermute | solution.py:23
  11.4 16.4 %collective-permute-start.5 = (f32[768,128]{1,0:T(8,128)S(1)}, f32[768,128]{1,0:T(8,128)S(1)}, u32[]{:S(2)}, u32[]{:S(2)}) collective-permute-start(f32[768,128]{1,0:T(8,128)S(1)} %term.10), channel_id=1, source_target_pairs={{0,6},{2,0},{4,2},{6,4},{1,7},{3,1},{5,3},{7,5},{8,14},{10,8},{12,... | collective-permute-start | bytes 1179656 | tf_op jit(solution)/shard_map/ppermute | solution.py:23
  13.5 14.5 %collective-permute-start.6 = (f32[768,128]{1,0:T(8,128)S(1)}, f32[768,128]{1,0:T(8,128)S(1)}, u32[]{:S(2)}, u32[]{:S(2)}) collective-permute-start(f32[768,128]{1,0:T(8,128)S(1)} %term.9), channel_id=1, source_target_pairs={{0,2},{2,4},{4,6},{6,0},{1,3},{3,5},{5,7},{7,1},{8,10},{10,12},{12... | collective-permute-start | bytes 1179656 | tf_op jit(solution)/shard_map/ppermute | solution.py:23
  20.0 16.5 %collective-permute-start.9 = (f32[768,128]{1,0:T(8,128)S(1)}, f32[768,128]{1,0:T(8,128)S(1)}, u32[]{:S(2)}, u32[]{:S(2)}) collective-permute-start(f32[768,128]{1,0:T(8,128)S(1)} %term.12), channel_id=1, source_target_pairs={{0,2},{2,4},{4,6},{6,0},{1,3},{3,5},{5,7},{7,1},{8,10},{10,12},{12... | collective-permute-start | bytes 1179656 | tf_op jit(solution)/shard_map/ppermute | solution.py:23
  21.4 15.0 %collective-permute-start.10 = (f32[768,128]{1,0:T(8,128)S(1)}, f32[768,128]{1,0:T(8,128)S(1)}, u32[]{:S(2)}, u32[]{:S(2)}) collective-permute-start(f32[768,128]{1,0:T(8,128)S(1)} %term.13), channel_id=1, source_target_pairs={{0,6},{2,0},{4,2},{6,4},{1,7},{3,1},{5,3},{7,5},{8,14},{10,8},{12,... | collective-permute-start | bytes 1179656 | tf_op jit(solution)/shard_map/ppermute | solution.py:23
  36.7 27.0 %collective-permute-start.19 = (f32[2,128,768]{2,1,0:T(8,128)S(1)}, f32[2,128,768]{2,1,0:T(8,128)S(1)}, u32[]{:S(2)}, u32[]{:S(2)}) collective-permute-start(f32[2,128,768]{2,1,0:T(8,128)S(1)} %get-tuple-element.63.turned_ref.refs_0_), channel_id=1, source_target_pairs={{0,6},{2,0},{4,2},{6,4},{1,7},{3,1},{5,3},{7,5},{8,14},{10,8},{12,... | collective-permute-start | bytes 2359304 | tf_op jit(solution)/shard_map/ppermute | solution.py:23
  39.2 24.6 %collective-permute-start.18 = (f32[2,128,768]{2,1,0:T(8,128)S(1)}, f32[2,128,768]{2,1,0:T(8,128)S(1)}, u32[]{:S(2)}, u32[]{:S(2)}) collective-permute-start(f32[2,128,768]{2,1,0:T(8,128)S(1)} %get-tuple-element.63.turned_ref.refs_0_), channel_id=1, source_target_pairs={{0,2},{2,4},{4,6},{6,0},{1,3},{3,5},{5,7},{7,1},{8,10},{10,12},{12... | collective-permute-start | bytes 2359304 | tf_op jit(solution)/shard_map/ppermute | solution.py:23
  42.6 4.5 %collective-permute-start.14 = (f32[64,128]{1,0:T(8,128)S(1)}, f32[64,128]{1,0:T(8,128)S(1)}, u32[]{:S(2)}, u32[]{:S(2)}) collective-permute-start(f32[64,128]{1,0:T(8,128)S(1)} %add.30), channel_id=1, source_target_pairs={{0,64},{32,96},{64,0},{96,32},{1,65},{33,97},{65,1},{97,33},{2,66}... | collective-permute-start | bytes 98312 | tf_op jit(solution)/shard_map/ppermute | solution.py:23
  45.6 3.1 %collective-permute-start.13 = (f32[64,128]{1,0:T(8,128)S(1)}, f32[64,128]{1,0:T(8,128)S(1)}, u32[]{:S(2)}, u32[]{:S(2)}) collective-permute-start(f32[64,128]{1,0:T(8,128)S(1)} %add.30), channel_id=1, source_target_pairs={{0,96},{32,0},{64,32},{96,64},{1,97},{33,1},{65,33},{97,65},{2,98}... | collective-permute-start | bytes 98312 | tf_op jit(solution)/shard_map/ppermute | solution.py:23
  46.4 4.3 %collective-permute-start.12 = (f32[64,128]{1,0:T(8,128)S(1)}, f32[64,128]{1,0:T(8,128)S(1)}, u32[]{:S(2)}, u32[]{:S(2)}) collective-permute-start(f32[64,128]{1,0:T(8,128)S(1)} %add.30), channel_id=1, source_target_pairs={{0,32},{32,64},{64,96},{96,0},{1,33},{33,65},{65,97},{97,1},{2,34}... | collective-permute-start | bytes 98312 | tf_op jit(solution)/shard_map/ppermute | solution.py:23
  50.6 5.1 %collective-permute-start.17 = (f32[64,128]{1,0:T(8,128)S(1)}, f32[64,128]{1,0:T(8,128)S(1)}, u32[]{:S(2)}, u32[]{:S(2)}) collective-permute-start(f32[64,128]{1,0:T(8,128)S(1)} %add_add_fusion.2), channel_id=1, source_target_pairs={{0,16},{8,24},{16,0},{24,8},{1,17},{9,25},{17,1},{25,9},{2,18},{10... | collective-permute-start | bytes 98312 | tf_op jit(solution)/shard_map/ppermute | solution.py:23
  54.3 3.1 %collective-permute-start.16 = (f32[64,128]{1,0:T(8,128)S(1)}, f32[64,128]{1,0:T(8,128)S(1)}, u32[]{:S(2)}, u32[]{:S(2)}) collective-permute-start(f32[64,128]{1,0:T(8,128)S(1)} %add_add_fusion.2), channel_id=1, source_target_pairs={{0,24},{8,0},{16,8},{24,16},{1,25},{9,1},{17,9},{25,17},{2,26},{10... | collective-permute-start | bytes 98312 | tf_op jit(solution)/shard_map/ppermute | solution.py:23
  54.8 4.3 %collective-permute-start.15 = (f32[64,128]{1,0:T(8,128)S(1)}, f32[64,128]{1,0:T(8,128)S(1)}, u32[]{:S(2)}, u32[]{:S(2)}) collective-permute-start(f32[64,128]{1,0:T(8,128)S(1)} %add_add_fusion.2), channel_id=1, source_target_pairs={{0,8},{8,16},{16,24},{24,0},{1,9},{9,17},{17,25},{25,1},{2,10},{10... | collective-permute-start | bytes 98312 | tf_op jit(solution)/shard_map/ppermute | solution.py:23
  59.0 8.8 %collective-permute-start.22 = (f32[64,128]{1,0:T(8,128)S(1)}, f32[64,128]{1,0:T(8,128)S(1)}, u32[]{:S(2)}, u32[]{:S(2)}) collective-permute-start(f32[64,128]{1,0:T(8,128)S(1)} %add_add_fusion.1), channel_id=1, source_target_pairs={{0,6},{2,0},{4,2},{6,4},{1,7},{3,1},{5,3},{7,5},{8,14},{10,8},{12,... | collective-permute-start | bytes 98312 | tf_op jit(solution)/shard_map/ppermute | solution.py:23
  61.8 6.1 %collective-permute-start.21 = (f32[64,128]{1,0:T(8,128)S(1)}, f32[64,128]{1,0:T(8,128)S(1)}, u32[]{:S(2)}, u32[]{:S(2)}) collective-permute-start(f32[64,128]{1,0:T(8,128)S(1)} %add_add_fusion.1), channel_id=1, source_target_pairs={{0,2},{2,4},{4,6},{6,0},{1,3},{3,5},{5,7},{7,1},{8,10},{10,12},{12... | collective-permute-start | bytes 98312 | tf_op jit(solution)/shard_map/ppermute | solution.py:23
  61.8 6.1 %collective-permute-start.20 = (f32[64,128]{1,0:T(8,128)S(1)}, f32[64,128]{1,0:T(8,128)S(1)}, u32[]{:S(2)}, u32[]{:S(2)}) collective-permute-start(f32[64,128]{1,0:T(8,128)S(1)} %add_add_fusion.1), channel_id=1, source_target_pairs={{0,4},{2,6},{4,0},{6,2},{1,5},{3,7},{5,1},{7,3},{8,12},{10,14},{12... | collective-permute-start | bytes 98312 | tf_op jit(solution)/shard_map/ppermute | solution.py:23
  63.8 13.5 %collective-permute-start.25 = (f32[1,128,768]{2,1,0:T(8,128)S(1)}, f32[1,128,768]{2,1,0:T(8,128)S(1)}, u32[]{:S(2)}, u32[]{:S(2)}) collective-permute-start(f32[1,128,768]{2,1,0:T(8,128)S(1)} %slice.7), channel_id=1, source_target_pairs={{0,2},{2,4},{4,6},{6,0},{1,3},{3,5},{5,7},{7,1},{8,10},{10,12},{12... | collective-permute-start | bytes 1179656 | tf_op jit(solution)/shard_map/ppermute | solution.py:23
  65.9 11.4 %collective-permute-start.24 = (f32[1,128,768]{2,1,0:T(8,128)S(1)}, f32[1,128,768]{2,1,0:T(8,128)S(1)}, u32[]{:S(2)}, u32[]{:S(2)}) collective-permute-start(f32[1,128,768]{2,1,0:T(8,128)S(1)} %slice.6), channel_id=1, source_target_pairs={{0,6},{2,0},{4,2},{6,4},{1,7},{3,1},{5,3},{7,5},{8,14},{10,8},{12,... | collective-permute-start | bytes 1179656 | tf_op jit(solution)/shard_map/ppermute | solution.py:23
  67.9 5.5 %collective-permute-start.23 = (f32[64,128]{1,0:T(8,128)S(1)}, f32[64,128]{1,0:T(8,128)S(1)}, u32[]{:S(2)}, u32[]{:S(2)}) collective-permute-start(f32[64,128]{1,0:T(8,128)S(1)} %add_add_fusion.mine_ref), channel_id=1, source_target_pairs={{0,1},{1,0},{2,3},{3,2},{4,5},{5,4},{6,7},{7,6},{8,9},{9,8},{10,11... | collective-permute-start | bytes 98312 | tf_op jit(solution)/shard_map/ppermute | solution.py:23
  79.1 12.3 %all-to-all-start = ((f32[32,8,128]{2,1,0:T(8,128)}), f32[32,8,128]{2,1,0:T(8,128)S(1)}, u32[]{:S(2)}, u32[]{:S(2)}) async-start(f32[32,8,128]{2,1,0:T(8,128)} %bitcast), calls=%async_computation | async-start | bytes 262144 | tf_op jit(solution)/shard_map/all_to_all | solution.py:380
  (5 other events, 35.6 us)

commit v5 on v4

--- a/solution.py
+++ b/solution.py
@@ -318,6 +318,26 @@
     )(*args)
 
 
+def total_body(parts_ref, out_ref):
+    rows = out_ref.shape[0]
+    total = parts_ref[:rows, :]
+    for at in range(rows, parts_ref.shape[0], rows):
+        total = total + parts_ref[at : at + rows, :]
+    out_ref[...] = total
+
+
+def total_of(parts, rows):
+    return pl.pallas_call(
+        total_body,
+        out_shape=jax.ShapeDtypeStruct((rows, parts.shape[1]), F32),
+        in_specs=[WHOLE],
+        out_specs=WHOLE,
+        compiler_params=PARAMS,
+        cost_estimate=COST,
+        name="total",
+    )(parts)
+
+
 def shards(panel, test_matrix, prior_sketch):
     rows, rank = prior_sketch.shape
     half = rows // 2
@@ -357,18 +377,16 @@
     keep, give = gather(gram_of(own, turned))
     gram = keep + swap(give)
     gram = axis_sum(axis_sum(gram, "y"), "z")
-    gram, turned = lax.optimization_barrier((gram, turned))
-    acc = weigh([turned], [here], [(0, 0, 0, 0), (0, 1, 0, 1)])
     across = [shift(gram, "x", by) for by in (2, 1, 3)]
-
-    acc, from_left, from_right = lax.optimization_barrier((acc, from_left, from_right))
+    gram, from_left, from_right, turned = lax.optimization_barrier(
+        (gram, from_left, from_right, turned)
+    )
     far_bot = shift(from_left[1:], "x", 1)
     far_top = shift(from_right[:1], "x", 3)
     acc = weigh(
-        [from_left, from_right],
-        [left, right],
-        [(0, 0, 0, 0), (0, 1, 0, 1), (1, 0, 1, 0), (1, 1, 1, 1)],
-        acc,
+        [turned, from_left, from_right],
+        [here, left, right],
+        [(source, part, source, part) for source in range(3) for part in range(2)],
     )
     acc, across = lax.optimization_barrier((acc, across))
     gram = gram + across[0] + across[1] + across[2]
@@ -378,7 +396,7 @@
     far_top, far_bot, inverse = lax.optimization_barrier((far_top, far_bot, inverse))
     weights = weigh([far_top, far_bot], [far], [(0, 0, 0, 0), (1, 0, 0, 1)], acc, inverse)
     parts = lax.all_to_all(weights.reshape(2 * rank, -1), ("y", "z", "core"), 0, 0, tiled=True)
-    return basis, jnp.sum(parts.reshape(-1, rank // 16, rank), 0)
+    return basis, total_of(parts, rank // 16)
 
 
 def solution(mesh):

time: 92.2 us -> 90.8 us (0.985)
    pallas_call x3 -> x2, Pallas kernels: 3.73 us -> 3.56 us  [weigh(): pl.pallas_call(functools.partial(weigh_body, plan=plan, block=block, widt...]
where the time goes in v5:
time: 90.8 us; the launch traced here: 90.6 us
  starting transfers between devices  39.1 us (43%)
  waiting for transfers between devices  32.5 us (36%)
  Pallas kernels  18.1 us (20%)
    ppermute x26, starting transfers between devices, shift(): return lax.ppermute(block, axis, [(i, (i + by) % n) for i in range(n)])  35.1 us
    ppermute x26, waiting for transfers between devices, shift(): return lax.ppermute(block, axis, [(i, (i + by) % n) for i in range(n)])  27 us
    all_to_all x1, waiting for transfers between devices, shards(): lax.all_to_all(weights.reshape(2 * rank, -1), ('y', 'z', 'core'), 0, 0, t...  5.5 us
    all_to_all x1, starting transfers between devices, shards(): lax.all_to_all(weights.reshape(2 * rank, -1), ('y', 'z', 'core'), 0, 0, t...  3.95 us
    pallas_call x1, Pallas kernels, factor_inverse(): pl.pallas_call(functools.partial(factor_body, scale=scale), out_shape=(ou...  3.87 us
    pallas_call x2, Pallas kernels, fetch(): pl.pallas_call(functools.partial(fetch_body, plan=plan), out_shape=[pltpu...  3.76 us
    pallas_call x2, Pallas kernels, weigh(): pl.pallas_call(functools.partial(weigh_body, plan=plan, block=block, widt...  3.56 us
    pallas_call x7, Pallas kernels, term(): pl.pallas_call(functools.partial(term_body, first=first, sizes=sizes, blo...  2.85 us
  transfers between devices with their start and end apart: 27, of which 11 were waited for; matrix products, arithmetic and copies ran while one was open for 0% of the time, Pallas kernels for 16%

profile of v5, /device:TPU:1, one launch (start us, length us, event | category | flops | bytes accessed | tf_op | source)
XLA Modules:
  0.0 90.6 jit_solution(17051281479706721214)
XLA Ops:
  0.6 1.5 %collective-permute-start = (f32[128,128]{1,0:T(8,128)}, f32[128,128]{1,0:T(8,128)S(1)}, u32[]{:S(2)}, u32[]{:S(2)}) collective-permute-start(f32[128,128]{1,0:T(8,128)} %test_ref.13), channel_id=1, source_target_pairs={{0,1},{1,0},{2,3},{3,2},{4,5},{5,4},{6,7},{7,6},{8,9},{9,8},{10,11... | collective-permute-start | bytes 196616 | tf_op jit(solution)/shard_map/ppermute | solution.py:23
  3.6 2.6 %fetch.3 = (f32[1536,128]{1,0:T(8,128)S(1)}, f32[1536,128]{1,0:T(8,128)S(1)}, f32[1536,128]{1,0:T(8,128)S(1)}, f32[1536,128]{1,0:T(8,128)S(1)}, f32[1536,128]{1,...) custom-call(f32[12288,128]{1,0:T(8,128)} %panel_ref.2), custom_call_target="tpu_custom_call" | custom-call | tf_op jit(solution)/shard_map/fetch/pallas_call | solution.py:65
  9.2 1.4 %collective-permute-start.8 = (f32[768,128]{1,0:T(8,128)S(1)}, f32[768,128]{1,0:T(8,128)S(1)}, u32[]{:S(2)}, u32[]{:S(2)}) collective-permute-start(f32[768,128]{1,0:T(8,128)S(1)} %term.8), channel_id=1, source_target_pairs={{0,6},{2,0},{4,2},{6,4},{1,7},{3,1},{5,3},{7,5},{8,14},{10,8},{12,... | collective-permute-start | bytes 1179656 | tf_op jit(solution)/shard_map/ppermute | solution.py:23
  11.4 2.2 %collective-permute-start.5 = (f32[768,128]{1,0:T(8,128)S(1)}, f32[768,128]{1,0:T(8,128)S(1)}, u32[]{:S(2)}, u32[]{:S(2)}) collective-permute-start(f32[768,128]{1,0:T(8,128)S(1)} %term.10), channel_id=1, source_target_pairs={{0,6},{2,0},{4,2},{6,4},{1,7},{3,1},{5,3},{7,5},{8,14},{10,8},{12,... | collective-permute-start | bytes 1179656 | tf_op jit(solution)/shard_map/ppermute | solution.py:23
  13.5 6.1 %collective-permute-done.7.rest_0_ = f32[768,128]{1,0:T(8,128)S(1)} collective-permute-done((f32[768,128]{1,0:T(8,128)S(1)}, f32[768,128]{1,0:T(8,128)S(1)}, u32[]{:S(2)}, u32[]{:S(2)}) %collective-permute-start.7) | collective-permute-done | bytes 393248 | tf_op jit(solution)/shard_map/ppermute | solution.py:23
  21.4 1.8 %collective-permute-start.10 = (f32[768,128]{1,0:T(8,128)S(1)}, f32[768,128]{1,0:T(8,128)S(1)}, u32[]{:S(2)}, u32[]{:S(2)}) collective-permute-start(f32[768,128]{1,0:T(8,128)S(1)} %term.13), channel_id=1, source_target_pairs={{0,6},{2,0},{4,2},{6,4},{1,7},{3,1},{5,3},{7,5},{8,14},{10,8},{12,... | collective-permute-start | bytes 1179656 | tf_op jit(solution)/shard_map/ppermute | solution.py:23
  23.2 4.6 %collective-permute-done.5.rest_1_ = f32[768,128]{1,0:T(8,128)S(1)} collective-permute-done((f32[768,128]{1,0:T(8,128)S(1)}, f32[768,128]{1,0:T(8,128)S(1)}, u32[]{:S(2)}, u32[]{:S(2)}) %collective-permute-start.5) | collective-permute-done | bytes 393248 | tf_op jit(solution)/shard_map/ppermute | solution.py:23
  28.6 7.8 %collective-permute-done.9.top_ref = f32[768,128]{1,0:T(8,128)S(1)} collective-permute-done((f32[768,128]{1,0:T(8,128)S(1)}, f32[768,128]{1,0:T(8,128)S(1)}, u32[]{:S(2)}, u32[]{:S(2)}) %collective-permute-start.9) | collective-permute-done | bytes 393248 | tf_op jit(solution)/shard_map/ppermute | solution.py:23
  37.8 1.7 %collective-permute-start.19 = (f32[2,128,768]{2,1,0:T(8,128)S(1)}, f32[2,128,768]{2,1,0:T(8,128)S(1)}, u32[]{:S(2)}, u32[]{:S(2)}) collective-permute-start(f32[2,128,768]{2,1,0:T(8,128)S(1)} %get-tuple-element.62.turned_ref.refs_0_), channel_id=1, source_target_pairs={{0,6},{2,0},{4,2},{6,4},{1,7},{3,1},{5,3},{7,5},{8,14},{10,8},{12,... | collective-permute-start | bytes 2359304 | tf_op jit(solution)/shard_map/ppermute | solution.py:23
  40.3 1.8 %collective-permute-start.11 = (f32[64,128]{1,0:T(8,128)S(1)}, f32[64,128]{1,0:T(8,128)S(1)}, u32[]{:S(2)}, u32[]{:S(2)}) collective-permute-start(f32[64,128]{1,0:T(8,128)S(1)} %get-tuple-element.60), channel_id=1, source_target_pairs={{0,1},{1,0},{2,3},{3,2},{4,5},{5,4},{6,7},{7,6},{8,9},{9,8},{10,11... | collective-permute-start | bytes 98312 | tf_op jit(solution)/shard_map/ppermute | solution.py:23
  42.9 2.9 %collective-permute-start.14 = (f32[64,128]{1,0:T(8,128)S(1)}, f32[64,128]{1,0:T(8,128)S(1)}, u32[]{:S(2)}, u32[]{:S(2)}) collective-permute-start(f32[64,128]{1,0:T(8,128)S(1)} %add.30), channel_id=1, source_target_pairs={{0,64},{32,96},{64,0},{96,32},{1,65},{33,97},{65,1},{97,33},{2,66}... | collective-permute-start | bytes 98312 | tf_op jit(solution)/shard_map/ppermute | solution.py:23
  47.3 1.7 %collective-permute-done.13 = f32[64,128]{1,0:T(8,128)S(1)} collective-permute-done((f32[64,128]{1,0:T(8,128)S(1)}, f32[64,128]{1,0:T(8,128)S(1)}, u32[]{:S(2)}, u32[]{:S(2)}) %collective-permute-start.13) | collective-permute-done | bytes 32800 | tf_op jit(solution)/shard_map/ppermute | solution.py:23
  49.0 1.9 %collective-permute-done.12 = f32[64,128]{1,0:T(8,128)S(1)} collective-permute-done((f32[64,128]{1,0:T(8,128)S(1)}, f32[64,128]{1,0:T(8,128)S(1)}, u32[]{:S(2)}, u32[]{:S(2)}) %collective-permute-start.12) | collective-permute-done | bytes 32800 | tf_op jit(solution)/shard_map/ppermute | solution.py:23
  50.9 3.7 %collective-permute-start.17 = (f32[64,128]{1,0:T(8,128)S(1)}, f32[64,128]{1,0:T(8,128)S(1)}, u32[]{:S(2)}, u32[]{:S(2)}) collective-permute-start(f32[64,128]{1,0:T(8,128)S(1)} %add_add_fusion.2), channel_id=1, source_target_pairs={{0,16},{8,24},{16,0},{24,8},{1,17},{9,25},{17,1},{25,9},{2,18},{10... | collective-permute-start | bytes 98312 | tf_op jit(solution)/shard_map/ppermute | solution.py:23
  56.1 1.6 %collective-permute-done.16 = f32[64,128]{1,0:T(8,128)S(1)} collective-permute-done((f32[64,128]{1,0:T(8,128)S(1)}, f32[64,128]{1,0:T(8,128)S(1)}, u32[]{:S(2)}, u32[]{:S(2)}) %collective-permute-start.16) | collective-permute-done | bytes 32800 | tf_op jit(solution)/shard_map/ppermute | solution.py:23
  61.1 1.6 %collective-permute-start.22 = (f32[64,128]{1,0:T(8,128)S(1)}, f32[64,128]{1,0:T(8,128)S(1)}, u32[]{:S(2)}, u32[]{:S(2)}) collective-permute-start(f32[64,128]{1,0:T(8,128)S(1)} %add_add_fusion.1), channel_id=1, source_target_pairs={{0,6},{2,0},{4,2},{6,4},{1,7},{3,1},{5,3},{7,5},{8,14},{10,8},{12,... | collective-permute-start | bytes 98312 | tf_op jit(solution)/shard_map/ppermute | solution.py:23
  62.9 1.7 %collective-permute-start.25 = (f32[1,128,768]{2,1,0:T(8,128)S(1)}, f32[1,128,768]{2,1,0:T(8,128)S(1)}, u32[]{:S(2)}, u32[]{:S(2)}) collective-permute-start(f32[1,128,768]{2,1,0:T(8,128)S(1)} %slice.7), channel_id=1, source_target_pairs={{0,2},{2,4},{4,6},{6,0},{1,3},{3,5},{5,7},{7,1},{8,10},{10,12},{12... | collective-permute-start | bytes 1179656 | tf_op jit(solution)/shard_map/ppermute | solution.py:23
  64.6 1.8 %weigh.2.refs_4_ = f32[128,256]{1,0:T(8,128)S(1)} custom-call(f32[2,128,768]{2,1,0:T(8,128)S(1)} %get-tuple-element.62.turned_ref.refs_0_, f32[2,128,768]{2,1,0:T(8,128)S(1)} %collective-permute-done.18.refs_1_, f32[2,128,768]{2,1,0:T(8,128)S(1)} %collective-permute-done.19.refs_2_, f32[1536,128]{1,0:T(8,128)S(1)} %get-tuple-element.39.mine_ref.refs_3_, ...), custom_call_target="tpu_custom_call" | custom-call | tf_op jit(solution)/shard_map/weigh/pallas_call | solution.py:310
  66.5 5.2 %collective-permute-start.23 = (f32[64,128]{1,0:T(8,128)S(1)}, f32[64,128]{1,0:T(8,128)S(1)}, u32[]{:S(2)}, u32[]{:S(2)}) collective-permute-start(f32[64,128]{1,0:T(8,128)S(1)} %add_add_fusion.mine_ref), channel_id=1, source_target_pairs={{0,1},{1,0},{2,3},{3,2},{4,5},{5,4},{6,7},{7,6},{8,9},{9,8},{10,11... | collective-permute-start | bytes 98312 | tf_op jit(solution)/shard_map/ppermute | solution.py:23
  72.6 3.9 %factor.1 = (f32[128,128]{1,0:T(8,128)S(1)}, f32[128,128]{1,0:T(8,128)S(1)}) custom-call(f32[64,128]{1,0:T(8,128)S(1)} %add_add_fusion.mine_ref, f32[64,128]{1,0:T(8,128)S(1)} %collective-permute-done.23.other_ref), custom_call_target="tpu_custom_call" | custom-call | flops 1300000000 | tf_op jit(solution)/shard_map/factor/pallas_call | solution.py:231
  76.5 1.8 %weigh.3 = f32[16,2,8,128]{3,2,1,0:T(8,128)} custom-call(f32[1,128,768]{2,1,0:T(8,128)S(1)} %collective-permute-done.24.refs_0_, f32[1,128,768]{2,1,0:T(8,128)S(1)} %collective-permute-done.25.refs_1_, f32[1536,128]{1,0:T(8,128)S(1)} %get-tuple-element.40.mine_ref.refs_2_, f32[1536,128]{1,0:T(8,128)S(1)} %collective-permute-done.1.other_ref.refs_3_, ...), custom_call_target="tpu_custom_call" | custom-call | tf_op jit(solution)/shard_map/weigh/pallas_call | solution.py:310
  78.2 4.0 %all-to-all-start = ((f32[32,8,128]{2,1,0:T(8,128)}), f32[32,8,128]{2,1,0:T(8,128)S(1)}, u32[]{:S(2)}, u32[]{:S(2)}) async-start(f32[32,8,128]{2,1,0:T(8,128)} %bitcast), calls=%async_computation | async-start | bytes 262144 | tf_op jit(solution)/shard_map/all_to_all | solution.py:398
  82.2 2.3 %basis.1 = f32[1536,128]{1,0:T(8,128)} custom-call(f32[1536,128]{1,0:T(8,128)S(1)} %get-tuple-element.57.own_ref, f32[128,128]{1,0:T(8,128)S(1)} %get-tuple-element.68.turned_ref), custom_call_target="tpu_custom_call" | custom-call | tf_op jit(solution)/shard_map/basis/pallas_call | solution.py:251
  84.5 5.5 %all-to-all-done = f32[32,8,128]{2,1,0:T(8,128)S(1)} async-done(((f32[32,8,128]{2,1,0:T(8,128)}), f32[32,8,128]{2,1,0:T(8,128)S(1)}, u32[]{:S(2)}, u32[]{:S(2)}) %all-to-all-start) | async-done | bytes 131104 | tf_op jit(solution)/shard_map/all_to_all | solution.py:398
  (57 shorter events, 18.8 us)
Async XLA Ops:
  7.0 3.5 %collective-permute-start.3 = (f32[1536,128]{1,0:T(8,128)S(1)}, f32[1536,128]{1,0:T(8,128)S(1)}, u32[]{:S(2)}, u32[]{:S(2)}) collective-permute-start(f32[1536,128]{1,0:T(8,128)S(1)} %get-tuple-element.48), channel_id=1, source_target_pairs={{0,1},{1,0},{2,3},{3,2},{4,5},{5,4},{6,7},{7,6},{8,9},{9,8},{10,11... | collective-permute-start | bytes 2359304 | tf_op jit(solution)/shard_map/ppermute | solution.py:23
  7.4 3.6 %collective-permute-start.4 = (f32[1536,128]{1,0:T(8,128)S(1)}, f32[1536,128]{1,0:T(8,128)S(1)}, u32[]{:S(2)}, u32[]{:S(2)}) collective-permute-start(f32[1536,128]{1,0:T(8,128)S(1)} %get-tuple-element.50), channel_id=1, source_target_pairs={{0,1},{1,0},{2,3},{3,2},{4,5},{5,4},{6,7},{7,6},{8,9},{9,8},{10,11... | collective-permute-start | bytes 2359304 | tf_op jit(solution)/shard_map/ppermute | solution.py:23
  7.6 15.6 %collective-permute-start.2 = (f32[1536,128]{1,0:T(8,128)S(1)}, f32[1536,128]{1,0:T(8,128)S(1)}, u32[]{:S(2)}, u32[]{:S(2)}) collective-permute-start(f32[1536,128]{1,0:T(8,128)S(1)} %get-tuple-element.46), channel_id=1, source_target_pairs={{0,1},{1,0},{2,3},{3,2},{4,5},{5,4},{6,7},{7,6},{8,9},{9,8},{10,11... | collective-permute-start | bytes 2359304 | tf_op jit(solution)/shard_map/ppermute | solution.py:23
  7.9 11.7 %collective-permute-start.7 = (f32[768,128]{1,0:T(8,128)S(1)}, f32[768,128]{1,0:T(8,128)S(1)}, u32[]{:S(2)}, u32[]{:S(2)}) collective-permute-start(f32[768,128]{1,0:T(8,128)S(1)} %term.7), channel_id=1, source_target_pairs={{0,2},{2,4},{4,6},{6,0},{1,3},{3,5},{5,7},{7,1},{8,10},{10,12},{12... | collective-permute-start | bytes 1179656 | tf_op jit(solution)/shard_map/ppermute | solution.py:23
  9.2 10.4 %collective-permute-start.8 = (f32[768,128]{1,0:T(8,128)S(1)}, f32[768,128]{1,0:T(8,128)S(1)}, u32[]{:S(2)}, u32[]{:S(2)}) collective-permute-start(f32[768,128]{1,0:T(8,128)S(1)} %term.8), channel_id=1, source_target_pairs={{0,6},{2,0},{4,2},{6,4},{1,7},{3,1},{5,3},{7,5},{8,14},{10,8},{12,... | collective-permute-start | bytes 1179656 | tf_op jit(solution)/shard_map/ppermute | solution.py:23
  11.4 16.4 %collective-permute-start.5 = (f32[768,128]{1,0:T(8,128)S(1)}, f32[768,128]{1,0:T(8,128)S(1)}, u32[]{:S(2)}, u32[]{:S(2)}) collective-permute-start(f32[768,128]{1,0:T(8,128)S(1)} %term.10), channel_id=1, source_target_pairs={{0,6},{2,0},{4,2},{6,4},{1,7},{3,1},{5,3},{7,5},{8,14},{10,8},{12,... | collective-permute-start | bytes 1179656 | tf_op jit(solution)/shard_map/ppermute | solution.py:23
  13.5 14.5 %collective-permute-start.6 = (f32[768,128]{1,0:T(8,128)S(1)}, f32[768,128]{1,0:T(8,128)S(1)}, u32[]{:S(2)}, u32[]{:S(2)}) collective-permute-start(f32[768,128]{1,0:T(8,128)S(1)} %term.9), channel_id=1, source_target_pairs={{0,2},{2,4},{4,6},{6,0},{1,3},{3,5},{5,7},{7,1},{8,10},{10,12},{12... | collective-permute-start | bytes 1179656 | tf_op jit(solution)/shard_map/ppermute | solution.py:23
  20.0 16.5 %collective-permute-start.9 = (f32[768,128]{1,0:T(8,128)S(1)}, f32[768,128]{1,0:T(8,128)S(1)}, u32[]{:S(2)}, u32[]{:S(2)}) collective-permute-start(f32[768,128]{1,0:T(8,128)S(1)} %term.12), channel_id=1, source_target_pairs={{0,2},{2,4},{4,6},{6,0},{1,3},{3,5},{5,7},{7,1},{8,10},{10,12},{12... | collective-permute-start | bytes 1179656 | tf_op jit(solution)/shard_map/ppermute | solution.py:23
  21.4 15.0 %collective-permute-start.10 = (f32[768,128]{1,0:T(8,128)S(1)}, f32[768,128]{1,0:T(8,128)S(1)}, u32[]{:S(2)}, u32[]{:S(2)}) collective-permute-start(f32[768,128]{1,0:T(8,128)S(1)} %term.13), channel_id=1, source_target_pairs={{0,6},{2,0},{4,2},{6,4},{1,7},{3,1},{5,3},{7,5},{8,14},{10,8},{12,... | collective-permute-start | bytes 1179656 | tf_op jit(solution)/shard_map/ppermute | solution.py:23
  36.7 26.0 %collective-permute-start.18 = (f32[2,128,768]{2,1,0:T(8,128)S(1)}, f32[2,128,768]{2,1,0:T(8,128)S(1)}, u32[]{:S(2)}, u32[]{:S(2)}) collective-permute-start(f32[2,128,768]{2,1,0:T(8,128)S(1)} %get-tuple-element.62.turned_ref.refs_0_), channel_id=1, source_target_pairs={{0,2},{2,4},{4,6},{6,0},{1,3},{3,5},{5,7},{7,1},{8,10},{10,12},{12... | collective-permute-start | bytes 2359304 | tf_op jit(solution)/shard_map/ppermute | solution.py:23
  37.8 25.0 %collective-permute-start.19 = (f32[2,128,768]{2,1,0:T(8,128)S(1)}, f32[2,128,768]{2,1,0:T(8,128)S(1)}, u32[]{:S(2)}, u32[]{:S(2)}) collective-permute-start(f32[2,128,768]{2,1,0:T(8,128)S(1)} %get-tuple-element.62.turned_ref.refs_0_), channel_id=1, source_target_pairs={{0,6},{2,0},{4,2},{6,4},{1,7},{3,1},{5,3},{7,5},{8,14},{10,8},{12,... | collective-permute-start | bytes 2359304 | tf_op jit(solution)/shard_map/ppermute | solution.py:23
  42.9 4.4 %collective-permute-start.14 = (f32[64,128]{1,0:T(8,128)S(1)}, f32[64,128]{1,0:T(8,128)S(1)}, u32[]{:S(2)}, u32[]{:S(2)}) collective-permute-start(f32[64,128]{1,0:T(8,128)S(1)} %add.30), channel_id=1, source_target_pairs={{0,64},{32,96},{64,0},{96,32},{1,65},{33,97},{65,1},{97,33},{2,66}... | collective-permute-start | bytes 98312 | tf_op jit(solution)/shard_map/ppermute | solution.py:23
  45.9 3.1 %collective-permute-start.13 = (f32[64,128]{1,0:T(8,128)S(1)}, f32[64,128]{1,0:T(8,128)S(1)}, u32[]{:S(2)}, u32[]{:S(2)}) collective-permute-start(f32[64,128]{1,0:T(8,128)S(1)} %add.30), channel_id=1, source_target_pairs={{0,96},{32,0},{64,32},{96,64},{1,97},{33,1},{65,33},{97,65},{2,98}... | collective-permute-start | bytes 98312 | tf_op jit(solution)/shard_map/ppermute | solution.py:23
  46.6 4.3 %collective-permute-start.12 = (f32[64,128]{1,0:T(8,128)S(1)}, f32[64,128]{1,0:T(8,128)S(1)}, u32[]{:S(2)}, u32[]{:S(2)}) collective-permute-start(f32[64,128]{1,0:T(8,128)S(1)} %add.30), channel_id=1, source_target_pairs={{0,32},{32,64},{64,96},{96,0},{1,33},{33,65},{65,97},{97,1},{2,34}... | collective-permute-start | bytes 98312 | tf_op jit(solution)/shard_map/ppermute | solution.py:23
  50.9 5.1 %collective-permute-start.17 = (f32[64,128]{1,0:T(8,128)S(1)}, f32[64,128]{1,0:T(8,128)S(1)}, u32[]{:S(2)}, u32[]{:S(2)}) collective-permute-start(f32[64,128]{1,0:T(8,128)S(1)} %add_add_fusion.2), channel_id=1, source_target_pairs={{0,16},{8,24},{16,0},{24,8},{1,17},{9,25},{17,1},{25,9},{2,18},{10... | collective-permute-start | bytes 98312 | tf_op jit(solution)/shard_map/ppermute | solution.py:23
  54.6 3.1 %collective-permute-start.16 = (f32[64,128]{1,0:T(8,128)S(1)}, f32[64,128]{1,0:T(8,128)S(1)}, u32[]{:S(2)}, u32[]{:S(2)}) collective-permute-start(f32[64,128]{1,0:T(8,128)S(1)} %add_add_fusion.2), channel_id=1, source_target_pairs={{0,24},{8,0},{16,8},{24,16},{1,25},{9,1},{17,9},{25,17},{2,26},{10... | collective-permute-start | bytes 98312 | tf_op jit(solution)/shard_map/ppermute | solution.py:23
  55.0 4.0 %collective-permute-start.15 = (f32[64,128]{1,0:T(8,128)S(1)}, f32[64,128]{1,0:T(8,128)S(1)}, u32[]{:S(2)}, u32[]{:S(2)}) collective-permute-start(f32[64,128]{1,0:T(8,128)S(1)} %add_add_fusion.2), channel_id=1, source_target_pairs={{0,8},{8,16},{16,24},{24,0},{1,9},{9,17},{17,25},{25,1},{2,10},{10... | collective-permute-start | bytes 98312 | tf_op jit(solution)/shard_map/ppermute | solution.py:23
  59.0 7.4 %collective-permute-start.20 = (f32[64,128]{1,0:T(8,128)S(1)}, f32[64,128]{1,0:T(8,128)S(1)}, u32[]{:S(2)}, u32[]{:S(2)}) collective-permute-start(f32[64,128]{1,0:T(8,128)S(1)} %add_add_fusion.1), channel_id=1, source_target_pairs={{0,4},{2,6},{4,0},{6,2},{1,5},{3,7},{5,1},{7,3},{8,12},{10,14},{12... | collective-permute-start | bytes 98312 | tf_op jit(solution)/shard_map/ppermute | solution.py:23
  60.1 6.3 %collective-permute-start.21 = (f32[64,128]{1,0:T(8,128)S(1)}, f32[64,128]{1,0:T(8,128)S(1)}, u32[]{:S(2)}, u32[]{:S(2)}) collective-permute-start(f32[64,128]{1,0:T(8,128)S(1)} %add_add_fusion.1), channel_id=1, source_target_pairs={{0,2},{2,4},{4,6},{6,0},{1,3},{3,5},{5,7},{7,1},{8,10},{10,12},{12... | collective-permute-start | bytes 98312 | tf_op jit(solution)/shard_map/ppermute | solution.py:23
  61.1 5.3 %collective-permute-start.22 = (f32[64,128]{1,0:T(8,128)S(1)}, f32[64,128]{1,0:T(8,128)S(1)}, u32[]{:S(2)}, u32[]{:S(2)}) collective-permute-start(f32[64,128]{1,0:T(8,128)S(1)} %add_add_fusion.1), channel_id=1, source_target_pairs={{0,6},{2,0},{4,2},{6,4},{1,7},{3,1},{5,3},{7,5},{8,14},{10,8},{12,... | collective-permute-start | bytes 98312 | tf_op jit(solution)/shard_map/ppermute | solution.py:23
  62.8 13.6 %collective-permute-start.24 = (f32[1,128,768]{2,1,0:T(8,128)S(1)}, f32[1,128,768]{2,1,0:T(8,128)S(1)}, u32[]{:S(2)}, u32[]{:S(2)}) collective-permute-start(f32[1,128,768]{2,1,0:T(8,128)S(1)} %slice.6), channel_id=1, source_target_pairs={{0,6},{2,0},{4,2},{6,4},{1,7},{3,1},{5,3},{7,5},{8,14},{10,8},{12,... | collective-permute-start | bytes 1179656 | tf_op jit(solution)/shard_map/ppermute | solution.py:23
  62.9 13.5 %collective-permute-start.25 = (f32[1,128,768]{2,1,0:T(8,128)S(1)}, f32[1,128,768]{2,1,0:T(8,128)S(1)}, u32[]{:S(2)}, u32[]{:S(2)}) collective-permute-start(f32[1,128,768]{2,1,0:T(8,128)S(1)} %slice.7), channel_id=1, source_target_pairs={{0,2},{2,4},{4,6},{6,0},{1,3},{3,5},{5,7},{7,1},{8,10},{10,12},{12... | collective-permute-start | bytes 1179656 | tf_op jit(solution)/shard_map/ppermute | solution.py:23
  66.5 6.1 %collective-permute-start.23 = (f32[64,128]{1,0:T(8,128)S(1)}, f32[64,128]{1,0:T(8,128)S(1)}, u32[]{:S(2)}, u32[]{:S(2)}) collective-permute-start(f32[64,128]{1,0:T(8,128)S(1)} %add_add_fusion.mine_ref), channel_id=1, source_target_pairs={{0,1},{1,0},{2,3},{3,2},{4,5},{5,4},{6,7},{7,6},{8,9},{9,8},{10,11... | collective-permute-start | bytes 98312 | tf_op jit(solution)/shard_map/ppermute | solution.py:23
  78.2 11.8 %all-to-all-start = ((f32[32,8,128]{2,1,0:T(8,128)}), f32[32,8,128]{2,1,0:T(8,128)S(1)}, u32[]{:S(2)}, u32[]{:S(2)}) async-start(f32[32,8,128]{2,1,0:T(8,128)} %bitcast), calls=%async_computation | async-start | bytes 262144 | tf_op jit(solution)/shard_map/all_to_all | solution.py:398
  (5 other events, 35.6 us)

commit v6 on v5

--- a/solution.py
+++ b/solution.py
@@ -376,17 +376,18 @@
     from_right = shift(turned, "x", 3)
     keep, give = gather(gram_of(own, turned))
     gram = keep + swap(give)
-    gram = axis_sum(axis_sum(gram, "y"), "z")
+    acc = weigh([turned], [here], [(0, 0, 0, 0), (0, 1, 0, 1)])
+    gram, acc = lax.optimization_barrier((axis_sum(gram, "y"), acc))
+    gram = axis_sum(gram, "z")
     across = [shift(gram, "x", by) for by in (2, 1, 3)]
-    gram, from_left, from_right, turned = lax.optimization_barrier(
-        (gram, from_left, from_right, turned)
-    )
+    gram, from_left, from_right = lax.optimization_barrier((gram, from_left, from_right))
     far_bot = shift(from_left[1:], "x", 1)
     far_top = shift(from_right[:1], "x", 3)
     acc = weigh(
-        [turned, from_left, from_right],
-        [here, left, right],
-        [(source, part, source, part) for source in range(3) for part in range(2)],
+        [from_left, from_right],
+        [left, right],
+        [(source, part, source, part) for source in range(2) for part in range(2)],
+        acc,
     )
     acc, across = lax.optimization_barrier((acc, across))
     gram = gram + across[0] + across[1] + across[2]

time: 90.8 us -> 92 us (1.013)
  starting transfers between devices: 39.1 us -> 40.5 us
    all_to_all x1, starting transfers between devices: 3.95 us -> 5.29 us  [shards(): lax.all_to_all(weights.reshape(2 * rank, -1), ('y', 'z', 'core'), 0, 0, t...]
    pallas_call x2 -> x3, Pallas kernels: 3.56 us -> 3.72 us  [weigh(): pl.pallas_call(functools.partial(weigh_body, plan=plan, block=block, widt...]
where the time goes in v6:
time: 92 us; the launch traced here: 91.8 us
  starting transfers between devices  40.5 us (44%)
  waiting for transfers between devices  32.1 us (35%)
  Pallas kernels  18.2 us (20%)
    ppermute x26, starting transfers between devices, shift(): return lax.ppermute(block, axis, [(i, (i + by) % n) for i in range(n)])  35.2 us
    ppermute x26, waiting for transfers between devices, shift(): return lax.ppermute(block, axis, [(i, (i + by) % n) for i in range(n)])  26.6 us
    all_to_all x1, waiting for transfers between devices, shards(): lax.all_to_all(weights.reshape(2 * rank, -1), ('y', 'z', 'core'), 0, 0, t...  5.5 us
    all_to_all x1, starting transfers between devices, shards(): lax.all_to_all(weights.reshape(2 * rank, -1), ('y', 'z', 'core'), 0, 0, t...  5.29 us
    pallas_call x1, Pallas kernels, factor_inverse(): pl.pallas_call(functools.partial(factor_body, scale=scale), out_shape=(ou...  3.87 us
    pallas_call x2, Pallas kernels, fetch(): pl.pallas_call(functools.partial(fetch_body, plan=plan), out_shape=[pltpu...  3.76 us
    pallas_call x3, Pallas kernels, weigh(): pl.pallas_call(functools.partial(weigh_body, plan=plan, block=block, widt...  3.72 us
    pallas_call x7, Pallas kernels, term(): pl.pallas_call(functools.partial(term_body, first=first, sizes=sizes, blo...  2.85 us
  transfers between devices with their start and end apart: 27, of which 11 were waited for; matrix products, arithmetic and copies ran while one was open for 0% of the time, Pallas kernels for 16%

profile of v6, /device:TPU:1, one launch (start us, length us, event | category | flops | bytes accessed | tf_op | source)
XLA Modules:
  0.0 91.8 jit_solution(7697373023562163036)
XLA Ops:
  0.6 1.5 %collective-permute-start = (f32[128,128]{1,0:T(8,128)}, f32[128,128]{1,0:T(8,128)S(1)}, u32[]{:S(2)}, u32[]{:S(2)}) collective-permute-start(f32[128,128]{1,0:T(8,128)} %test_ref.13), channel_id=1, source_target_pairs={{0,1},{1,0},{2,3},{3,2},{4,5},{5,4},{6,7},{7,6},{8,9},{9,8},{10,11... | collective-permute-start | bytes 196616 | tf_op jit(solution)/shard_map/ppermute | solution.py:23
  3.6 2.6 %fetch.3 = (f32[1536,128]{1,0:T(8,128)S(1)}, f32[1536,128]{1,0:T(8,128)S(1)}, f32[1536,128]{1,0:T(8,128)S(1)}, f32[1536,128]{1,0:T(8,128)S(1)}, f32[1536,128]{1,...) custom-call(f32[12288,128]{1,0:T(8,128)} %panel_ref.2), custom_call_target="tpu_custom_call" | custom-call | tf_op jit(solution)/shard_map/fetch/pallas_call | solution.py:65
  7.9 1.3 %collective-permute-start.7 = (f32[768,128]{1,0:T(8,128)S(1)}, f32[768,128]{1,0:T(8,128)S(1)}, u32[]{:S(2)}, u32[]{:S(2)}) collective-permute-start(f32[768,128]{1,0:T(8,128)S(1)} %term.7), channel_id=1, source_target_pairs={{0,2},{2,4},{4,6},{6,0},{1,3},{3,5},{5,7},{7,1},{8,10},{10,12},{12... | collective-permute-start | bytes 1179656 | tf_op jit(solution)/shard_map/ppermute | solution.py:23
  9.2 1.4 %collective-permute-start.8 = (f32[768,128]{1,0:T(8,128)S(1)}, f32[768,128]{1,0:T(8,128)S(1)}, u32[]{:S(2)}, u32[]{:S(2)}) collective-permute-start(f32[768,128]{1,0:T(8,128)S(1)} %term.8), channel_id=1, source_target_pairs={{0,6},{2,0},{4,2},{6,4},{1,7},{3,1},{5,3},{7,5},{8,14},{10,8},{12,... | collective-permute-start | bytes 1179656 | tf_op jit(solution)/shard_map/ppermute | solution.py:23
  11.4 2.2 %collective-permute-start.5 = (f32[768,128]{1,0:T(8,128)S(1)}, f32[768,128]{1,0:T(8,128)S(1)}, u32[]{:S(2)}, u32[]{:S(2)}) collective-permute-start(f32[768,128]{1,0:T(8,128)S(1)} %term.10), channel_id=1, source_target_pairs={{0,6},{2,0},{4,2},{6,4},{1,7},{3,1},{5,3},{7,5},{8,14},{10,8},{12,... | collective-permute-start | bytes 1179656 | tf_op jit(solution)/shard_map/ppermute | solution.py:23
  13.5 6.1 %collective-permute-done.7.rest_0_ = f32[768,128]{1,0:T(8,128)S(1)} collective-permute-done((f32[768,128]{1,0:T(8,128)S(1)}, f32[768,128]{1,0:T(8,128)S(1)}, u32[]{:S(2)}, u32[]{:S(2)}) %collective-permute-start.7) | collective-permute-done | bytes 393248 | tf_op jit(solution)/shard_map/ppermute | solution.py:23
  21.4 1.8 %collective-permute-start.10 = (f32[768,128]{1,0:T(8,128)S(1)}, f32[768,128]{1,0:T(8,128)S(1)}, u32[]{:S(2)}, u32[]{:S(2)}) collective-permute-start(f32[768,128]{1,0:T(8,128)S(1)} %term.13), channel_id=1, source_target_pairs={{0,6},{2,0},{4,2},{6,4},{1,7},{3,1},{5,3},{7,5},{8,14},{10,8},{12,... | collective-permute-start | bytes 1179656 | tf_op jit(solution)/shard_map/ppermute | solution.py:23
  23.2 4.6 %collective-permute-done.5.rest_1_ = f32[768,128]{1,0:T(8,128)S(1)} collective-permute-done((f32[768,128]{1,0:T(8,128)S(1)}, f32[768,128]{1,0:T(8,128)S(1)}, u32[]{:S(2)}, u32[]{:S(2)}) %collective-permute-start.5) | collective-permute-done | bytes 393248 | tf_op jit(solution)/shard_map/ppermute | solution.py:23
  28.6 7.8 %collective-permute-done.9.top_ref = f32[768,128]{1,0:T(8,128)S(1)} collective-permute-done((f32[768,128]{1,0:T(8,128)S(1)}, f32[768,128]{1,0:T(8,128)S(1)}, u32[]{:S(2)}, u32[]{:S(2)}) %collective-permute-start.9) | collective-permute-done | bytes 393248 | tf_op jit(solution)/shard_map/ppermute | solution.py:23
  36.7 2.4 %collective-permute-start.19 = (f32[2,128,768]{2,1,0:T(8,128)S(1)}, f32[2,128,768]{2,1,0:T(8,128)S(1)}, u32[]{:S(2)}, u32[]{:S(2)}) collective-permute-start(f32[2,128,768]{2,1,0:T(8,128)S(1)} %get-tuple-element.59.turned_ref.refs_0_), channel_id=1, source_target_pairs={{0,6},{2,0},{4,2},{6,4},{1,7},{3,1},{5,3},{7,5},{8,14},{10,8},{12,... | collective-permute-start | bytes 2359304 | tf_op jit(solution)/shard_map/ppermute | solution.py:23
  40.0 1.7 %collective-permute-start.11 = (f32[64,128]{1,0:T(8,128)S(1)}, f32[64,128]{1,0:T(8,128)S(1)}, u32[]{:S(2)}, u32[]{:S(2)}) collective-permute-start(f32[64,128]{1,0:T(8,128)S(1)} %get-tuple-element.61), channel_id=1, source_target_pairs={{0,1},{1,0},{2,3},{3,2},{4,5},{5,4},{6,7},{7,6},{8,9},{9,8},{10,11... | collective-permute-start | bytes 98312 | tf_op jit(solution)/shard_map/ppermute | solution.py:23
  42.6 3.0 %collective-permute-start.14 = (f32[64,128]{1,0:T(8,128)S(1)}, f32[64,128]{1,0:T(8,128)S(1)}, u32[]{:S(2)}, u32[]{:S(2)}) collective-permute-start(f32[64,128]{1,0:T(8,128)S(1)} %add.30), channel_id=1, source_target_pairs={{0,64},{32,96},{64,0},{96,32},{1,65},{33,97},{65,1},{97,33},{2,66}... | collective-permute-start | bytes 98312 | tf_op jit(solution)/shard_map/ppermute | solution.py:23
  48.7 1.9 %collective-permute-done.12 = f32[64,128]{1,0:T(8,128)S(1)} collective-permute-done((f32[64,128]{1,0:T(8,128)S(1)}, f32[64,128]{1,0:T(8,128)S(1)}, u32[]{:S(2)}, u32[]{:S(2)}) %collective-permute-start.12) | collective-permute-done | bytes 32800 | tf_op jit(solution)/shard_map/ppermute | solution.py:23
  50.6 3.7 %collective-permute-start.17 = (f32[64,128]{1,0:T(8,128)S(1)}, f32[64,128]{1,0:T(8,128)S(1)}, u32[]{:S(2)}, u32[]{:S(2)}) collective-permute-start(f32[64,128]{1,0:T(8,128)S(1)} %add_add_fusion.2), channel_id=1, source_target_pairs={{0,16},{8,24},{16,0},{24,8},{1,17},{9,25},{17,1},{25,9},{2,18},{10... | collective-permute-start | bytes 98312 | tf_op jit(solution)/shard_map/ppermute | solution.py:23
  55.8 1.6 %collective-permute-done.16 = f32[64,128]{1,0:T(8,128)S(1)} collective-permute-done((f32[64,128]{1,0:T(8,128)S(1)}, f32[64,128]{1,0:T(8,128)S(1)}, u32[]{:S(2)}, u32[]{:S(2)}) %collective-permute-start.16) | collective-permute-done | bytes 32800 | tf_op jit(solution)/shard_map/ppermute | solution.py:23
  57.4 1.6 %collective-permute-done.15 = f32[64,128]{1,0:T(8,128)S(1)} collective-permute-done((f32[64,128]{1,0:T(8,128)S(1)}, f32[64,128]{1,0:T(8,128)S(1)}, u32[]{:S(2)}, u32[]{:S(2)}) %collective-permute-start.15) | collective-permute-done | bytes 32800 | tf_op jit(solution)/shard_map/ppermute | solution.py:23
  59.0 2.7 %collective-permute-start.22 = (f32[64,128]{1,0:T(8,128)S(1)}, f32[64,128]{1,0:T(8,128)S(1)}, u32[]{:S(2)}, u32[]{:S(2)}) collective-permute-start(f32[64,128]{1,0:T(8,128)S(1)} %add_add_fusion.1), channel_id=1, source_target_pairs={{0,6},{2,0},{4,2},{6,4},{1,7},{3,1},{5,3},{7,5},{8,14},{10,8},{12,... | collective-permute-start | bytes 98312 | tf_op jit(solution)/shard_map/ppermute | solution.py:23
  63.1 1.5 %collective-permute-start.24 = (f32[1,128,768]{2,1,0:T(8,128)S(1)}, f32[1,128,768]{2,1,0:T(8,128)S(1)}, u32[]{:S(2)}, u32[]{:S(2)}) collective-permute-start(f32[1,128,768]{2,1,0:T(8,128)S(1)} %slice.6), channel_id=1, source_target_pairs={{0,6},{2,0},{4,2},{6,4},{1,7},{3,1},{5,3},{7,5},{8,14},{10,8},{12,... | collective-permute-start | bytes 1179656 | tf_op jit(solution)/shard_map/ppermute | solution.py:23
  66.5 4.9 %collective-permute-start.23 = (f32[64,128]{1,0:T(8,128)S(1)}, f32[64,128]{1,0:T(8,128)S(1)}, u32[]{:S(2)}, u32[]{:S(2)}) collective-permute-start(f32[64,128]{1,0:T(8,128)S(1)} %add_add_fusion.mine_ref), channel_id=1, source_target_pairs={{0,1},{1,0},{2,3},{3,2},{4,5},{5,4},{6,7},{7,6},{8,9},{9,8},{10,11... | collective-permute-start | bytes 98312 | tf_op jit(solution)/shard_map/ppermute | solution.py:23
  72.3 3.9 %factor.1 = (f32[128,128]{1,0:T(8,128)S(1)}, f32[128,128]{1,0:T(8,128)S(1)}) custom-call(f32[64,128]{1,0:T(8,128)S(1)} %add_add_fusion.mine_ref, f32[64,128]{1,0:T(8,128)S(1)} %collective-permute-done.23.other_ref), custom_call_target="tpu_custom_call" | custom-call | flops 1300000000 | tf_op jit(solution)/shard_map/factor/pallas_call | solution.py:231
  76.2 1.8 %weigh.5 = f32[16,2,8,128]{3,2,1,0:T(8,128)} custom-call(f32[1,128,768]{2,1,0:T(8,128)S(1)} %collective-permute-done.24.refs_0_, f32[1,128,768]{2,1,0:T(8,128)S(1)} %collective-permute-done.25.refs_1_, f32[1536,128]{1,0:T(8,128)S(1)} %get-tuple-element.41.mine_ref.refs_2_, f32[1536,128]{1,0:T(8,128)S(1)} %collective-permute-done.1.other_ref.refs_3_, ...), custom_call_target="tpu_custom_call" | custom-call | tf_op jit(solution)/shard_map/weigh/pallas_call | solution.py:310
  78.0 5.3 %all-to-all-start = ((f32[32,8,128]{2,1,0:T(8,128)}), f32[32,8,128]{2,1,0:T(8,128)S(1)}, u32[]{:S(2)}, u32[]{:S(2)}) async-start(f32[32,8,128]{2,1,0:T(8,128)} %bitcast), calls=%async_computation | async-start | bytes 262144 | tf_op jit(solution)/shard_map/all_to_all | solution.py:399
  83.3 2.3 %basis.1 = f32[1536,128]{1,0:T(8,128)} custom-call(f32[1536,128]{1,0:T(8,128)S(1)} %get-tuple-element.58.own_ref, f32[128,128]{1,0:T(8,128)S(1)} %get-tuple-element.70.turned_ref), custom_call_target="tpu_custom_call" | custom-call | tf_op jit(solution)/shard_map/basis/pallas_call | solution.py:251
  85.6 5.5 %all-to-all-done = f32[32,8,128]{2,1,0:T(8,128)S(1)} async-done(((f32[32,8,128]{2,1,0:T(8,128)}), f32[32,8,128]{2,1,0:T(8,128)S(1)}, u32[]{:S(2)}, u32[]{:S(2)}) %all-to-all-start) | async-done | bytes 131104 | tf_op jit(solution)/shard_map/all_to_all | solution.py:399
  (58 shorter events, 17.8 us)
Async XLA Ops:
  7.0 3.5 %collective-permute-start.3 = (f32[1536,128]{1,0:T(8,128)S(1)}, f32[1536,128]{1,0:T(8,128)S(1)}, u32[]{:S(2)}, u32[]{:S(2)}) collective-permute-start(f32[1536,128]{1,0:T(8,128)S(1)} %get-tuple-element.49), channel_id=1, source_target_pairs={{0,1},{1,0},{2,3},{3,2},{4,5},{5,4},{6,7},{7,6},{8,9},{9,8},{10,11... | collective-permute-start | bytes 2359304 | tf_op jit(solution)/shard_map/ppermute | solution.py:23
  7.4 3.6 %collective-permute-start.4 = (f32[1536,128]{1,0:T(8,128)S(1)}, f32[1536,128]{1,0:T(8,128)S(1)}, u32[]{:S(2)}, u32[]{:S(2)}) collective-permute-start(f32[1536,128]{1,0:T(8,128)S(1)} %get-tuple-element.51), channel_id=1, source_target_pairs={{0,1},{1,0},{2,3},{3,2},{4,5},{5,4},{6,7},{7,6},{8,9},{9,8},{10,11... | collective-permute-start | bytes 2359304 | tf_op jit(solution)/shard_map/ppermute | solution.py:23
  7.6 15.6 %collective-permute-start.2 = (f32[1536,128]{1,0:T(8,128)S(1)}, f32[1536,128]{1,0:T(8,128)S(1)}, u32[]{:S(2)}, u32[]{:S(2)}) collective-permute-start(f32[1536,128]{1,0:T(8,128)S(1)} %get-tuple-element.47), channel_id=1, source_target_pairs={{0,1},{1,0},{2,3},{3,2},{4,5},{5,4},{6,7},{7,6},{8,9},{9,8},{10,11... | collective-permute-start | bytes 2359304 | tf_op jit(solution)/shard_map/ppermute | solution.py:23
  7.9 11.7 %collective-permute-start.7 = (f32[768,128]{1,0:T(8,128)S(1)}, f32[768,128]{1,0:T(8,128)S(1)}, u32[]{:S(2)}, u32[]{:S(2)}) collective-permute-start(f32[768,128]{1,0:T(8,128)S(1)} %term.7), channel_id=1, source_target_pairs={{0,2},{2,4},{4,6},{6,0},{1,3},{3,5},{5,7},{7,1},{8,10},{10,12},{12... | collective-permute-start | bytes 1179656 | tf_op jit(solution)/shard_map/ppermute | solution.py:23
  9.2 10.4 %collective-permute-start.8 = (f32[768,128]{1,0:T(8,128)S(1)}, f32[768,128]{1,0:T(8,128)S(1)}, u32[]{:S(2)}, u32[]{:S(2)}) collective-permute-start(f32[768,128]{1,0:T(8,128)S(1)} %term.8), channel_id=1, source_target_pairs={{0,6},{2,0},{4,2},{6,4},{1,7},{3,1},{5,3},{7,5},{8,14},{10,8},{12,... | collective-permute-start | bytes 1179656 | tf_op jit(solution)/shard_map/ppermute | solution.py:23
  11.4 16.4 %collective-permute-start.5 = (f32[768,128]{1,0:T(8,128)S(1)}, f32[768,128]{1,0:T(8,128)S(1)}, u32[]{:S(2)}, u32[]{:S(2)}) collective-permute-start(f32[768,128]{1,0:T(8,128)S(1)} %term.10), channel_id=1, source_target_pairs={{0,6},{2,0},{4,2},{6,4},{1,7},{3,1},{5,3},{7,5},{8,14},{10,8},{12,... | collective-permute-start | bytes 1179656 | tf_op jit(solution)/shard_map/ppermute | solution.py:23
  13.5 14.5 %collective-permute-start.6 = (f32[768,128]{1,0:T(8,128)S(1)}, f32[768,128]{1,0:T(8,128)S(1)}, u32[]{:S(2)}, u32[]{:S(2)}) collective-permute-start(f32[768,128]{1,0:T(8,128)S(1)} %term.9), channel_id=1, source_target_pairs={{0,2},{2,4},{4,6},{6,0},{1,3},{3,5},{5,7},{7,1},{8,10},{10,12},{12... | collective-permute-start | bytes 1179656 | tf_op jit(solution)/shard_map/ppermute | solution.py:23
  20.0 16.5 %collective-permute-start.9 = (f32[768,128]{1,0:T(8,128)S(1)}, f32[768,128]{1,0:T(8,128)S(1)}, u32[]{:S(2)}, u32[]{:S(2)}) collective-permute-start(f32[768,128]{1,0:T(8,128)S(1)} %term.12), channel_id=1, source_target_pairs={{0,2},{2,4},{4,6},{6,0},{1,3},{3,5},{5,7},{7,1},{8,10},{10,12},{12... | collective-permute-start | bytes 1179656 | tf_op jit(solution)/shard_map/ppermute | solution.py:23
  21.4 15.0 %collective-permute-start.10 = (f32[768,128]{1,0:T(8,128)S(1)}, f32[768,128]{1,0:T(8,128)S(1)}, u32[]{:S(2)}, u32[]{:S(2)}) collective-permute-start(f32[768,128]{1,0:T(8,128)S(1)} %term.13), channel_id=1, source_target_pairs={{0,6},{2,0},{4,2},{6,4},{1,7},{3,1},{5,3},{7,5},{8,14},{10,8},{12,... | collective-permute-start | bytes 1179656 | tf_op jit(solution)/shard_map/ppermute | solution.py:23
  36.7 26.3 %collective-permute-start.19 = (f32[2,128,768]{2,1,0:T(8,128)S(1)}, f32[2,128,768]{2,1,0:T(8,128)S(1)}, u32[]{:S(2)}, u32[]{:S(2)}) collective-permute-start(f32[2,128,768]{2,1,0:T(8,128)S(1)} %get-tuple-element.59.turned_ref.refs_0_), channel_id=1, source_target_pairs={{0,6},{2,0},{4,2},{6,4},{1,7},{3,1},{5,3},{7,5},{8,14},{10,8},{12,... | collective-permute-start | bytes 2359304 | tf_op jit(solution)/shard_map/ppermute | solution.py:23
  39.2 23.9 %collective-permute-start.18 = (f32[2,128,768]{2,1,0:T(8,128)S(1)}, f32[2,128,768]{2,1,0:T(8,128)S(1)}, u32[]{:S(2)}, u32[]{:S(2)}) collective-permute-start(f32[2,128,768]{2,1,0:T(8,128)S(1)} %get-tuple-element.59.turned_ref.refs_0_), channel_id=1, source_target_pairs={{0,2},{2,4},{4,6},{6,0},{1,3},{3,5},{5,7},{7,1},{8,10},{10,12},{12... | collective-permute-start | bytes 2359304 | tf_op jit(solution)/shard_map/ppermute | solution.py:23
  42.6 5.2 %collective-permute-start.14 = (f32[64,128]{1,0:T(8,128)S(1)}, f32[64,128]{1,0:T(8,128)S(1)}, u32[]{:S(2)}, u32[]{:S(2)}) collective-permute-start(f32[64,128]{1,0:T(8,128)S(1)} %add.30), channel_id=1, source_target_pairs={{0,64},{32,96},{64,0},{96,32},{1,65},{33,97},{65,1},{97,33},{2,66}... | collective-permute-start | bytes 98312 | tf_op jit(solution)/shard_map/ppermute | solution.py:23
  45.6 3.1 %collective-permute-start.13 = (f32[64,128]{1,0:T(8,128)S(1)}, f32[64,128]{1,0:T(8,128)S(1)}, u32[]{:S(2)}, u32[]{:S(2)}) collective-permute-start(f32[64,128]{1,0:T(8,128)S(1)} %add.30), channel_id=1, source_target_pairs={{0,96},{32,0},{64,32},{96,64},{1,97},{33,1},{65,33},{97,65},{2,98}... | collective-permute-start | bytes 98312 | tf_op jit(solution)/shard_map/ppermute | solution.py:23
  46.4 4.3 %collective-permute-start.12 = (f32[64,128]{1,0:T(8,128)S(1)}, f32[64,128]{1,0:T(8,128)S(1)}, u32[]{:S(2)}, u32[]{:S(2)}) collective-permute-start(f32[64,128]{1,0:T(8,128)S(1)} %add.30), channel_id=1, source_target_pairs={{0,32},{32,64},{64,96},{96,0},{1,33},{33,65},{65,97},{97,1},{2,34}... | collective-permute-start | bytes 98312 | tf_op jit(solution)/shard_map/ppermute | solution.py:23
  50.6 5.1 %collective-permute-start.17 = (f32[64,128]{1,0:T(8,128)S(1)}, f32[64,128]{1,0:T(8,128)S(1)}, u32[]{:S(2)}, u32[]{:S(2)}) collective-permute-start(f32[64,128]{1,0:T(8,128)S(1)} %add_add_fusion.2), channel_id=1, source_target_pairs={{0,16},{8,24},{16,0},{24,8},{1,17},{9,25},{17,1},{25,9},{2,18},{10... | collective-permute-start | bytes 98312 | tf_op jit(solution)/shard_map/ppermute | solution.py:23
  54.3 3.1 %collective-permute-start.16 = (f32[64,128]{1,0:T(8,128)S(1)}, f32[64,128]{1,0:T(8,128)S(1)}, u32[]{:S(2)}, u32[]{:S(2)}) collective-permute-start(f32[64,128]{1,0:T(8,128)S(1)} %add_add_fusion.2), channel_id=1, source_target_pairs={{0,24},{8,0},{16,8},{24,16},{1,25},{9,1},{17,9},{25,17},{2,26},{10... | collective-permute-start | bytes 98312 | tf_op jit(solution)/shard_map/ppermute | solution.py:23
  54.8 4.3 %collective-permute-start.15 = (f32[64,128]{1,0:T(8,128)S(1)}, f32[64,128]{1,0:T(8,128)S(1)}, u32[]{:S(2)}, u32[]{:S(2)}) collective-permute-start(f32[64,128]{1,0:T(8,128)S(1)} %add_add_fusion.2), channel_id=1, source_target_pairs={{0,8},{8,16},{16,24},{24,0},{1,9},{9,17},{17,25},{25,1},{2,10},{10... | collective-permute-start | bytes 98312 | tf_op jit(solution)/shard_map/ppermute | solution.py:23
  59.0 7.5 %collective-permute-start.22 = (f32[64,128]{1,0:T(8,128)S(1)}, f32[64,128]{1,0:T(8,128)S(1)}, u32[]{:S(2)}, u32[]{:S(2)}) collective-permute-start(f32[64,128]{1,0:T(8,128)S(1)} %add_add_fusion.1), channel_id=1, source_target_pairs={{0,6},{2,0},{4,2},{6,4},{1,7},{3,1},{5,3},{7,5},{8,14},{10,8},{12,... | collective-permute-start | bytes 98312 | tf_op jit(solution)/shard_map/ppermute | solution.py:23
  61.8 4.7 %collective-permute-start.21 = (f32[64,128]{1,0:T(8,128)S(1)}, f32[64,128]{1,0:T(8,128)S(1)}, u32[]{:S(2)}, u32[]{:S(2)}) collective-permute-start(f32[64,128]{1,0:T(8,128)S(1)} %add_add_fusion.1), channel_id=1, source_target_pairs={{0,2},{2,4},{4,6},{6,0},{1,3},{3,5},{5,7},{7,1},{8,10},{10,12},{12... | collective-permute-start | bytes 98312 | tf_op jit(solution)/shard_map/ppermute | solution.py:23
  61.8 4.8 %collective-permute-start.20 = (f32[64,128]{1,0:T(8,128)S(1)}, f32[64,128]{1,0:T(8,128)S(1)}, u32[]{:S(2)}, u32[]{:S(2)}) collective-permute-start(f32[64,128]{1,0:T(8,128)S(1)} %add_add_fusion.1), channel_id=1, source_target_pairs={{0,4},{2,6},{4,0},{6,2},{1,5},{3,7},{5,1},{7,3},{8,12},{10,14},{12... | collective-permute-start | bytes 98312 | tf_op jit(solution)/shard_map/ppermute | solution.py:23
  63.1 13.1 %collective-permute-start.24 = (f32[1,128,768]{2,1,0:T(8,128)S(1)}, f32[1,128,768]{2,1,0:T(8,128)S(1)}, u32[]{:S(2)}, u32[]{:S(2)}) collective-permute-start(f32[1,128,768]{2,1,0:T(8,128)S(1)} %slice.6), channel_id=1, source_target_pairs={{0,6},{2,0},{4,2},{6,4},{1,7},{3,1},{5,3},{7,5},{8,14},{10,8},{12,... | collective-permute-start | bytes 1179656 | tf_op jit(solution)/shard_map/ppermute | solution.py:23
  64.6 11.6 %collective-permute-start.25 = (f32[1,128,768]{2,1,0:T(8,128)S(1)}, f32[1,128,768]{2,1,0:T(8,128)S(1)}, u32[]{:S(2)}, u32[]{:S(2)}) collective-permute-start(f32[1,128,768]{2,1,0:T(8,128)S(1)} %slice.7), channel_id=1, source_target_pairs={{0,2},{2,4},{4,6},{6,0},{1,3},{3,5},{5,7},{7,1},{8,10},{10,12},{12... | collective-permute-start | bytes 1179656 | tf_op jit(solution)/shard_map/ppermute | solution.py:23
  66.5 5.8 %collective-permute-start.23 = (f32[64,128]{1,0:T(8,128)S(1)}, f32[64,128]{1,0:T(8,128)S(1)}, u32[]{:S(2)}, u32[]{:S(2)}) collective-permute-start(f32[64,128]{1,0:T(8,128)S(1)} %add_add_fusion.mine_ref), channel_id=1, source_target_pairs={{0,1},{1,0},{2,3},{3,2},{4,5},{5,4},{6,7},{7,6},{8,9},{9,8},{10,11... | collective-permute-start | bytes 98312 | tf_op jit(solution)/shard_map/ppermute | solution.py:23
  78.0 13.1 %all-to-all-start = ((f32[32,8,128]{2,1,0:T(8,128)}), f32[32,8,128]{2,1,0:T(8,128)S(1)}, u32[]{:S(2)}, u32[]{:S(2)}) async-start(f32[32,8,128]{2,1,0:T(8,128)} %bitcast), calls=%async_computation | async-start | bytes 262144 | tf_op jit(solution)/shard_map/all_to_all | solution.py:399
  (5 other events, 35.6 us)

commit v7 on v5

--- a/solution.py
+++ b/solution.py
@@ -372,9 +372,10 @@
     both_bot = shift(term(left, half, half, tests, (far_bot,)), "x", 3)
     own, turned = finish(base, both_top, both_bot)
 
-    from_left = shift(turned, "x", 1)
     from_right = shift(turned, "x", 3)
     keep, give = gather(gram_of(own, turned))
+    keep, give, turned = lax.optimization_barrier((keep, give, turned))
+    from_left = shift(turned, "x", 1)
     gram = keep + swap(give)
     gram = axis_sum(axis_sum(gram, "y"), "z")
     across = [shift(gram, "x", by) for by in (2, 1, 3)]

time: 90.8 us -> 90.8 us (level)
  transfers between devices with their start and end apart: 27 -> 27, of which waited for: 11 -> 11; matrix products, arithmetic and copies ran while one was open for 0% -> 0% of each run, Pallas kernels for 16% -> 15%
where the time goes in v7:
time: 90.8 us; the launch traced here: 90.6 us
  starting transfers between devices  39.2 us (43%)
  waiting for transfers between devices  32.4 us (36%)
  Pallas kernels  18.1 us (20%)
    ppermute x26, starting transfers between devices, shift(): return lax.ppermute(block, axis, [(i, (i + by) % n) for i in range(n)])  35 us
    ppermute x26, waiting for transfers between devices, shift(): return lax.ppermute(block, axis, [(i, (i + by) % n) for i in range(n)])  27 us
    all_to_all x1, waiting for transfers between devices, shards(): lax.all_to_all(weights.reshape(2 * rank, -1), ('y', 'z', 'core'), 0, 0, t...  5.39 us
    all_to_all x1, starting transfers between devices, shards(): lax.all_to_all(weights.reshape(2 * rank, -1), ('y', 'z', 'core'), 0, 0, t...  4.12 us
    pallas_call x1, Pallas kernels, factor_inverse(): pl.pallas_call(functools.partial(factor_body, scale=scale), out_shape=(ou...  3.87 us
    pallas_call x2, Pallas kernels, fetch(): pl.pallas_call(functools.partial(fetch_body, plan=plan), out_shape=[pltpu...  3.76 us
    pallas_call x2, Pallas kernels, weigh(): pl.pallas_call(functools.partial(weigh_body, plan=plan, block=block, widt...  3.56 us
    pallas_call x7, Pallas kernels, term(): pl.pallas_call(functools.partial(term_body, first=first, sizes=sizes, blo...  2.85 us
  transfers between devices with their start and end apart: 27, of which 11 were waited for; matrix products, arithmetic and copies ran while one was open for 0% of the time, Pallas kernels for 15%

profile of v7, /device:TPU:1, one launch (start us, length us, event | category | flops | bytes accessed | tf_op | source)
XLA Modules:
  0.0 90.6 jit_solution(17682725150568909138)
XLA Ops:
  0.6 1.5 %collective-permute-start = (f32[128,128]{1,0:T(8,128)}, f32[128,128]{1,0:T(8,128)S(1)}, u32[]{:S(2)}, u32[]{:S(2)}) collective-permute-start(f32[128,128]{1,0:T(8,128)} %test_ref.13), channel_id=1, source_target_pairs={{0,1},{1,0},{2,3},{3,2},{4,5},{5,4},{6,7},{7,6},{8,9},{9,8},{10,11... | collective-permute-start | bytes 196616 | tf_op jit(solution)/shard_map/ppermute | solution.py:23
  3.6 2.6 %fetch.3 = (f32[1536,128]{1,0:T(8,128)S(1)}, f32[1536,128]{1,0:T(8,128)S(1)}, f32[1536,128]{1,0:T(8,128)S(1)}, f32[1536,128]{1,0:T(8,128)S(1)}, f32[1536,128]{1,...) custom-call(f32[12288,128]{1,0:T(8,128)} %panel_ref.2), custom_call_target="tpu_custom_call" | custom-call | tf_op jit(solution)/shard_map/fetch/pallas_call | solution.py:65
  9.2 1.4 %collective-permute-start.8 = (f32[768,128]{1,0:T(8,128)S(1)}, f32[768,128]{1,0:T(8,128)S(1)}, u32[]{:S(2)}, u32[]{:S(2)}) collective-permute-start(f32[768,128]{1,0:T(8,128)S(1)} %term.8), channel_id=1, source_target_pairs={{0,6},{2,0},{4,2},{6,4},{1,7},{3,1},{5,3},{7,5},{8,14},{10,8},{12,... | collective-permute-start | bytes 1179656 | tf_op jit(solution)/shard_map/ppermute | solution.py:23
  11.4 2.2 %collective-permute-start.5 = (f32[768,128]{1,0:T(8,128)S(1)}, f32[768,128]{1,0:T(8,128)S(1)}, u32[]{:S(2)}, u32[]{:S(2)}) collective-permute-start(f32[768,128]{1,0:T(8,128)S(1)} %term.10), channel_id=1, source_target_pairs={{0,6},{2,0},{4,2},{6,4},{1,7},{3,1},{5,3},{7,5},{8,14},{10,8},{12,... | collective-permute-start | bytes 1179656 | tf_op jit(solution)/shard_map/ppermute | solution.py:23
  13.5 6.1 %collective-permute-done.7.rest_0_ = f32[768,128]{1,0:T(8,128)S(1)} collective-permute-done((f32[768,128]{1,0:T(8,128)S(1)}, f32[768,128]{1,0:T(8,128)S(1)}, u32[]{:S(2)}, u32[]{:S(2)}) %collective-permute-start.7) | collective-permute-done | bytes 393248 | tf_op jit(solution)/shard_map/ppermute | solution.py:23
  21.4 1.8 %collective-permute-start.10 = (f32[768,128]{1,0:T(8,128)S(1)}, f32[768,128]{1,0:T(8,128)S(1)}, u32[]{:S(2)}, u32[]{:S(2)}) collective-permute-start(f32[768,128]{1,0:T(8,128)S(1)} %term.13), channel_id=1, source_target_pairs={{0,6},{2,0},{4,2},{6,4},{1,7},{3,1},{5,3},{7,5},{8,14},{10,8},{12,... | collective-permute-start | bytes 1179656 | tf_op jit(solution)/shard_map/ppermute | solution.py:23
  23.2 4.6 %collective-permute-done.5.rest_1_ = f32[768,128]{1,0:T(8,128)S(1)} collective-permute-done((f32[768,128]{1,0:T(8,128)S(1)}, f32[768,128]{1,0:T(8,128)S(1)}, u32[]{:S(2)}, u32[]{:S(2)}) %collective-permute-start.5) | collective-permute-done | bytes 393248 | tf_op jit(solution)/shard_map/ppermute | solution.py:23
  28.6 7.8 %collective-permute-done.9.top_ref = f32[768,128]{1,0:T(8,128)S(1)} collective-permute-done((f32[768,128]{1,0:T(8,128)S(1)}, f32[768,128]{1,0:T(8,128)S(1)}, u32[]{:S(2)}, u32[]{:S(2)}) %collective-permute-start.9) | collective-permute-done | bytes 393248 | tf_op jit(solution)/shard_map/ppermute | solution.py:23
  38.6 1.7 %collective-permute-start.19 = (f32[2,128,768]{2,1,0:T(8,128)S(1)}, f32[2,128,768]{2,1,0:T(8,128)S(1)}, u32[]{:S(2)}, u32[]{:S(2)}) collective-permute-start(f32[2,128,768]{2,1,0:T(8,128)S(1)} %get-tuple-element.68.turned_ref.refs_0_), channel_id=1, source_target_pairs={{0,6},{2,0},{4,2},{6,4},{1,7},{3,1},{5,3},{7,5},{8,14},{10,8},{12,... | collective-permute-start | bytes 2359304 | tf_op jit(solution)/shard_map/ppermute | solution.py:23
  40.3 1.7 %collective-permute-start.11 = (f32[64,128]{1,0:T(8,128)S(1)}, f32[64,128]{1,0:T(8,128)S(1)}, u32[]{:S(2)}, u32[]{:S(2)}) collective-permute-start(f32[64,128]{1,0:T(8,128)S(1)} %get-tuple-element.65), channel_id=1, source_target_pairs={{0,1},{1,0},{2,3},{3,2},{4,5},{5,4},{6,7},{7,6},{8,9},{9,8},{10,11... | collective-permute-start | bytes 98312 | tf_op jit(solution)/shard_map/ppermute | solution.py:23
  42.9 2.9 %collective-permute-start.14 = (f32[64,128]{1,0:T(8,128)S(1)}, f32[64,128]{1,0:T(8,128)S(1)}, u32[]{:S(2)}, u32[]{:S(2)}) collective-permute-start(f32[64,128]{1,0:T(8,128)S(1)} %add.30), channel_id=1, source_target_pairs={{0,64},{32,96},{64,0},{96,32},{1,65},{33,97},{65,1},{97,33},{2,66}... | collective-permute-start | bytes 98312 | tf_op jit(solution)/shard_map/ppermute | solution.py:23
  47.3 1.7 %collective-permute-done.13 = f32[64,128]{1,0:T(8,128)S(1)} collective-permute-done((f32[64,128]{1,0:T(8,128)S(1)}, f32[64,128]{1,0:T(8,128)S(1)}, u32[]{:S(2)}, u32[]{:S(2)}) %collective-permute-start.13) | collective-permute-done | bytes 32800 | tf_op jit(solution)/shard_map/ppermute | solution.py:23
  48.9 1.9 %collective-permute-done.12 = f32[64,128]{1,0:T(8,128)S(1)} collective-permute-done((f32[64,128]{1,0:T(8,128)S(1)}, f32[64,128]{1,0:T(8,128)S(1)}, u32[]{:S(2)}, u32[]{:S(2)}) %collective-permute-start.12) | collective-permute-done | bytes 32800 | tf_op jit(solution)/shard_map/ppermute | solution.py:23
  50.8 3.7 %collective-permute-start.17 = (f32[64,128]{1,0:T(8,128)S(1)}, f32[64,128]{1,0:T(8,128)S(1)}, u32[]{:S(2)}, u32[]{:S(2)}) collective-permute-start(f32[64,128]{1,0:T(8,128)S(1)} %add_add_fusion.2), channel_id=1, source_target_pairs={{0,16},{8,24},{16,0},{24,8},{1,17},{9,25},{17,1},{25,9},{2,18},{10... | collective-permute-start | bytes 98312 | tf_op jit(solution)/shard_map/ppermute | solution.py:23
  56.0 1.6 %collective-permute-done.16 = f32[64,128]{1,0:T(8,128)S(1)} collective-permute-done((f32[64,128]{1,0:T(8,128)S(1)}, f32[64,128]{1,0:T(8,128)S(1)}, u32[]{:S(2)}, u32[]{:S(2)}) %collective-permute-start.16) | collective-permute-done | bytes 32800 | tf_op jit(solution)/shard_map/ppermute | solution.py:23
  57.6 1.4 %collective-permute-done.15 = f32[64,128]{1,0:T(8,128)S(1)} collective-permute-done((f32[64,128]{1,0:T(8,128)S(1)}, f32[64,128]{1,0:T(8,128)S(1)}, u32[]{:S(2)}, u32[]{:S(2)}) %collective-permute-start.15) | collective-permute-done | bytes 32800 | tf_op jit(solution)/shard_map/ppermute | solution.py:23
  62.8 1.7 %collective-permute-start.25 = (f32[1,128,768]{2,1,0:T(8,128)S(1)}, f32[1,128,768]{2,1,0:T(8,128)S(1)}, u32[]{:S(2)}, u32[]{:S(2)}) collective-permute-start(f32[1,128,768]{2,1,0:T(8,128)S(1)} %slice.7), channel_id=1, source_target_pairs={{0,2},{2,4},{4,6},{6,0},{1,3},{3,5},{5,7},{7,1},{8,10},{10,12},{12... | collective-permute-start | bytes 1179656 | tf_op jit(solution)/shard_map/ppermute | solution.py:23
  64.5 1.8 %weigh.2.refs_4_ = f32[128,256]{1,0:T(8,128)S(1)} custom-call(f32[2,128,768]{2,1,0:T(8,128)S(1)} %get-tuple-element.68.turned_ref.refs_0_, f32[2,128,768]{2,1,0:T(8,128)S(1)} %collective-permute-done.18.refs_1_, f32[2,128,768]{2,1,0:T(8,128)S(1)} %collective-permute-done.19.refs_2_, f32[1536,128]{1,0:T(8,128)S(1)} %get-tuple-element.42.mine_ref.refs_3_, ...), custom_call_target="tpu_custom_call" | custom-call | tf_op jit(solution)/shard_map/weigh/pallas_call | solution.py:310
  66.4 5.2 %collective-permute-start.23 = (f32[64,128]{1,0:T(8,128)S(1)}, f32[64,128]{1,0:T(8,128)S(1)}, u32[]{:S(2)}, u32[]{:S(2)}) collective-permute-start(f32[64,128]{1,0:T(8,128)S(1)} %add_add_fusion.mine_ref), channel_id=1, source_target_pairs={{0,1},{1,0},{2,3},{3,2},{4,5},{5,4},{6,7},{7,6},{8,9},{9,8},{10,11... | collective-permute-start | bytes 98312 | tf_op jit(solution)/shard_map/ppermute | solution.py:23
  72.5 3.9 %factor.1 = (f32[128,128]{1,0:T(8,128)S(1)}, f32[128,128]{1,0:T(8,128)S(1)}) custom-call(f32[64,128]{1,0:T(8,128)S(1)} %add_add_fusion.mine_ref, f32[64,128]{1,0:T(8,128)S(1)} %collective-permute-done.23.other_ref), custom_call_target="tpu_custom_call" | custom-call | flops 1300000000 | tf_op jit(solution)/shard_map/factor/pallas_call | solution.py:231
  76.4 1.8 %weigh.3 = f32[16,2,8,128]{3,2,1,0:T(8,128)} custom-call(f32[1,128,768]{2,1,0:T(8,128)S(1)} %collective-permute-done.24.refs_0_, f32[1,128,768]{2,1,0:T(8,128)S(1)} %collective-permute-done.25.refs_1_, f32[1536,128]{1,0:T(8,128)S(1)} %get-tuple-element.43.mine_ref.refs_2_, f32[1536,128]{1,0:T(8,128)S(1)} %collective-permute-done.1.other_ref.refs_3_, ...), custom_call_target="tpu_custom_call" | custom-call | tf_op jit(solution)/shard_map/weigh/pallas_call | solution.py:310
  78.2 4.1 %all-to-all-start = ((f32[32,8,128]{2,1,0:T(8,128)}), f32[32,8,128]{2,1,0:T(8,128)S(1)}, u32[]{:S(2)}, u32[]{:S(2)}) async-start(f32[32,8,128]{2,1,0:T(8,128)} %bitcast), calls=%async_computation | async-start | bytes 262144 | tf_op jit(solution)/shard_map/all_to_all | solution.py:399
  82.3 2.3 %basis.1 = f32[1536,128]{1,0:T(8,128)} custom-call(f32[1536,128]{1,0:T(8,128)S(1)} %get-tuple-element.60.own_ref, f32[128,128]{1,0:T(8,128)S(1)} %get-tuple-element.74.turned_ref), custom_call_target="tpu_custom_call" | custom-call | tf_op jit(solution)/shard_map/basis/pallas_call | solution.py:251
  84.6 5.4 %all-to-all-done = f32[32,8,128]{2,1,0:T(8,128)S(1)} async-done(((f32[32,8,128]{2,1,0:T(8,128)}), f32[32,8,128]{2,1,0:T(8,128)S(1)}, u32[]{:S(2)}, u32[]{:S(2)}) %all-to-all-start) | async-done | bytes 131104 | tf_op jit(solution)/shard_map/all_to_all | solution.py:399
  (57 shorter events, 19.1 us)
Async XLA Ops:
  7.0 3.5 %collective-permute-start.3 = (f32[1536,128]{1,0:T(8,128)S(1)}, f32[1536,128]{1,0:T(8,128)S(1)}, u32[]{:S(2)}, u32[]{:S(2)}) collective-permute-start(f32[1536,128]{1,0:T(8,128)S(1)} %get-tuple-element.51), channel_id=1, source_target_pairs={{0,1},{1,0},{2,3},{3,2},{4,5},{5,4},{6,7},{7,6},{8,9},{9,8},{10,11... | collective-permute-start | bytes 2359304 | tf_op jit(solution)/shard_map/ppermute | solution.py:23
  7.4 3.6 %collective-permute-start.4 = (f32[1536,128]{1,0:T(8,128)S(1)}, f32[1536,128]{1,0:T(8,128)S(1)}, u32[]{:S(2)}, u32[]{:S(2)}) collective-permute-start(f32[1536,128]{1,0:T(8,128)S(1)} %get-tuple-element.53), channel_id=1, source_target_pairs={{0,1},{1,0},{2,3},{3,2},{4,5},{5,4},{6,7},{7,6},{8,9},{9,8},{10,11... | collective-permute-start | bytes 2359304 | tf_op jit(solution)/shard_map/ppermute | solution.py:23
  7.6 15.6 %collective-permute-start.2 = (f32[1536,128]{1,0:T(8,128)S(1)}, f32[1536,128]{1,0:T(8,128)S(1)}, u32[]{:S(2)}, u32[]{:S(2)}) collective-permute-start(f32[1536,128]{1,0:T(8,128)S(1)} %get-tuple-element.49), channel_id=1, source_target_pairs={{0,1},{1,0},{2,3},{3,2},{4,5},{5,4},{6,7},{7,6},{8,9},{9,8},{10,11... | collective-permute-start | bytes 2359304 | tf_op jit(solution)/shard_map/ppermute | solution.py:23
  7.9 11.7 %collective-permute-start.7 = (f32[768,128]{1,0:T(8,128)S(1)}, f32[768,128]{1,0:T(8,128)S(1)}, u32[]{:S(2)}, u32[]{:S(2)}) collective-permute-start(f32[768,128]{1,0:T(8,128)S(1)} %term.7), channel_id=1, source_target_pairs={{0,2},{2,4},{4,6},{6,0},{1,3},{3,5},{5,7},{7,1},{8,10},{10,12},{12... | collective-permute-start | bytes 1179656 | tf_op jit(solution)/shard_map/ppermute | solution.py:23
  9.2 10.4 %collective-permute-start.8 = (f32[768,128]{1,0:T(8,128)S(1)}, f32[768,128]{1,0:T(8,128)S(1)}, u32[]{:S(2)}, u32[]{:S(2)}) collective-permute-start(f32[768,128]{1,0:T(8,128)S(1)} %term.8), channel_id=1, source_target_pairs={{0,6},{2,0},{4,2},{6,4},{1,7},{3,1},{5,3},{7,5},{8,14},{10,8},{12,... | collective-permute-start | bytes 1179656 | tf_op jit(solution)/shard_map/ppermute | solution.py:23
  11.4 16.4 %collective-permute-start.5 = (f32[768,128]{1,0:T(8,128)S(1)}, f32[768,128]{1,0:T(8,128)S(1)}, u32[]{:S(2)}, u32[]{:S(2)}) collective-permute-start(f32[768,128]{1,0:T(8,128)S(1)} %term.10), channel_id=1, source_target_pairs={{0,6},{2,0},{4,2},{6,4},{1,7},{3,1},{5,3},{7,5},{8,14},{10,8},{12,... | collective-permute-start | bytes 1179656 | tf_op jit(solution)/shard_map/ppermute | solution.py:23
  13.5 14.5 %collective-permute-start.6 = (f32[768,128]{1,0:T(8,128)S(1)}, f32[768,128]{1,0:T(8,128)S(1)}, u32[]{:S(2)}, u32[]{:S(2)}) collective-permute-start(f32[768,128]{1,0:T(8,128)S(1)} %term.9), channel_id=1, source_target_pairs={{0,2},{2,4},{4,6},{6,0},{1,3},{3,5},{5,7},{7,1},{8,10},{10,12},{12... | collective-permute-start | bytes 1179656 | tf_op jit(solution)/shard_map/ppermute | solution.py:23
  20.0 16.5 %collective-permute-start.9 = (f32[768,128]{1,0:T(8,128)S(1)}, f32[768,128]{1,0:T(8,128)S(1)}, u32[]{:S(2)}, u32[]{:S(2)}) collective-permute-start(f32[768,128]{1,0:T(8,128)S(1)} %term.12), channel_id=1, source_target_pairs={{0,2},{2,4},{4,6},{6,0},{1,3},{3,5},{5,7},{7,1},{8,10},{10,12},{12... | collective-permute-start | bytes 1179656 | tf_op jit(solution)/shard_map/ppermute | solution.py:23
  21.4 15.0 %collective-permute-start.10 = (f32[768,128]{1,0:T(8,128)S(1)}, f32[768,128]{1,0:T(8,128)S(1)}, u32[]{:S(2)}, u32[]{:S(2)}) collective-permute-start(f32[768,128]{1,0:T(8,128)S(1)} %term.13), channel_id=1, source_target_pairs={{0,6},{2,0},{4,2},{6,4},{1,7},{3,1},{5,3},{7,5},{8,14},{10,8},{12,... | collective-permute-start | bytes 1179656 | tf_op jit(solution)/shard_map/ppermute | solution.py:23
  37.6 25.1 %collective-permute-start.18 = (f32[2,128,768]{2,1,0:T(8,128)S(1)}, f32[2,128,768]{2,1,0:T(8,128)S(1)}, u32[]{:S(2)}, u32[]{:S(2)}) collective-permute-start(f32[2,128,768]{2,1,0:T(8,128)S(1)} %get-tuple-element.68.turned_ref.refs_0_), channel_id=1, source_target_pairs={{0,2},{2,4},{4,6},{6,0},{1,3},{3,5},{5,7},{7,1},{8,10},{10,12},{12... | collective-permute-start | bytes 2359304 | tf_op jit(solution)/shard_map/ppermute | solution.py:23
  38.6 24.1 %collective-permute-start.19 = (f32[2,128,768]{2,1,0:T(8,128)S(1)}, f32[2,128,768]{2,1,0:T(8,128)S(1)}, u32[]{:S(2)}, u32[]{:S(2)}) collective-permute-start(f32[2,128,768]{2,1,0:T(8,128)S(1)} %get-tuple-element.68.turned_ref.refs_0_), channel_id=1, source_target_pairs={{0,6},{2,0},{4,2},{6,4},{1,7},{3,1},{5,3},{7,5},{8,14},{10,8},{12,... | collective-permute-start | bytes 2359304 | tf_op jit(solution)/shard_map/ppermute | solution.py:23
  42.9 4.4 %collective-permute-start.14 = (f32[64,128]{1,0:T(8,128)S(1)}, f32[64,128]{1,0:T(8,128)S(1)}, u32[]{:S(2)}, u32[]{:S(2)}) collective-permute-start(f32[64,128]{1,0:T(8,128)S(1)} %add.30), channel_id=1, source_target_pairs={{0,64},{32,96},{64,0},{96,32},{1,65},{33,97},{65,1},{97,33},{2,66}... | collective-permute-start | bytes 98312 | tf_op jit(solution)/shard_map/ppermute | solution.py:23
  45.8 3.1 %collective-permute-start.13 = (f32[64,128]{1,0:T(8,128)S(1)}, f32[64,128]{1,0:T(8,128)S(1)}, u32[]{:S(2)}, u32[]{:S(2)}) collective-permute-start(f32[64,128]{1,0:T(8,128)S(1)} %add.30), channel_id=1, source_target_pairs={{0,96},{32,0},{64,32},{96,64},{1,97},{33,1},{65,33},{97,65},{2,98}... | collective-permute-start | bytes 98312 | tf_op jit(solution)/shard_map/ppermute | solution.py:23
  46.6 4.3 %collective-permute-start.12 = (f32[64,128]{1,0:T(8,128)S(1)}, f32[64,128]{1,0:T(8,128)S(1)}, u32[]{:S(2)}, u32[]{:S(2)}) collective-permute-start(f32[64,128]{1,0:T(8,128)S(1)} %add.30), channel_id=1, source_target_pairs={{0,32},{32,64},{64,96},{96,0},{1,33},{33,65},{65,97},{97,1},{2,34}... | collective-permute-start | bytes 98312 | tf_op jit(solution)/shard_map/ppermute | solution.py:23
  50.8 5.1 %collective-permute-start.17 = (f32[64,128]{1,0:T(8,128)S(1)}, f32[64,128]{1,0:T(8,128)S(1)}, u32[]{:S(2)}, u32[]{:S(2)}) collective-permute-start(f32[64,128]{1,0:T(8,128)S(1)} %add_add_fusion.2), channel_id=1, source_target_pairs={{0,16},{8,24},{16,0},{24,8},{1,17},{9,25},{17,1},{25,9},{2,18},{10... | collective-permute-start | bytes 98312 | tf_op jit(solution)/shard_map/ppermute | solution.py:23
  54.5 3.1 %collective-permute-start.16 = (f32[64,128]{1,0:T(8,128)S(1)}, f32[64,128]{1,0:T(8,128)S(1)}, u32[]{:S(2)}, u32[]{:S(2)}) collective-permute-start(f32[64,128]{1,0:T(8,128)S(1)} %add_add_fusion.2), channel_id=1, source_target_pairs={{0,24},{8,0},{16,8},{24,16},{1,25},{9,1},{17,9},{25,17},{2,26},{10... | collective-permute-start | bytes 98312 | tf_op jit(solution)/shard_map/ppermute | solution.py:23
  55.0 4.0 %collective-permute-start.15 = (f32[64,128]{1,0:T(8,128)S(1)}, f32[64,128]{1,0:T(8,128)S(1)}, u32[]{:S(2)}, u32[]{:S(2)}) collective-permute-start(f32[64,128]{1,0:T(8,128)S(1)} %add_add_fusion.2), channel_id=1, source_target_pairs={{0,8},{8,16},{16,24},{24,0},{1,9},{9,17},{17,25},{25,1},{2,10},{10... | collective-permute-start | bytes 98312 | tf_op jit(solution)/shard_map/ppermute | solution.py:23
  58.9 7.4 %collective-permute-start.20 = (f32[64,128]{1,0:T(8,128)S(1)}, f32[64,128]{1,0:T(8,128)S(1)}, u32[]{:S(2)}, u32[]{:S(2)}) collective-permute-start(f32[64,128]{1,0:T(8,128)S(1)} %add_add_fusion.1), channel_id=1, source_target_pairs={{0,4},{2,6},{4,0},{6,2},{1,5},{3,7},{5,1},{7,3},{8,12},{10,14},{12... | collective-permute-start | bytes 98312 | tf_op jit(solution)/shard_map/ppermute | solution.py:23
  60.0 6.3 %collective-permute-start.21 = (f32[64,128]{1,0:T(8,128)S(1)}, f32[64,128]{1,0:T(8,128)S(1)}, u32[]{:S(2)}, u32[]{:S(2)}) collective-permute-start(f32[64,128]{1,0:T(8,128)S(1)} %add_add_fusion.1), channel_id=1, source_target_pairs={{0,2},{2,4},{4,6},{6,0},{1,3},{3,5},{5,7},{7,1},{8,10},{10,12},{12... | collective-permute-start | bytes 98312 | tf_op jit(solution)/shard_map/ppermute | solution.py:23
  61.4 5.0 %collective-permute-start.22 = (f32[64,128]{1,0:T(8,128)S(1)}, f32[64,128]{1,0:T(8,128)S(1)}, u32[]{:S(2)}, u32[]{:S(2)}) collective-permute-start(f32[64,128]{1,0:T(8,128)S(1)} %add_add_fusion.1), channel_id=1, source_target_pairs={{0,6},{2,0},{4,2},{6,4},{1,7},{3,1},{5,3},{7,5},{8,14},{10,8},{12,... | collective-permute-start | bytes 98312 | tf_op jit(solution)/shard_map/ppermute | solution.py:23
  62.7 13.6 %collective-permute-start.24 = (f32[1,128,768]{2,1,0:T(8,128)S(1)}, f32[1,128,768]{2,1,0:T(8,128)S(1)}, u32[]{:S(2)}, u32[]{:S(2)}) collective-permute-start(f32[1,128,768]{2,1,0:T(8,128)S(1)} %slice.6), channel_id=1, source_target_pairs={{0,6},{2,0},{4,2},{6,4},{1,7},{3,1},{5,3},{7,5},{8,14},{10,8},{12,... | collective-permute-start | bytes 1179656 | tf_op jit(solution)/shard_map/ppermute | solution.py:23
  62.8 13.5 %collective-permute-start.25 = (f32[1,128,768]{2,1,0:T(8,128)S(1)}, f32[1,128,768]{2,1,0:T(8,128)S(1)}, u32[]{:S(2)}, u32[]{:S(2)}) collective-permute-start(f32[1,128,768]{2,1,0:T(8,128)S(1)} %slice.7), channel_id=1, source_target_pairs={{0,2},{2,4},{4,6},{6,0},{1,3},{3,5},{5,7},{7,1},{8,10},{10,12},{12... | collective-permute-start | bytes 1179656 | tf_op jit(solution)/shard_map/ppermute | solution.py:23
  66.4 6.1 %collective-permute-start.23 = (f32[64,128]{1,0:T(8,128)S(1)}, f32[64,128]{1,0:T(8,128)S(1)}, u32[]{:S(2)}, u32[]{:S(2)}) collective-permute-start(f32[64,128]{1,0:T(8,128)S(1)} %add_add_fusion.mine_ref), channel_id=1, source_target_pairs={{0,1},{1,0},{2,3},{3,2},{4,5},{5,4},{6,7},{7,6},{8,9},{9,8},{10,11... | collective-permute-start | bytes 98312 | tf_op jit(solution)/shard_map/ppermute | solution.py:23
  78.2 11.8 %all-to-all-start = ((f32[32,8,128]{2,1,0:T(8,128)}), f32[32,8,128]{2,1,0:T(8,128)S(1)}, u32[]{:S(2)}, u32[]{:S(2)}) async-start(f32[32,8,128]{2,1,0:T(8,128)} %bitcast), calls=%async_computation | async-start | bytes 262144 | tf_op jit(solution)/shard_map/all_to_all | solution.py:399
  (5 other events, 35.5 us)
